TPU v7x, 32 devices: a whole 2x2x4 slice. The times are simulated.
32 devices in a mesh: img: 16 (over z, x, core), seq: 2 (over y).
Axes of the slice: x: 2, y: 2, z: 4, core: 2. Of those that a mesh axis runs over, the one named last changes fastest.
Arguments:
- tokens: bfloat16 [16, 16, 64, 768], P('img', 'seq'), may hold values from -6 to 6
- valid_rows: int32 [16], P('img'), may hold values from 8 to 16, as said below
- valid_cols: int32 [16], P('img'), may hold values from 32 to 64, as said below
- block_gains: bfloat16 [768, 2], replicated, may hold values from 0.5 to 1.5
- block_shifts: bfloat16 [768, 2], replicated, may hold values from -1.25 to 1.25
- qkv_weight: bfloat16 [768, 2304], replicated, may hold values from -0.21875 to 0.21875
- qv_bias: bfloat16 [768, 2], replicated, may hold values from -1.25 to 1.25
- table_rows: bfloat16 [64, 31], replicated, may hold values from -0.625 to 0.625
- table_cols: bfloat16 [64, 127], replicated, may hold values from -0.625 to 0.625
- proj_weight: bfloat16 [768, 768], replicated, may hold values from -4 to 4
- proj_bias: bfloat16 [768], replicated, may hold values from -1.25 to 1.25
- fc1_weight: bfloat16 [768, 3072], replicated, may hold values from -0.21875 to 0.21875
- fc1_bias: bfloat16 [3072], replicated, may hold values from -1.25 to 1.25
- fc2_weight: bfloat16 [3072, 768], replicated, may hold values from -0.109375 to 0.109375
- fc2_bias: bfloat16 [768], replicated, may hold values from -1.25 to 1.25
- fine_first: bfloat16 [768, 1536], replicated, may hold values from -0.21875 to 0.21875
- fine_first_bias: bfloat16 [384], replicated, may hold values from -1.25 to 1.25
- fine_norm_gain: bfloat16 [384], replicated, may hold values from 0.5 to 1.5
- fine_norm_shift: bfloat16 [384], replicated, may hold values from -1.25 to 1.25
- fine_second: bfloat16 [768, 384], replicated, may hold values from -0.3125 to 0.3125
- fine_second_bias: bfloat16 [192], replicated, may hold values from -1.25 to 1.25
- middle_up: bfloat16 [768, 1536], replicated, may hold values from -0.21875 to 0.21875
- middle_up_bias: bfloat16 [384], replicated, may hold values from -1.25 to 1.25
- lateral_fine: bfloat16 [192, 256], replicated, may hold values from -0.4375 to 0.4375
- lateral_middle: bfloat16 [384, 256], replicated, may hold values from -0.3125 to 0.3125
- lateral_coarse: bfloat16 [768, 2, 256], replicated, may hold values from -0.21875 to 0.21875
- level_gains: bfloat16 [256, 8], replicated, may hold values from 0.5 to 1.5
- level_shifts: bfloat16 [256, 8], replicated, may hold values from -1.25 to 1.25
- output_convs: bfloat16 [2304, 4, 256], replicated, may hold values from -0.125 to 0.125
- cotan_fine: bfloat16 [16, 64, 256, 256], P('img', 'seq'), may hold values from -6 to 6
- cotan_middle: bfloat16 [16, 32, 128, 256], P('img', 'seq'), may hold values from -6 to 6
- cotan_base: bfloat16 [16, 16, 64, 256], P('img', 'seq'), may hold values from -6 to 6
- cotan_coarse: bfloat16 [16, 8, 32, 256], P('img', 'seq'), may hold values from -6 to 6
Outputs:
- map_fine: bfloat16 [16, 64, 256, 256], P('img', 'seq')
- map_middle: bfloat16 [16, 32, 128, 256], P('img', 'seq')
- map_base: bfloat16 [16, 16, 64, 256], P('img', 'seq')
- map_coarse: bfloat16 [16, 8, 32, 256], P('img', 'seq')
- input_grad: float32 [16, 16, 64, 768], P('img', 'seq')
- block_gains_grad: float32 [768, 2], P('img')
- block_shifts_grad: float32 [768, 2], P('img')
- qkv_weight_grad: float32 [768, 2304], P('img')
- qv_bias_grad: float32 [768, 2], P('img')
- table_rows_grad: float32 [64, 31], P('img')
- table_cols_grad: float32 [64, 127], P('img')
- proj_weight_grad: float32 [768, 768], P('img')
- proj_bias_grad: float32 [768], P('img')
- fc1_weight_grad: float32 [768, 3072], P('img')
- fc1_bias_grad: float32 [3072], P('img')
- fc2_weight_grad: float32 [3072, 768], P('img')
- fc2_bias_grad: float32 [768], P('img')
- fine_first_grad: float32 [768, 1536], P('img')
- fine_first_bias_grad: float32 [384], P('img')
- fine_norm_gain_grad: float32 [384], P('img')
- fine_norm_shift_grad: float32 [384], P('img')
- fine_second_grad: float32 [768, 384], P('img')
- fine_second_bias_grad: float32 [192], P('img')
- middle_up_grad: float32 [768, 1536], P('img')
- middle_up_bias_grad: float32 [384], P('img')
- lateral_fine_grad: float32 [192, 256], P('img')
- lateral_middle_grad: float32 [384, 256], P('img')
- lateral_coarse_grad: float32 [768, 2, 256], P('img')
- level_gains_grad: float32 [256, 8], P('img')
- level_shifts_grad: float32 [256, 8], P('img')
- output_convs_grad: float32 [2304, 4, 256], P('img')
Inputs may be any that keep to these rules, and one draw needn't show every extreme that they name: Some image has valid_rows equal to 16 and some image equal to 8. Some image has valid_cols equal to 64 and some image equal to 32.
All inputs are finite; a program needn't handle non-finite values.
Results may differ from a plain program's by a relative error of at most 0.025.
Values may be sent and summed in bfloat16 or wider, within the bound.
No kernel may reach another device: no remote copies, remote signals or barrier semaphores. Data moves between devices by JAX's collectives and lax.ppermute only.
A program may use at most 512 MiB of HBM per device.

v0:
```python
import jax
import jax.numpy as jnp
from jax import lax
from jax.sharding import PartitionSpec as P

HIGH = lax.Precision.HIGHEST
NEG = -1e30


def extended(shard, sides, width):
    for axis, dim in sides:
        peers, length = (lax.axis_size(axis), shard.shape[dim])
        up = [(i, (i + 1) % peers) for i in range(peers - 1)]
        down = [(j, i) for i, j in up]
        last = lax.slice_in_dim(shard, length - width, length, axis=dim)
        first = lax.slice_in_dim(shard, 0, width, axis=dim)
        before = lax.ppermute(last, axis, up)
        after = lax.ppermute(first, axis, down)
        shard = jnp.concatenate([before, shard, after], axis=dim)
    return shard


def shortened(shard):
    return jax.tree.map(lambda a: a.astype(jnp.bfloat16) if a.dtype == jnp.float32 else a, shard)


def value_plain(values):
    return lax.optimization_barrier(values.astype(jnp.bfloat16)).astype(jnp.float32)


def identity_plain(values):
    return values


def narrow_value_keep(values):
    return (value_plain(values), None)


def narrow_value_back(kept, grad):
    return (grad,)


def narrow_value(values):
    rounder = jax.custom_vjp(value_plain)
    rounder.defvjp(narrow_value_keep, narrow_value_back)
    return rounder(values)


def narrow_grad_keep(values):
    return (values, None)


def narrow_grad_back(kept, grad):
    return (value_plain(grad),)


def narrow_grad(values):
    rounder = jax.custom_vjp(identity_plain)
    rounder.defvjp(narrow_grad_keep, narrow_grad_back)
    return rounder(values)


def plain_product(left, right):
    return jnp.dot(
        left.astype(jnp.bfloat16), right.astype(jnp.bfloat16), preferred_element_type=jnp.float32
    )


def product_keep(left, right):
    return (plain_product(left, right), (left.astype(jnp.bfloat16), right.astype(jnp.bfloat16)))


def product_back(kept, grad):
    left_low, right_low = kept
    grad_low = grad.astype(jnp.bfloat16)
    return (
        jnp.dot(grad_low, right_low.T, preferred_element_type=jnp.float32),
        jnp.dot(left_low.T, grad_low, preferred_element_type=jnp.float32),
    )


def narrow_product(left, right):
    multiply = jax.custom_vjp(plain_product)
    multiply.defvjp(product_keep, product_back)
    return multiply(left, right)


def normalize(values, gain_vec, shift_vec):
    average = jnp.mean(values, axis=-1, keepdims=True)
    centred = values - average
    spread = jnp.mean(centred * centred, axis=-1, keepdims=True)
    return centred * lax.rsqrt(spread + 1e-06) * gain_vec + shift_vec


def deconvolve(values, weight, bias_vec):
    rows_in, cols_in, channels = values.shape
    outs_chan = bias_vec.shape[0]
    spread = narrow_product(values.reshape(rows_in * cols_in, channels), weight)
    spread = spread.reshape(rows_in, cols_in, 2, 2, outs_chan).transpose(0, 2, 1, 3, 4)
    return spread.reshape(2 * rows_in, 2 * cols_in, outs_chan) + bias_vec


def conv_three(padded, weight):
    rows_out = padded.shape[0] - 2
    cols_out = padded.shape[1] - 2
    channels = padded.shape[2]
    result = jnp.zeros((rows_out * cols_out, weight.shape[1]), jnp.float32)
    for offset_row in range(3):
        for offset_col in range(3):
            window = padded[
                offset_row : offset_row + rows_out, offset_col : offset_col + cols_out
            ].reshape(rows_out * cols_out, channels)
            tap_start = (3 * offset_row + offset_col) * channels
            result = result + narrow_product(window, weight[tap_start : tap_start + channels])
    return result.reshape(rows_out, cols_out, weight.shape[1])


def table_lookup(table, places, length):
    offsets = places[:, None] - jnp.arange(length, dtype=jnp.int32)[None, :] + (length - 1)
    chooser = (
        offsets[:, :, None] == jnp.arange(2 * length - 1, dtype=jnp.int32)[None, None, :]
    ).astype(jnp.float32)
    return jnp.einsum("ijt,ct->ijc", chooser, table, precision=HIGH)


def lateral_level(values, lateral, level_at, weights):
    rows_in, cols_in, channels = values.shape
    lateral_out = narrow_grad(narrow_product(values.reshape(rows_in * cols_in, channels), lateral))
    lateral_out = narrow_value(
        normalize(lateral_out, weights[11][:, level_at], weights[12][:, level_at])
    )
    return lateral_out.reshape(rows_in, cols_in, -1)


def per_device(
    tokens,
    valid_rows,
    valid_cols,
    block_gains,
    block_shifts,
    qkv_weight,
    qv_bias,
    table_rows,
    table_cols,
    proj_weight,
    proj_bias,
    fc1_weight,
    fc1_bias,
    fc2_weight,
    fc2_bias,
    fine_first,
    fine_first_bias,
    fine_norm_gain,
    fine_norm_shift,
    fine_second,
    fine_second_bias,
    middle_up,
    middle_up_bias,
    lateral_fine,
    lateral_middle,
    lateral_coarse,
    level_gains,
    level_shifts,
    output_convs,
    cotan_fine,
    cotan_middle,
    cotan_base,
    cotan_coarse,
):
    block_list = tuple(
        (
            weight_arg.astype(jnp.float32)
            for weight_arg in (
                block_gains,
                block_shifts,
                qkv_weight,
                qv_bias,
                table_rows,
                table_cols,
                proj_weight,
                proj_bias,
                fc1_weight,
                fc1_bias,
                fc2_weight,
                fc2_bias,
            )
        )
    )
    pyramid_list = tuple(
        (
            weight_arg.astype(jnp.float32)
            for weight_arg in (
                fine_first,
                fine_first_bias,
                fine_norm_gain,
                fine_norm_shift,
                fine_second,
                fine_second_bias,
                middle_up,
                middle_up_bias,
                lateral_fine,
                lateral_middle,
                lateral_coarse,
                level_gains,
                level_shifts,
                output_convs,
            )
        )
    )
    local_rows = tokens.shape[1]
    col_count = tokens.shape[2]
    model_width = tokens.shape[3]
    head_size = table_rows.shape[0]
    head_count = model_width // head_size
    seq_count = lax.axis_size("seq")
    total_rows = local_rows * seq_count
    local_count = local_rows * col_count
    first_row = lax.axis_index("seq") * local_rows
    image_flat = tokens[0].astype(jnp.float32).reshape(local_count, model_width)
    score_scale = head_size ** (-0.5)

    def before(flat_tokens, weights):
        normed = narrow_value(normalize(flat_tokens, weights[0][:, 0], weights[1][:, 0]))
        projected = narrow_product(normed, weights[2])
        queries = narrow_grad(narrow_value(projected[:, :model_width] + weights[3][:, 0]))
        keys_low = narrow_grad(narrow_value(projected[:, model_width : 2 * model_width]))
        values_low = narrow_grad(narrow_value(projected[:, 2 * model_width :] + weights[3][:, 1]))
        grid_query = queries.reshape(local_rows, col_count, head_count, head_size)
        row_places = first_row + jnp.arange(local_rows, dtype=jnp.int32)
        row_table = table_lookup(weights[4], row_places, total_rows)
        col_table = table_lookup(weights[5], jnp.arange(col_count, dtype=jnp.int32), col_count)
        rows_bias = jnp.einsum("ijhc,ikc->hijk", grid_query, row_table, precision=HIGH).reshape(
            head_count, local_count, total_rows
        )
        cols_bias = jnp.einsum("ijhc,jkc->hijk", grid_query, col_table, precision=HIGH).reshape(
            head_count, local_count, col_count
        )
        head_shape = (local_count, head_count, head_size)
        return (
            queries.reshape(head_shape),
            keys_low.reshape(head_shape),
            values_low.reshape(head_shape),
            rows_bias,
            cols_bias,
        )

    (queries, keys_local, values_local, rows_bias, cols_bias), pull_before = jax.vjp(
        before, image_flat, block_list
    )
    keys_send = keys_local.astype(jnp.bfloat16)
    values_send = values_local.astype(jnp.bfloat16)
    all_keys, all_values = (
        lax.all_gather(keys_send, "seq", axis=0, tiled=True),
        lax.all_gather(values_send, "seq", axis=0, tiled=True),
    )
    query_low = queries.astype(jnp.bfloat16)
    row_ids = jnp.arange(total_rows, dtype=jnp.int32)
    key_ok = (
        (row_ids[:, None] < valid_rows[0])
        & (jnp.arange(col_count, dtype=jnp.int32)[None, :] < valid_cols[0])
    ).reshape(seq_count, local_count)
    block_ids = jnp.arange(seq_count, dtype=jnp.int32)
    block_shape = (seq_count, local_count, head_count, head_size)

    def key_blocks(keys_full, values_full):
        return (block_ids, keys_full.reshape(block_shape), values_full.reshape(block_shape), key_ok)

    def block_scores(block_at, key_block, mask_block):
        raw = (
            jnp.einsum("qhc,khc->hqk", query_low, key_block, preferred_element_type=jnp.float32)
            * score_scale
        )
        rows_part = lax.dynamic_slice_in_dim(rows_bias, block_at * local_rows, local_rows, 2)
        position_bias = (rows_part[:, :, :, None] + cols_bias[:, :, None, :]).reshape(
            head_count, local_count, local_count
        )
        return jnp.where(mask_block[None, None, :], raw + position_bias, NEG)

    def stats_step(running, inputs):
        running_top, running_sum = running
        block_at, key_block, value_block, mask_block = inputs
        scores = block_scores(block_at, key_block, mask_block)
        new_top = jnp.maximum(running_top, scores.max(axis=-1))
        running_sum = running_sum * jnp.exp(running_top - new_top) + jnp.exp(
            scores - new_top[:, :, None]
        ).sum(axis=-1)
        return ((new_top, running_sum), None)

    start_top = jnp.full((head_count, local_count), NEG, jnp.float32)
    (top_score, score_total), _ = lax.scan(
        stats_step, (start_top, jnp.zeros_like(start_top)), key_blocks(all_keys, all_values)
    )
    log_total = top_score + jnp.log(score_total)

    def output_step(running, inputs):
        block_at, key_block, value_block, mask_block = inputs
        attention = jnp.exp(
            block_scores(block_at, key_block, mask_block) - log_total[:, :, None]
        ).astype(jnp.bfloat16)
        return (
            running
            + jnp.einsum(
                "hqk,khc->qhc", attention, value_block, preferred_element_type=jnp.float32
            ),
            None,
        )

    attended, _ = lax.scan(
        output_step,
        jnp.zeros((local_count, head_count, head_size), jnp.float32),
        key_blocks(all_keys, all_values),
    )

    def after(attended_in, flat_tokens, weights):
        rounded = narrow_grad(narrow_value(attended_in.reshape(local_count, model_width)))
        middle = flat_tokens + narrow_grad(narrow_product(rounded, weights[6]) + weights[7])
        normed_two = narrow_value(normalize(middle, weights[0][:, 1], weights[1][:, 1]))
        hidden = narrow_grad(narrow_product(normed_two, weights[8]) + weights[9])
        hidden = narrow_value(jax.nn.gelu(hidden, approximate=False))
        return middle + narrow_grad(narrow_product(hidden, weights[10]) + weights[11])

    block_out, pull_after = jax.vjp(after, attended, image_flat, block_list)

    def pyramid_inputs(block_values, weights):
        feature_map = block_values.reshape(local_rows, col_count, model_width)
        rounded = narrow_value(feature_map)
        fine_map = narrow_grad(deconvolve(rounded, weights[0], weights[1]))
        fine_map = narrow_value(
            jax.nn.gelu(normalize(fine_map, weights[2], weights[3]), approximate=False)
        )
        fine_map = narrow_grad(narrow_value(deconvolve(fine_map, weights[4].T, weights[5])))
        middle_map = narrow_grad(narrow_value(deconvolve(rounded, weights[6], weights[7])))
        coarse_map = rounded.reshape(local_rows // 2, 2, col_count // 2, 2, model_width).max(
            axis=(1, 3)
        )
        return (
            lateral_level(fine_map, weights[8], 0, weights),
            lateral_level(middle_map, weights[9], 1, weights),
            lateral_level(rounded, weights[10][:, 0, :], 2, weights),
            lateral_level(coarse_map, weights[10][:, 1, :], 3, weights),
        )

    def pyramid_outputs(padded_levels, weights):
        results = []
        for level_at in range(4):
            padded = jnp.pad(padded_levels[level_at], ((0, 0), (1, 1), (0, 0)))
            convolved = narrow_grad(conv_three(padded, weights[13][:, level_at, :]))
            results.append(
                normalize(convolved, weights[11][:, 4 + level_at], weights[12][:, 4 + level_at])
            )
        return tuple(results)

    level_inputs, pull_inputs = jax.vjp(pyramid_inputs, block_out, pyramid_list)
    padded_list = []
    for level_in in level_inputs:
        moved_rows = extended(level_in.astype(jnp.bfloat16), (("seq", 0),), 1)
        padded_list.append(moved_rows.astype(jnp.float32))
    level_maps, pull_outputs = jax.vjp(pyramid_outputs, tuple(padded_list), pyramid_list)
    cotangents = tuple(
        (
            cotan[0].astype(jnp.float32)
            for cotan in (cotan_fine, cotan_middle, cotan_base, cotan_coarse)
        )
    )
    grad_padded, grads_outputs = pull_outputs(cotangents)
    grad_levels = []
    for grad_in in grad_padded:
        rim_rows = jnp.stack([grad_in[0], grad_in[-1]])
        moved_grads = extended(shortened(rim_rows), (("seq", 0),), 1).astype(rim_rows.dtype)
        inner = grad_in[1:-1]
        inner = inner.at[0].add(moved_grads[0])
        inner = inner.at[-1].add(moved_grads[3])
        grad_levels.append(inner)
    grad_block_out, grads_inputs = pull_inputs(tuple(grad_levels))
    pyramid_grads = tuple(
        (
            from_outputs + from_inputs
            for from_outputs, from_inputs in zip(grads_outputs, grads_inputs)
        )
    )
    grad_attended, grad_tokens_after, grads_after = pull_after(grad_block_out)
    grad_out_low = grad_attended.astype(jnp.bfloat16)
    all_keys, all_values = (
        lax.all_gather(keys_send, "seq", axis=0, tiled=True),
        lax.all_gather(values_send, "seq", axis=0, tiled=True),
    )
    backward_blocks = key_blocks(all_keys, all_values)

    def delta_step(running, inputs):
        block_at, key_block, value_block, mask_block = inputs
        attention = jnp.exp(block_scores(block_at, key_block, mask_block) - log_total[:, :, None])
        grad_attention = jnp.einsum(
            "qhc,khc->hqk", grad_out_low, value_block, preferred_element_type=jnp.float32
        )
        return (running + (attention * grad_attention).sum(axis=-1), None)

    row_delta, _ = lax.scan(
        delta_step, jnp.zeros((head_count, local_count), jnp.float32), backward_blocks
    )

    def grad_step(running, inputs):
        grad_query, grad_cols = running
        block_at, key_block, value_block, mask_block = inputs
        attention = jnp.exp(block_scores(block_at, key_block, mask_block) - log_total[:, :, None])
        grad_attention = jnp.einsum(
            "qhc,khc->hqk", grad_out_low, value_block, preferred_element_type=jnp.float32
        )
        grad_scores = (attention * (grad_attention - row_delta[:, :, None])).astype(jnp.bfloat16)
        grad_query = (
            grad_query
            + jnp.einsum("hqk,khc->qhc", grad_scores, key_block, preferred_element_type=jnp.float32)
            * score_scale
        )
        grad_key_block = (
            jnp.einsum("hqk,qhc->khc", grad_scores, query_low, preferred_element_type=jnp.float32)
            * score_scale
        )
        grad_value_block = jnp.einsum(
            "hqk,qhc->khc",
            attention.astype(jnp.bfloat16),
            grad_out_low,
            preferred_element_type=jnp.float32,
        )
        scores_grid = grad_scores.astype(jnp.float32).reshape(
            head_count, local_count, local_rows, col_count
        )
        grad_cols = grad_cols + scores_grid.sum(axis=2)
        return (
            (grad_query, grad_cols),
            (grad_key_block, grad_value_block, scores_grid.sum(axis=3)),
        )

    start_grads = (
        jnp.zeros((local_count, head_count, head_size), jnp.float32),
        jnp.zeros((head_count, local_count, col_count), jnp.float32),
    )
    (grad_query, grad_cols), (key_parts, value_parts, row_parts) = lax.scan(
        grad_step, start_grads, backward_blocks
    )
    whole_shape = (total_rows * col_count, head_count, head_size)
    grad_keys, grad_values = (
        lax.psum_scatter(
            key_parts.reshape(whole_shape).astype(jnp.bfloat16),
            "seq",
            scatter_dimension=0,
            tiled=True,
        ).astype(jnp.float32),
        lax.psum_scatter(
            value_parts.reshape(whole_shape).astype(jnp.bfloat16),
            "seq",
            scatter_dimension=0,
            tiled=True,
        ).astype(jnp.float32),
    )
    grad_rows = row_parts.transpose(1, 2, 0, 3).reshape(head_count, local_count, total_rows)
    grad_tokens_before, grads_before = pull_before(
        (grad_query, grad_keys, grad_values, grad_rows, grad_cols)
    )
    block_grads = tuple(
        (from_before + from_after for from_before, from_after in zip(grads_before, grads_after))
    )
    all_shards = jax.tree.map(
        lambda part: part.astype(jnp.float32),
        lax.psum_scatter(
            shortened(block_grads + pyramid_grads), "img", scatter_dimension=0, tiled=True
        ),
    )
    totals = jax.tree.map(
        lambda part: part.astype(jnp.float32), lax.psum(shortened(all_shards), "seq")
    )
    token_grad = (grad_tokens_before + grad_tokens_after).reshape(
        1, local_rows, col_count, model_width
    )
    return (
        level_maps[0].astype(jnp.bfloat16)[None],
        level_maps[1].astype(jnp.bfloat16)[None],
        level_maps[2].astype(jnp.bfloat16)[None],
        level_maps[3].astype(jnp.bfloat16)[None],
        token_grad,
        totals[0],
        totals[1],
        totals[2],
        totals[3],
        totals[4],
        totals[5],
        totals[6],
        totals[7],
        totals[8],
        totals[9],
        totals[10],
        totals[11],
        totals[12],
        totals[13],
        totals[14],
        totals[15],
        totals[16],
        totals[17],
        totals[18],
        totals[19],
        totals[20],
        totals[21],
        totals[22],
        totals[23],
        totals[24],
        totals[25],
    )


def solution(mesh):
    in_specs = (
        P("img", "seq", None, None),
        P("img"),
        P("img"),
        P(),
        P(),
        P(),
        P(),
        P(),
        P(),
        P(),
        P(),
        P(),
        P(),
        P(),
        P(),
        P(),
        P(),
        P(),
        P(),
        P(),
        P(),
        P(),
        P(),
        P(),
        P(),
        P(),
        P(),
        P(),
        P(),
        P("img", "seq", None, None),
        P("img", "seq", None, None),
        P("img", "seq", None, None),
        P("img", "seq", None, None),
    )
    out_specs = (
        P("img", "seq", None, None),
        P("img", "seq", None, None),
        P("img", "seq", None, None),
        P("img", "seq", None, None),
        P("img", "seq", None, None),
        P("img", None),
        P("img", None),
        P("img", None),
        P("img", None),
        P("img", None),
        P("img", None),
        P("img", None),
        P("img"),
        P("img", None),
        P("img"),
        P("img", None),
        P("img"),
        P("img", None),
        P("img"),
        P("img"),
        P("img"),
        P("img", None),
        P("img"),
        P("img", None),
        P("img"),
        P("img", None),
        P("img", None),
        P("img", None, None),
        P("img", None),
        P("img", None),
        P("img", None, None),
    )
    return jax.shard_map(
        per_device, mesh=mesh, in_specs=in_specs, out_specs=out_specs, check_vma=False
    )
```

profile of v0, /device:TPU:0, one launch (start us, length us, event | category | flops | bytes accessed | tf_op | source)
XLA Modules:
  0.0 2213.5 jit_solution(8773625988387191994)
XLA Ops:
  117.9 38.1 %while.66 = (s32[]{:T(128)}, f32[12,512]{1,0:T(8,128)}, f32[12,512]{1,0:T(8,128)}, pred[2,512]{1,0:T(4,128)(4,1)S(1)}, bf16[2,512,12,64]{1,3,2,0:T(8,128)(2,1)},...) while((s32[]{:T(128)}, f32[12,512]{1,0:T(8,128)}, ...), condition=%wide.wide.region_5.6_spmd.clone, body=%wide.wide.region_2.5_spmd.clone.sunk | while | flops 424704000 | bytes 64120676 | solution.py:290
  157.4 35.7 %while.67 = (s32[]{:T(128)}, f32[512,12,64]{0,2,1:T(8,128)}, bf16[2,512,12,64]{1,3,2,0:T(8,128)(2,1)}, pred[2,512]{1,0:T(4,128)(4,1)S(1)}, bf16[2,512,12,64]{1,3...) while((s32[]{:T(128)}, f32[512,12,64]{0,2,1:T(8,128)}, ...), condition=%wide.wide.region_7.8_spmd.clone, body=%wide.wide.region_6.7_spmd.clone.sunk | while | flops 824967168 | bytes 61278040 | solution.py:308
  198.4 18.6 multiply_convert_fusion
  310.8 12.6 copy.303
  323.5 10.9 reshape.1559
  609.0 19.7 fusion.366
  804.8 29.1 %fusion.362 = (bf16[34,258,256]{2,1,0:T(8,128)(2,1)S(1)}, f32[34,258,256]{2,1,0:T(8,128)}) fusion(f32[32,256,256]{2,1,0:T(8,128)} %fusion.170, f32[32,256,256]{2,1,0:T(8,128)} %fusion.172, f32[32,256,256]{2,1,0:T(8,128)} %fusion.174, f32[32,256,256]{2,1,0:T(8,128)} %fusion.176, f32[32,256,256]{2,1,0:T(8,128)} %fusion.178, f32[32,256,256]{2,1,0:T(8,128)} %fusion.180, ...), kind=kLoop, calls=%fused_computation.757 | loop fusion | flops 20210688 | bytes 88971264 | tf_op jit(solution)/shard_map/convert.16
  902.9 10.8 copy.342
  965.9 42.0 %while.68 = (s32[]{:T(128)}, f32[12,512]{1,0:T(8,128)}, pred[2,512]{1,0:T(4,128)(4,1)S(1)}, bf16[2,512,12,64]{1,3,2,0:T(8,128)(2,1)}, bf16[512,12,64]{0,2,1:T(8,...) while((s32[]{:T(128)}, f32[12,512]{1,0:T(8,128)}, ...), condition=%wide.wide.region_52.53_spmd.clone, body=%wide.wide.region_50.52_spmd.clone.sunk | while | flops 827332608 | bytes 74942384 | solution.py:397
  1007.9 69.5 %while.69 = (s32[]{:T(128)}, f32[512,12,64]{0,2,1:T(8,128)}, f32[12,512,64]{1,2,0:T(8,128)}, bf16[2,512,12,64]{1,3,2,0:T(8,128)(2,1)}, bf16[2,512,12,64]{1,3,2,0...) while((s32[]{:T(128)}, f32[512,12,64]{0,2,1:T(8,128)}, ...), condition=%wide.wide.region_56.57_spmd.clone, body=%wide.wide.region_53.56_spmd.clone.sunk | while | flops 2056077312 | bytes 181537008 | solution.py:437
  1322.1 35.6 %fusion = bf16[16,256]{1,0:T(8,128)(2,1)} fusion(bf16[192,256]{1,0:T(8,128)(2,1)} %convolution_convert_fusion.10), kind=kCustom, calls=%all-reduce-scatter | all-reduce-scatter fusion | flops 65537 | bytes 107008
  1385.6 58.9 %all-reduce.119 = (bf16[64,31]{1,0:T(8,128)(2,1)}, bf16[64,127]{1,0:T(8,128)(2,1)}, bf16[768]{0:T(1024)(128)(2,1)}, bf16[3072]{0:T(1024)(128)(2,1)}, bf16[768]{0...) all-reduce(bf16[64,31]{1,0:T(8,128)(2,1)} %fusion.119, ...), channel_id=8, replica_groups=mesh['img'=16,'seq'=2] {'img'}, use_global_device_ids=true, to_apply=%region_75.76.clone | all-reduce | flops 16448 | bytes 65792
  1471.9 20.9 reduce-scatter.48.cloned.1.call-done
  1492.8 58.0 %reduce-scatter.44.cloned.1.call-done = bf16[48,384]{1,0:T(8,128)(2,1)} async-done(((bf16[768,384]{1,0:T(8,128)(2,1)}), bf16[48,384]{1,0:T(8,128)(2,1)}) %reduce-scatter.44.cloned.1.call-update) | async-done | bytes 36880 | tf_op jit(solution)/shard_map/reduce_scatter | solution.py:464
  1550.8 60.1 %reduce-scatter.50.cloned.1.call-done = bf16[48,2,256]{2,0,1:T(8,128)(2,1)} async-done(((bf16[768,2,256]{2,0,1:T(8,128)(2,1)}), bf16[48,2,256]{2,0,1:T(8,128)(2,1)}) %reduce-scatter.50.cloned.1.call-update) | async-done | bytes 49168 | tf_op jit(solution)/shard_map/reduce_scatter | solution.py:464
  1613.1 58.5 %reduce-scatter.36.cloned.1.call-done = bf16[48,768]{1,0:T(8,128)(2,1)} async-done(((bf16[768,768]{1,0:T(8,128)(2,1)}), bf16[48,768]{1,0:T(8,128)(2,1)}) %reduce-scatter.36.cloned.1.call-update) | async-done | bytes 73744 | tf_op jit(solution)/shard_map/reduce_scatter | solution.py:464
  1671.6 65.6 %reduce-scatter.46.cloned.1.call-done = bf16[48,1536]{1,0:T(8,128)(2,1)} async-done(((bf16[768,1536]{1,0:T(8,128)(2,1)}), bf16[48,1536]{1,0:T(8,128)(2,1)}) %reduce-scatter.46.cloned.1.call-update) | async-done | bytes 147472 | tf_op jit(solution)/shard_map/reduce_scatter | solution.py:464
  1737.2 66.0 %reduce-scatter.42.cloned.1.call-done = bf16[48,1536]{1,0:T(8,128)(2,1)} async-done(((bf16[768,1536]{1,0:T(8,128)(2,1)}), bf16[48,1536]{1,0:T(8,128)(2,1)}) %reduce-scatter.42.cloned.1.call-update) | async-done | bytes 147472 | tf_op jit(solution)/shard_map/reduce_scatter | solution.py:464
  1803.2 78.4 %reduce-scatter.52.cloned.1.call-done = bf16[144,4,256]{2,0,1:T(8,128)(2,1)} async-done(((bf16[2304,4,256]{2,0,1:T(8,128)(2,1)}), bf16[144,4,256]{2,0,1:T(8,128)(2,1)}) %reduce-scatter.52.cloned.1.call-update) | async-done | bytes 294928 | tf_op jit(solution)/shard_map/reduce_scatter | solution.py:464
  1881.5 78.8 %reduce-scatter.40.cloned.1.call-done = bf16[192,768]{1,0:T(8,128)(2,1)} async-done(((bf16[3072,768]{1,0:T(8,128)(2,1)}), bf16[192,768]{1,0:T(8,128)(2,1)}) %reduce-scatter.40.cloned.1.call-update) | async-done | bytes 294928 | tf_op jit(solution)/shard_map/reduce_scatter | solution.py:464
  1960.3 78.3 %reduce-scatter.38.cloned.1.call-done = bf16[48,3072]{1,0:T(8,128)(2,1)} async-done(((bf16[768,3072]{1,0:T(8,128)(2,1)}), bf16[48,3072]{1,0:T(8,128)(2,1)}) %reduce-scatter.38.cloned.1.call-update) | async-done | bytes 294928 | tf_op jit(solution)/shard_map/reduce_scatter | solution.py:464
  2038.7 72.0 %reduce-scatter.34.cloned.1.call-done = bf16[48,2304]{1,0:T(8,128)(2,1)} async-done(((bf16[768,2304]{1,0:T(8,128)(2,1)}), bf16[48,2304]{1,0:T(8,128)(2,1)}) %reduce-scatter.34.cloned.1.call-update) | async-done | bytes 221200 | tf_op jit(solution)/shard_map/reduce_scatter | solution.py:464
  2123.0 18.9 all-reduce.125.cloned.1.call-done
  2165.2 30.0 %all-reduce.127.cloned.1.call-done = (bf16[144,4,256]{2,0,1:T(8,128)(2,1)}, bf16[48,2304]{1,0:T(8,128)(2,1)}, bf16[48,768]{1,0:T(8,128)(2,1)}, bf16[48,3072]{1,0...) async-done(((bf16[144,4,256]{2,0,1:T(8,128)(2,1)}, bf16[48,2304]{1,0:T(8,128)(2,1)}, bf16[48,768]{1,0:T(8,128)(2,1)}, ...) | async-done | bytes 1474576 | tf_op jit(solution)/shard_map/psum | solution.py:469
  (1336 shorter events, 1300.9 us)
Async XLA Ops:
  27.7 1136.8 %reduce-scatter.30.cloned.1.call-start = ((), (), s32[]{:S(2)}) async-start(), calls=%async_computation.19 | async-start | bytes 2359296 | tf_op jit(solution)/shard_map/reduce_scatter | solution.py:448
  261.5 143.8 %collective-permute-start.4 = (bf16[1,64,256]{1,2,0:T(8,128)(2,1)}, bf16[1,64,256]{1,2,0:T(8,128)(2,1)}, u32[]{:S(2)}, u32[]{:S(2)}) collective-permute-start(bf16[1,64,256]{1,2,0:T(8,128)(2,1)} %get-tuple-element.1056), channel_id=1, source_target_pairs={{0,1},{2,3},{4,5},{6,7},{8,9},{10,11},{12,13},{14,15},{16,17},{18,... | collective-permute-start | bytes 98312 | tf_op jit(solution)/shard_map/ppermute | solution.py:17
  267.0 141.6 %collective-permute-start.5 = (bf16[1,64,256]{1,2,0:T(8,128)(2,1)}, bf16[1,64,256]{1,2,0:T(8,128)(2,1)}, u32[]{:S(2)}, u32[]{:S(2)}) collective-permute-start(bf16[1,64,256]{1,2,0:T(8,128)(2,1)} %get-tuple-element.1057), channel_id=1, source_target_pairs={{1,0},{3,2},{5,4},{7,6},{9,8},{11,10},{13,12},{15,14},{17,16},{19,... | collective-permute-start | bytes 98312 | tf_op jit(solution)/shard_map/ppermute | solution.py:18
  364.6 210.6 %collective-permute-start = (bf16[1,256,256]{1,2,0:T(8,128)(2,1)}, bf16[1,256,256]{1,2,0:T(8,128)(2,1)}, u32[]{:S(2)}, u32[]{:S(2)}) collective-permute-start(bf16[1,256,256]{1,2,0:T(8,128)(2,1)} %get-tuple-element.1030), channel_id=1, source_target_pairs={{0,1},{2,3},{4,5},{6,7},{8,9},{10,11},{12,13},{14,15},{16,17},{18,... | collective-permute-start | bytes 393224 | tf_op jit(solution)/shard_map/ppermute | solution.py:17
  448.3 128.8 %collective-permute-start.1 = (bf16[1,256,256]{1,2,0:T(8,128)(2,1)}, bf16[1,256,256]{1,2,0:T(8,128)(2,1)}, u32[]{:S(2)}, u32[]{:S(2)}) collective-permute-start(bf16[1,256,256]{1,2,0:T(8,128)(2,1)} %get-tuple-element.1031), channel_id=1, source_target_pairs={{1,0},{3,2},{5,4},{7,6},{9,8},{11,10},{13,12},{15,14},{17,16},{19,... | collective-permute-start | bytes 393224 | tf_op jit(solution)/shard_map/ppermute | solution.py:18
  566.3 210.0 %collective-permute-start.12 = (bf16[1,128,256]{2,1,0:T(8,128)(2,1)}, bf16[1,128,256]{2,1,0:T(8,128)(2,1)}, u32[]{:S(2)}, u32[]{:S(2)}) collective-permute-start(bf16[1,128,256]{2,1,0:T(8,128)(2,1)} %get-tuple-element.1038), channel_id=1, source_target_pairs={{0,1},{2,3},{4,5},{6,7},{8,9},{10,11},{12,13},{14,15},{16,17},{18,... | collective-permute-start | bytes 196616 | tf_op jit(solution)/shard_map/ppermute | solution.py:17
  572.4 204.1 %collective-permute-start.13 = (bf16[1,128,256]{2,1,0:T(8,128)(2,1)}, bf16[1,128,256]{2,1,0:T(8,128)(2,1)}, u32[]{:S(2)}, u32[]{:S(2)}) collective-permute-start(bf16[1,128,256]{2,1,0:T(8,128)(2,1)} %get-tuple-element.1039), channel_id=1, source_target_pairs={{1,0},{3,2},{5,4},{7,6},{9,8},{11,10},{13,12},{15,14},{17,16},{19,... | collective-permute-start | bytes 196616 | tf_op jit(solution)/shard_map/ppermute | solution.py:18
  1092.3 364.9 %reduce-scatter.62.cloned.1.call-start = ((), (), s32[]{:S(2)}) async-start(), calls=%async_computation.35 | async-start | bytes 69632
  1157.8 300.7 %reduce-scatter.60.cloned.1.call-start = ((), (), s32[]{:S(2)}) async-start(), calls=%async_computation.34 | async-start | bytes 69632
  1164.4 303.6 %reduce-scatter.58.cloned.1.call-start = ((), (), s32[]{:S(2)}) async-start(), calls=%async_computation.33 | async-start | bytes 208896
  1176.0 293.2 %reduce-scatter.54.cloned.1.call-start = ((), (), s32[]{:S(2)}) async-start(), calls=%async_computation.31 | async-start | bytes 208896
  1178.3 292.2 %reduce-scatter.56.cloned.1.call-start = ((), (), s32[]{:S(2)}) async-start(), calls=%async_computation.32 | async-start | bytes 208896
  1179.5 313.3 %reduce-scatter.48.cloned.1.call-start = ((), (), s32[]{:S(2)}) async-start(), calls=%async_computation.28 | async-start | bytes 208896 | tf_op jit(solution)/shard_map/reduce_scatter | solution.py:464
  1182.5 368.2 %reduce-scatter.44.cloned.1.call-start = ((), (), s32[]{:S(2)}) async-start(), calls=%async_computation.26 | async-start | bytes 626688 | tf_op jit(solution)/shard_map/reduce_scatter | solution.py:464
  1195.3 415.5 %reduce-scatter.50.cloned.1.call-start = ((), (), s32[]{:S(2)}) async-start(), calls=%async_computation.29 | async-start | bytes 835584 | tf_op jit(solution)/shard_map/reduce_scatter | solution.py:464
  1205.1 466.4 %reduce-scatter.36.cloned.1.call-start = ((), (), s32[]{:S(2)}) async-start(), calls=%async_computation.22 | async-start | bytes 1253376 | tf_op jit(solution)/shard_map/reduce_scatter | solution.py:464
  1212.9 524.3 %reduce-scatter.46.cloned.1.call-start = ((), (), s32[]{:S(2)}) async-start(), calls=%async_computation.27 | async-start | bytes 2506752 | tf_op jit(solution)/shard_map/reduce_scatter | solution.py:464
  1233.9 569.3 %reduce-scatter.42.cloned.1.call-start = ((), (), s32[]{:S(2)}) async-start(), calls=%async_computation.25 | async-start | bytes 2506752 | tf_op jit(solution)/shard_map/reduce_scatter | solution.py:464
  1261.2 620.3 %reduce-scatter.52.cloned.1.call-start = ((), (), s32[]{:S(2)}) async-start(), calls=%async_computation.30 | async-start | bytes 5013504 | tf_op jit(solution)/shard_map/reduce_scatter | solution.py:464
  1283.1 677.2 %reduce-scatter.40.cloned.1.call-start = ((), (), s32[]{:S(2)}) async-start(), calls=%async_computation.24 | async-start | bytes 5013504 | tf_op jit(solution)/shard_map/reduce_scatter | solution.py:464
  1290.2 748.5 %reduce-scatter.38.cloned.1.call-start = ((), (), s32[]{:S(2)}) async-start(), calls=%async_computation.23 | async-start | bytes 5013504 | tf_op jit(solution)/shard_map/reduce_scatter | solution.py:464
  1297.3 813.4 %reduce-scatter.34.cloned.1.call-start = ((), (), s32[]{:S(2)}) async-start(), calls=%async_computation.21 | async-start | bytes 3760128 | tf_op jit(solution)/shard_map/reduce_scatter | solution.py:464
  1303.7 838.1 %all-reduce.125.cloned.1.call-start = ((), (), s32[]{:S(2)}) async-start(), calls=%async_computation.36 | async-start | bytes 236544 | tf_op jit(solution)/shard_map/psum | solution.py:469
  1610.9 584.4 %all-reduce.127.cloned.1.call-start = ((), (), s32[]{:S(2)}) async-start(), calls=%async_computation.37 | async-start | bytes 2949120 | tf_op jit(solution)/shard_map/psum | solution.py:469
  (345 other events, 4632.0 us)
Sparse Core Ops, SparseCore 0:
  22.1 29.8 all-gather.4
  53.6 27.1 all-gather.2
  1080.3 28.3 reduce-scatter.29
  1110.9 26.0 reduce-scatter.31
  1157.9 54.7 reduce-scatter.61
  1216.9 50.9 reduce-scatter.59
  1271.4 52.6 reduce-scatter.57
  1327.6 52.7 reduce-scatter.53
  1383.9 52.7 reduce-scatter.55
  1440.0 52.7 reduce-scatter.47
  1496.9 53.8 reduce-scatter.43
  1555.2 55.6 reduce-scatter.49
  1614.4 57.1 reduce-scatter.35
  1675.2 61.9 reduce-scatter.45
  1741.3 61.8 reduce-scatter.41
  1806.9 74.5 reduce-scatter.51
  1885.7 74.5 reduce-scatter.39
  1964.1 74.5 reduce-scatter.37
  2043.6 67.0 reduce-scatter.33
  2116.9 24.8 all-reduce.124
  2144.8 50.3 all-reduce.126
where the time goes:
time: 2230 us; the launch traced here: 2210 us
  waiting for transfers between devices  686 us (31%)
  matrix products  501 us (22%)
  local copies, waits for them, and re-layouts  490 us (22%)
  other arithmetic  349 us (16%)
  blocking collectives  94.5 us (4%)
  starting transfers between devices  62.3 us (3%)
  between operations  24 us (1%)
    reduce_scatter x10, waiting for transfers between devices, per_device(): lax.psum_scatter(shortened(block_grads + pyramid_grads), 'img', scatter_d...  637 us
    dot_general x94, matrix products, narrow_product(): return multiply(left, right)  252 us
    slice x24, local copies, waits for them, and re-layouts, conv_three(): padded[offset_row:offset_row + rows_out, offset_col:offset_col + cols_out]  104 us
    dot_general x47, matrix products, plain_product(): jnp.dot(left.astype(jnp.bfloat16), right.astype(jnp.bfloat16), preferred_...  102 us
    unnamed x2, blocking collectives  94.5 us
    unnamed x561, local copies, waits for them, and re-layouts  82.6 us
    convert_element_type x11, local copies, waits for them, and re-layouts, narrow_product(): return multiply(left, right)  62 us
    reduce_sum x21, other arithmetic, normalize(): return centred * lax.rsqrt(spread + 1e-06) * gain_vec + shift_vec  58.4 us
  transfers between devices with their start and end apart: 41, of which 12 were waited for; matrix products, arithmetic and copies ran while one was open for 41% of the time, Pallas kernels for 0%

commit v1 on v0

v1 whole, which is shorter than its diff:
```python
import functools

import jax
import jax.numpy as jnp
from jax import lax
from jax.experimental import pallas as pl
from jax.experimental.pallas import tpu as pltpu
from jax.sharding import PartitionSpec as P

F32 = jnp.float32
BF = jnp.bfloat16
NEG = -1e30
EPS = 1e-6
SQRT_HALF = 0.7071067811865476
INV_SQRT_2PI = 0.3989422804014327
VMEM_LIMIT = 60 * 1024 * 1024


def mm(left, right):
    return lax.dot_general(left, right, (((1,), (0,)), ((), ())), preferred_element_type=F32)


def mt(left, right):
    return lax.dot_general(left, right, (((1,), (1,)), ((), ())), preferred_element_type=F32)


def tm(left, right):
    return lax.dot_general(left, right, (((0,), (0,)), ((), ())), preferred_element_type=F32)


def call(
    kernel, outs, grid=(), in_specs=None, out_specs=None, scratch=(), flops=0, name=None, aliases=None
):
    return pl.pallas_call(
        kernel,
        out_shape=outs,
        grid=grid,
        in_specs=in_specs,
        out_specs=out_specs,
        scratch_shapes=scratch,
        name=name,
        input_output_aliases=aliases or {},
        cost_estimate=pl.CostEstimate(flops=int(flops), bytes_accessed=0, transcendentals=0),
        compiler_params=pltpu.CompilerParams(vmem_limit_bytes=VMEM_LIMIT),
    )


def whole(shape):
    return pl.BlockSpec(shape, lambda *_: (0,) * len(shape))


def sds(shape, dtype):
    return jax.ShapeDtypeStruct(shape, dtype)


def stats(values):
    average = jnp.mean(values, axis=-1, keepdims=True)
    centred = values - average
    spread = jnp.mean(centred * centred, axis=-1, keepdims=True)
    inverse = lax.rsqrt(spread + EPS)
    return centred * inverse, inverse


def norm_back(grad_hat, hat, inverse):
    first = jnp.mean(grad_hat, axis=-1, keepdims=True)
    second = jnp.mean(grad_hat * hat, axis=-1, keepdims=True)
    return inverse * (grad_hat - first - hat * second)


def rowsum(values):
    return jnp.sum(values, axis=0, keepdims=True)


def gelu_pair(values):
    half = 0.5 * (1.0 + lax.erf(values * SQRT_HALF))
    slope = half + values * (jnp.exp(-0.5 * values * values) * INV_SQRT_2PI)
    return values * half, slope


def shift_matrix(size, amount):
    out_at = lax.broadcasted_iota(jnp.int32, (size, size), 0)
    in_at = lax.broadcasted_iota(jnp.int32, (size, size), 1)
    return jnp.where(in_at == out_at + amount, 1.0, 0.0).astype(BF)


def weave_matrix(size, ways, inverse=False):
    out_at = lax.broadcasted_iota(jnp.int32, (size, size), 1 if inverse else 0)
    in_at = lax.broadcasted_iota(jnp.int32, (size, size), 0 if inverse else 1)
    source = lax.rem(out_at, ways) * (size // ways) + lax.div(out_at, ways)
    return jnp.where(in_at == source, 1.0, 0.0).astype(BF)


def qkv_kernel(x_ref, w_ref, b_ref, p_ref, out_ref, n1_ref):
    @pl.when(pl.program_id(1) == 0)
    def _():
        for at in range(0, x_ref.shape[0], 32):
            hat, _ = stats(x_ref[at : at + 32, :].astype(F32))
            n1_ref[at : at + 32, :] = (hat * p_ref[0:1, :] + p_ref[2:3, :]).astype(BF)

    out_ref[...] = (mm(n1_ref[...], w_ref[...]) + b_ref[0]).astype(BF)


def qkv_call(tokens, weight, bias3, p768, first):
    rows, width = tokens.shape
    block = 512
    count = 3 - first
    return call(
        qkv_kernel,
        sds((rows, count * width), BF),
        grid=(rows // block, count),
        in_specs=[
            pl.BlockSpec((block, width), lambda i, j: (i, 0)),
            pl.BlockSpec((width, width), lambda i, j: (0, j + first)),
            pl.BlockSpec((1, 1, width), lambda i, j: (j + first, 0, 0)),
            whole(p768.shape),
        ],
        out_specs=pl.BlockSpec((block, width), lambda i, j: (i, j)),
        scratch=[pltpu.VMEM((block, width), BF)],
        flops=2 * rows * width * width * count,
        name="qkv",
    )(tokens, weight, bias3, p768)


def aug_layout(total_rows):
    low_at = 64 + total_rows
    if low_at + total_rows + 1 > 128:
        low_at = 128
    width = 128 * (2 + (low_at + total_rows) // 128)
    return low_at, width


def build_kaug(kaug_ref, k_refs, oh1_ref, oh2_ref, odd):
    lane = lax.broadcasted_iota(jnp.int32, (512, 128), 1)
    mine = (lane >= 64) if odd else (lane < 64)
    at = 0
    for k_ref in k_refs:
        for row in range(0, k_ref.shape[0], 512):
            keys = k_ref[row : row + 512, :].astype(F32)
            hot = oh1_ref[at : at + 512, :].astype(F32)
            kaug_ref[at : at + 512, 0:128] = jnp.where(mine, keys, hot).astype(BF)
            at += 512


def build_qaug(first_row, qp, tw_ref, tr_ref, qaug_ref, odd, total_rows, scale):
    low_at, width = aug_layout(total_rows)
    tokens = qp.shape[0]
    lane = lax.broadcasted_iota(jnp.int32, (64, 128), 1)
    mine = (lane >= 64) if odd else (lane < 64)
    lane_all = lax.broadcasted_iota(jnp.int32, (tokens, 128), 1)
    mine_all = (lane_all >= 64) if odd else (lane_all < 64)
    qf = qp.astype(F32)
    qm = jnp.where(mine_all, qf, 0.0).astype(BF)
    cols = mm(qm, tw_ref[...])
    rows = mm(qm, tr_ref[...])
    for i in range(tokens // 64):
        sl = slice(64 * i, 64 * i + 64)
        upper = pltpu.roll(cols[sl], 1, 1, stride=1, stride_axis=0)
        lower = pltpu.roll(cols[sl], 65, 1, stride=1, stride_axis=0)
        first = jnp.where(mine, qf[sl] * scale, lower if odd else upper)
        col_low = lower - lower.astype(BF).astype(F32)
        shift = lax.rem(first_row + i + (65 - total_rows + 128), 128)
        row_part = pltpu.roll(rows[sl], shift, 1)
        row_low = row_part - row_part.astype(BF).astype(F32)
        qaug_ref[sl, 0:128] = first.astype(BF)
        one_at = low_at + total_rows
        if low_at < 128:
            rest = jnp.where(lane == one_at, 1.0, 0.0)
            rest = jnp.where(
                (lane >= low_at) & (lane < one_at), pltpu.roll(row_low, total_rows, 1), rest
            )
            second = jnp.where(lane < 64, col_low, jnp.where(lane < low_at, row_part, rest))
            qaug_ref[sl, 128:256] = second.astype(BF)
        else:
            second = jnp.where(
                lane < 64, col_low, jnp.where(lane < 64 + total_rows, row_part, 0.0)
            )
            third = jnp.where(
                lane < total_rows,
                pltpu.roll(row_low, 64, 1),
                jnp.where(lane == total_rows, 1.0, 0.0),
            )
            qaug_ref[sl, 128:256] = second.astype(BF)
            qaug_ref[sl, 256:384] = third.astype(BF)


def attend_kernel(total_rows, scale, others, *refs):
    first_ref, q_ref, tw_ref, tr_ref, oh1_ref, oh2_ref = refs[:6]
    k_refs = refs[6 : 6 + others]
    v_refs = refs[6 + others : 6 + 2 * others]
    o_ref, qaug_out, lse_ref, kaug_ref, v_ref, p_ref, ot_ref = refs[6 + 2 * others :]
    first_row = first_ref[0]
    tokens = q_ref.shape[0]
    keys = kaug_ref.shape[0]

    @pl.when(pl.program_id(0) == 0)
    def _():
        kaug_ref[:, 128:] = oh2_ref[...]

    at = 0
    for ref in v_refs:
        v_ref[at : at + ref.shape[0], :] = ref[...]
        at += ref.shape[0]
    qp = q_ref[...]
    for odd in (0, 1):
        build_kaug(kaug_ref, k_refs, oh1_ref, oh2_ref, odd)
        build_qaug(first_row, qp, tw_ref, tr_ref, qaug_out.at[odd], odd, total_rows, scale)
        for t in range(0, tokens, 256):
            scores = mt(kaug_ref[...], qaug_out[odd, t : t + 256, :])
            top = jnp.max(scores, axis=0, keepdims=True)
            total = jnp.zeros((1, 256), F32)
            for c in range(0, keys, 128):
                weight = jnp.exp(scores[c : c + 128] - top)
                total = total + rowsum(weight)
                p_ref[c : c + 128, :] = weight.astype(BF)
            lse_ref[0, odd : odd + 1, t : t + 256] = top + jnp.log(total)
            out_t = tm(v_ref[...], p_ref[...])
            ot_ref[64 * odd : 64 * odd + 64, t : t + 256] = (
                out_t[64 * odd : 64 * odd + 64] / total
            )
    o_ref[...] = ot_ref[...].T.astype(BF)


def attend_call(first, qkv_own, kv_others, tables, oh1, oh2, total_rows, heads):
    tokens = qkv_own.shape[0]
    width = qkv_own.shape[1] // 3
    keys = oh1.shape[0]
    aug = 128 + oh2.shape[1]
    pairs = width // 128
    tw, tr = tables
    parts = 1 + (1 if kv_others is not None else 0)
    in_specs = [
        pl.BlockSpec(memory_space=pltpu.SMEM),
        pl.BlockSpec((tokens, 128), lambda h: (0, h)),
        whole(tw.shape),
        whole(tr.shape),
        whole(oh1.shape),
        whole(oh2.shape),
    ]
    k_args, v_args, k_specs, v_specs = [qkv_own], [qkv_own], [], []
    k_specs.append(pl.BlockSpec((tokens, 128), lambda h: (0, h + pairs)))
    v_specs.append(pl.BlockSpec((tokens, 128), lambda h: (0, h + 2 * pairs)))
    if kv_others is not None:
        k_args.append(kv_others)
        v_args.append(kv_others)
        k_specs.append(pl.BlockSpec((keys - tokens, 128), lambda h: (0, h)))
        v_specs.append(pl.BlockSpec((keys - tokens, 128), lambda h: (0, h + pairs)))
    scale = (width // heads) ** -0.5
    return call(
        functools.partial(attend_kernel, total_rows, scale, parts),
        [
            sds((tokens, width), BF),
            sds((heads, tokens, aug), BF),
            sds((pairs, 2, tokens), F32),
        ],
        grid=(pairs,),
        in_specs=in_specs + k_specs + v_specs,
        out_specs=[
            pl.BlockSpec((tokens, 128), lambda h: (0, h)),
            pl.BlockSpec((2, tokens, aug), lambda h: (h, 0, 0)),
            pl.BlockSpec((1, 2, tokens), lambda h: (h, 0, 0)),
        ],
        scratch=[
            pltpu.VMEM((keys, aug), BF),
            pltpu.VMEM((keys, 128), BF),
            pltpu.VMEM((keys, 256), BF),
            pltpu.VMEM((128, tokens), F32),
        ],
        flops=12e9,
        name="attend",
    )(first, qkv_own, tw, tr, oh1, oh2, *k_args, *v_args)


def mlp_kernel(
    x_ref, o_ref, wp_ref, w1_ref, b1_ref, w2_ref, p_ref, x1_ref, g_ref, gp_ref, y_ref, n2_ref, acc_ref
):
    step = pl.program_id(0)
    tokens = x_ref.shape[0]

    @pl.when(step == 0)
    def _():
        product = mm(o_ref[...], wp_ref[...])
        for at in range(0, tokens, 32):
            sl = slice(at, at + 32)
            middle = x_ref[sl, :].astype(F32) + (product[sl] + p_ref[6:7, :])
            x1_ref[sl, :] = middle
            hat, _ = stats(middle)
            n2_ref[sl, :] = (hat * p_ref[1:2, :] + p_ref[3:4, :]).astype(BF)

    hidden = mm(n2_ref[...], w1_ref[...])
    for at in range(0, tokens, 32):
        sl = slice(at, at + 32)
        value, slope = gelu_pair(hidden[sl] + b1_ref[...])
        g_ref[sl, :] = value.astype(BF)
        gp_ref[sl, :] = slope.astype(BF)
    part = mm(g_ref[...], w2_ref[...])

    @pl.when(step == 0)
    def _():
        acc_ref[...] = part

    @pl.when(step > 0)
    def _():
        acc_ref[...] += part

    @pl.when(step == pl.num_programs(0) - 1)
    def _():
        y_ref[...] = (x1_ref[...] + (acc_ref[...] + p_ref[7:8, :])).astype(BF)


def mlp_call(tokens, attended, wp, w1, b1, w2, p768):
    rows, width = tokens.shape
    hidden = w1.shape[1]
    return call(
        mlp_kernel,
        [sds((rows, width), F32), sds((rows, hidden), BF), sds((rows, hidden), BF), sds((rows, width), BF)],
        grid=(hidden // width,),
        in_specs=[
            whole((rows, width)),
            whole((rows, width)),
            whole(wp.shape),
            pl.BlockSpec((width, width), lambda s: (0, s)),
            pl.BlockSpec((1, width), lambda s: (0, s)),
            pl.BlockSpec((width, width), lambda s: (s, 0)),
            whole(p768.shape),
        ],
        out_specs=[
            whole((rows, width)),
            pl.BlockSpec((rows, width), lambda s: (0, s)),
            pl.BlockSpec((rows, width), lambda s: (0, s)),
            whole((rows, width)),
        ],
        scratch=[pltpu.VMEM((rows, width), BF), pltpu.VMEM((rows, width), F32)],
        flops=11e9,
        name="mlp",
    )(tokens, attended, wp, w1, b1, w2, p768)


def pool_matrix(a, b, rows, cols):
    count = rows * cols // 4
    out_at = lax.broadcasted_iota(jnp.int32, (count, rows * cols), 0)
    in_at = lax.broadcasted_iota(jnp.int32, (count, rows * cols), 1)
    half = cols // 2
    source = (2 * lax.div(out_at, half) + a) * cols + 2 * lax.rem(out_at, half) + b
    return jnp.where(in_at == source, 1.0, 0.0).astype(BF)


def lateral_norm(product, gain, shift, write):
    for at in range(0, product.shape[0], 64):
        hat, _ = stats(product[at : at + 64])
        write(at, (hat * gain + shift).astype(BF))


def pyramid_kernel(
    lr, cols, y_ref, ff_ref, fs_ref, mu_ref, lf_ref, lm_ref, lc0_ref, lc1_ref, p384_ref, fsb_ref, p256_ref,
    zf_ref, zm_ref, zb_ref, zc_ref, plane_ref, mplane_ref, f2_ref,
):
    tokens = lr * cols
    y = y_ref[...]
    half = mu_ref.shape[1] // 2
    quart = fs_ref.shape[0] // 4

    for b in (0, 1):
        first = mm(y, ff_ref[:, half * b : half * b + half])
        for at in range(0, tokens, 64):
            sl = slice(at, at + 64)
            hat, _ = stats(first[sl] + p384_ref[0:1, :])
            value = hat * p384_ref[1:2, :] + p384_ref[2:3, :]
            f2_ref[sl, :] = (0.5 * value * (1.0 + lax.erf(value * SQRT_HALF))).astype(BF)

        for c in (0, 1):
            for d in (0, 1):
                at_row = (2 * c + d) * quart
                third = (mt(f2_ref[...], fs_ref[at_row : at_row + quart, :]) + fsb_ref[...]).astype(BF)
                product = mm(third, lf_ref[...])

                def write(at, values):
                    plane_ref[c, 2 * b + d, at : at + 64, :] = values

                lateral_norm(product, p256_ref[0:1, :], p256_ref[8:9, :], write)

        middle = (mm(y, mu_ref[:, half * b : half * b + half]) + p384_ref[3:4, :]).astype(BF)
        product = mm(middle, lm_ref[...])

        def write_middle(at, values):
            mplane_ref[b, at : at + 64, :] = values

        lateral_norm(product, p256_ref[1:2, :], p256_ref[9:10, :], write_middle)

    weave4 = weave_matrix(4 * cols, 4)
    weave2 = weave_matrix(2 * cols, 2)
    for i in range(lr):
        sl = slice(i * cols, (i + 1) * cols)
        for c in (0, 1):
            planes = jnp.concatenate([plane_ref[c, k, sl, :] for k in range(4)], axis=0)
            zf_ref[i, c] = mm(weave4, planes).astype(BF)
        planes = jnp.concatenate([mplane_ref[k, sl, :] for k in range(2)], axis=0)
        zm_ref[i, 0] = mm(weave2, planes).astype(BF)

    @pl.when(pl.program_id(0) == 0)
    def _():
        product = mm(y, lc0_ref[...])

        def write_base(at, values):
            zb_ref[at : at + 64, :] = values

        lateral_norm(product, p256_ref[2:3, :], p256_ref[10:11, :], write_base)
        pooled = mm(pool_matrix(0, 0, lr, cols), y)
        for a, b in ((0, 1), (1, 0), (1, 1)):
            pooled = jnp.maximum(pooled, mm(pool_matrix(a, b, lr, cols), y))
        product = mm(pooled.astype(BF), lc1_ref[...])

        def write_coarse(at, values):
            zc_ref[at : at + 64, :] = values

        lateral_norm(product, p256_ref[3:4, :], p256_ref[11:12, :], write_coarse)


def pyramid_call(y, lr, cols, ff, fs, mu, lf, lm, lc0, lc1, p384, fsb, p256):
    tokens, width = y.shape
    outs = lf.shape[1]
    half2 = ff.shape[1] // 2
    return call(
        functools.partial(pyramid_kernel, lr, cols),
        [
            sds((lr, 4, 4 * cols, outs), BF),
            sds((lr, 2, 2 * cols, outs), BF),
            sds((tokens, outs), BF),
            sds((tokens // 4, outs), BF),
        ],
        grid=(2,),
        in_specs=[
            whole(y.shape),
            pl.BlockSpec((width, half2), lambda a: (0, a)),
            whole(fs.shape),
            pl.BlockSpec((width, half2), lambda a: (0, a)),
            whole(lf.shape),
            whole(lm.shape),
            whole(lc0.shape),
            whole(lc1.shape),
            whole(p384.shape),
            whole(fsb.shape),
            whole(p256.shape),
        ],
        out_specs=[
            pl.BlockSpec((lr, 2, 4 * cols, outs), lambda a: (0, a, 0, 0)),
            pl.BlockSpec((lr, 1, 2 * cols, outs), lambda a: (0, a, 0, 0)),
            whole((tokens, outs)),
            whole((tokens // 4, outs)),
        ],
        scratch=[
            pltpu.VMEM((2, 4, tokens, outs), BF),
            pltpu.VMEM((2, tokens, outs), BF),
            pltpu.VMEM((tokens, half2 // 2), BF),
        ],
        flops=8e9,
        name="pyramid",
    )(y, ff, fs, mu, lf, lm, lc0, lc1, p384, fsb, p256)


def fill_padded(step, block, rows, src_ref, rim_ref, pad_ref, left, right):
    def put(at, row):
        pad_ref[at] = jnp.concatenate(
            [mm(left, row).astype(BF), row, mm(right, row).astype(BF)], axis=1
        )

    @pl.when(step == 0)
    def _():
        put(0, rim_ref[0])
        put(1, src_ref[0])

    def body(k, carry):
        at = step * block + k
        put(at + 2, src_ref[at + 1])
        return carry

    lax.fori_loop(0, block - 1, body, 0)

    @pl.when(step == rows // block - 1)
    def _():
        put(rows + 1, rim_ref[1])

    @pl.when(step < rows // block - 1)
    def _():
        at = step * block + block - 1
        put(at + 2, src_ref[at + 1])


def conv_kernel(
    level, block, shards, z_ref, rim_ref, w_ref, cot_ref, p_ref, *refs
):
    map_ref, dr_ref, dw_ref, sums_ref, pad_ref, dwt_ref, acc_ref, pack_ref = refs[-8:]
    step = pl.program_id(0)
    rows, cols, chan = z_ref.shape
    pixels = block * cols
    fill_padded(
        step, block, rows, z_ref, rim_ref, pad_ref, shift_matrix(cols, -1), shift_matrix(cols, 1)
    )
    windows = [
        pad_ref[pl.ds(step * block + a, block)].reshape(pixels, 3 * chan) for a in range(3)
    ]
    result = mm(windows[0], w_ref[0, 0])
    for a in (1, 2):
        result = result + mm(windows[a], w_ref[0, a])
    acc_ref[...] = result.reshape(block, cols, chan)
    gain = p_ref[4 + level : 5 + level, :]
    shift = p_ref[12 + level : 13 + level, :]
    part = min(cols, 64)
    per_row = cols // part

    def body(k, carry):
        sum_gain, sum_shift = carry
        for q in range(per_row):
            at = slice(q * part, (q + 1) * part)
            hat, inverse = stats(acc_ref[k, at, :])
            map_ref[k, at, :] = (hat * gain + shift).astype(BF)
            cot = cot_ref[k, at, :].astype(F32)
            sum_gain = sum_gain + rowsum(cot * hat)
            sum_shift = sum_shift + rowsum(cot)
            dr_ref[k, at, :] = norm_back(cot * gain, hat, inverse).astype(BF)
        return sum_gain, sum_shift

    zero = jnp.zeros((1, chan), F32)
    sum_gain, sum_shift = lax.fori_loop(0, block, body, (zero, zero))

    @pl.when(step == 0)
    def _():
        sums_ref[...] = jnp.zeros_like(sums_ref)
        dwt_ref[...] = jnp.zeros_like(dwt_ref)

    sums_ref[0:1, :] += sum_gain
    sums_ref[1:2, :] += sum_shift
    grad_t = dr_ref[...].reshape(pixels, chan).T
    for a in range(3):
        dwt_ref[a] += mm(grad_t, windows[a])

    @pl.when(step == pl.num_programs(0) - 1)
    def _():
        unit = chan * 3 // shards
        for a in range(3):
            grad = dwt_ref[a].T
            for m in range(shards):
                piece = a * shards + m
                to = piece // 3
                lane = chan * (piece % 3)
                pack_ref[to * unit : to * unit + unit, lane : lane + chan] = grad[
                    m * unit : m * unit + unit
                ]
        dw_ref[...] = pack_ref[...].astype(BF)


def conv_call(level, z, rims, weights, cot, p256, block, shards, packed):
    rows, cols, chan = z.shape
    before = [] if packed is None else [packed]
    spec = pl.BlockSpec((block, cols, chan), lambda s: (s, 0, 0))
    return call(
        functools.partial(conv_kernel, level, block, shards),
        [
            sds((rows, cols, chan), BF),
            sds((rows, cols, chan), BF),
            sds((3 * chan, 4 * 3 * chan), BF),
            sds((8, chan), F32),
        ],
        grid=(rows // block,),
        in_specs=[
            whole(z.shape),
            whole(rims.shape),
            pl.BlockSpec((1, 3, 3 * chan, chan), lambda s: (level, 0, 0, 0)),
            spec,
            whole(p256.shape),
        ]
        + [pl.BlockSpec(memory_space=pl.ANY)] * len(before),
        out_specs=[
            spec,
            spec,
            pl.BlockSpec((3 * chan, 3 * chan), lambda s: (0, level)),
            whole((8, chan)),
        ],
        scratch=[
            pltpu.VMEM((rows + 2, cols, 3 * chan), BF),
            pltpu.VMEM((3, chan, 3 * chan), F32),
            pltpu.VMEM((block, cols, chan), F32),
            pltpu.VMEM((3 * chan, 3 * chan), F32),
        ],
        flops=4 * 9 * rows * cols * chan * chan,
        name=f"conv{level}",
        aliases={5: 2} if before else {},
    )(z, rims, weights, cot, p256, *before)


def conv_back_kernel(ways, block, dr_ref, rim_ref, w_ref, dz_ref, pad_ref):
    step = pl.program_id(0)
    rows, cols, chan = dr_ref.shape
    pixels = block * cols
    fill_padded(
        step, block, rows, dr_ref, rim_ref, pad_ref, shift_matrix(cols, 1), shift_matrix(cols, -1)
    )
    result = None
    for a in range(3):
        window = pad_ref[pl.ds(step * block + 2 - a, block)].reshape(pixels, 3 * chan)
        for b in range(3):
            part = mt(
                window[:, b * chan : (b + 1) * chan], w_ref[0, a, b * chan : (b + 1) * chan, :]
            )
            result = part if result is None else result + part
    low = result.astype(BF)
    if ways == 1:
        dz_ref[...] = low.reshape(dz_ref.shape)
        return
    unweave = weave_matrix(cols, ways, inverse=True)
    base = cols // ways
    for k in range(block):
        planes = mm(unweave, low[k * cols : (k + 1) * cols]).astype(BF)
        token_row, offset = k // ways, k % ways
        for w in range(ways):
            dz_ref[offset, w, token_row * base : (token_row + 1) * base, :] = planes[
                w * base : (w + 1) * base
            ]


def conv_back_call(level, dr, rims, weights, ways, block):
    rows, cols, chan = dr.shape
    if ways == 1:
        out = sds((rows * cols, chan), BF)
        spec = pl.BlockSpec((block * cols, chan), lambda s: (s, 0))
    else:
        tokens = rows * cols // (ways * ways)
        out = sds((ways, ways, tokens, chan), BF)
        spec = pl.BlockSpec(
            (ways, ways, block * cols // (ways * ways), chan), lambda s: (0, 0, s, 0)
        )
    return call(
        functools.partial(conv_back_kernel, ways, block),
        out,
        grid=(rows // block,),
        in_specs=[
            whole(dr.shape),
            whole(rims.shape),
            pl.BlockSpec((1, 3, 3 * chan, chan), lambda s: (level, 0, 0, 0)),
        ],
        out_specs=spec,
        scratch=[pltpu.VMEM((rows + 2, cols, 3 * chan), BF)],
        flops=2 * 9 * rows * cols * chan * chan,
        name=f"conv_back{level}",
    )(dr, rims, weights)


def lateral_back(product, read, gain, dl_ref):
    chan = product.shape[1]
    sum_gain = jnp.zeros((1, chan), F32)
    sum_shift = jnp.zeros((1, chan), F32)
    for at in range(0, product.shape[0], 64):
        hat, inverse = stats(product[at : at + 64])
        grad = read(at)
        sum_gain = sum_gain + rowsum(grad * hat)
        sum_shift = sum_shift + rowsum(grad)
        dl_ref[at : at + 64, :] = norm_back(grad * gain, hat, inverse).astype(BF)
    return sum_gain, sum_shift


def pyramid_back_kernel(
    lr, cols, y_ref, ff_ref, fs_ref, mu_ref, lf_ref, lm_ref, lc0_ref, lc1_ref, p384_ref, fsb_ref, p256_ref,
    dzf_ref, dzm_ref, dzb_ref, dzc_ref, place_ref,
    dy_ref, pack_ref, s384_ref, s192_ref, s256_ref,
    yt_ref, hat_ref, slope_ref, inv_ref, f2_ref, df2_ref, df1_ref, dl_ref, fs_acc, lf_acc, lm_acc,
    dcol_ref, drest_ref, sem,
):
    step = pl.program_id(0)
    tokens = lr * cols
    half = ff_ref.shape[1]
    chan = lf_ref.shape[1]

    def col_copy(at, which):
        return pltpu.make_async_copy(
            dcol_ref.at[which, at],
            pack_ref.at[:, pl.ds((4 * which + at) * half, half)],
            sem.at[4 * which + at],
        )

    rest = drest_ref.shape[1]
    rest_copy = pltpu.make_async_copy(drest_ref, pack_ref.at[:, pl.ds(8 * half, rest)], sem.at[8])
    quart = fs_ref.shape[0] // 4

    @pl.when(step == 0)
    def _():
        yt_ref[...] = y_ref[...].T
        for ref in (fs_acc, lf_acc, lm_acc, s384_ref, s192_ref, s256_ref):
            ref[...] = jnp.zeros_like(ref)
        product = mm(y_ref[...], lc0_ref[...])
        sg, ss = lateral_back(
            product, lambda at: dzb_ref[at : at + 64, :].astype(F32), p256_ref[2:3, :], dl_ref
        )
        s256_ref[2:3, :] = sg
        s256_ref[10:11, :] = ss
        drest_ref[:, half : half + chan] = mm(yt_ref[...], dl_ref[...]).astype(BF)
        dy_ref[...] = mt(dl_ref[...], lc0_ref[...])
        picks = [mm(pool_matrix(a, b, lr, cols), y_ref[...]) for a in (0, 1) for b in (0, 1)]
        top = jnp.maximum(jnp.maximum(picks[0], picks[1]), jnp.maximum(picks[2], picks[3]))
        low = top.astype(BF)
        product = mm(low, lc1_ref[...])
        sg, ss = lateral_back(
            product, lambda at: dzc_ref[at : at + 64, :].astype(F32), p256_ref[3:4, :], dl_ref
        )
        s256_ref[3:4, :] = sg
        s256_ref[11:12, :] = ss
        grad = dl_ref[0 : tokens // 4, :]
        drest_ref[:, half + chan : half + 2 * chan] = tm(low, grad).astype(BF)
        dtop = mt(grad, lc1_ref[...])
        hits = [jnp.where(pick == top, 1.0, 0.0) for pick in picks]
        dtop = dtop / (hits[0] + hits[1] + hits[2] + hits[3])
        for index, hit in enumerate(hits):
            share = dtop * hit
            upper = share.astype(BF)
            lower = (share - upper.astype(F32)).astype(BF)
            spread = pool_matrix(index // 2, index % 2, lr, cols)
            dy_ref[...] += tm(spread, upper) + tm(spread, lower)

    first = mm(y_ref[...], ff_ref[...])
    for at in range(0, tokens, 64):
        sl = slice(at, at + 64)
        hat, inverse = stats(first[sl] + p384_ref[0:1, :])
        hat_ref[sl, :] = hat
        inv_ref[sl, :] = jnp.broadcast_to(inverse, (64, 128))
        value, slope = gelu_pair(hat * p384_ref[1:2, :] + p384_ref[2:3, :])
        f2_ref[sl, :] = value.astype(BF)
        slope_ref[sl, :] = slope
    for c in (0, 1):
        for d in (0, 1):
            at_row = (2 * c + d) * quart
            weight = fs_ref[at_row : at_row + quart, :]
            third = (mt(f2_ref[...], weight) + fsb_ref[...]).astype(BF)
            product = mm(third, lf_ref[...])
            sg, ss = lateral_back(
                product,
                lambda at: dzf_ref[0, c, 0, d, at : at + 64, :].astype(F32),
                p256_ref[0:1, :],
                dl_ref,
            )
            s256_ref[0:1, :] += sg
            s256_ref[8:9, :] += ss
            lf_acc[...] += tm(third, dl_ref[...])
            dthird = mt(dl_ref[...], lf_ref[...]).astype(BF)
            s192_ref[0:1, :] += rowsum(dthird.astype(F32))
            fs_acc[at_row : at_row + quart, :] += tm(dthird, f2_ref[...])
            part = mm(dthird, weight)
            if c + d == 0:
                df2_ref[...] = part
            else:
                df2_ref[...] += part
    zero = jnp.zeros((1, df2_ref.shape[1]), F32)
    sum_gain, sum_shift, sum_bias = zero, zero, zero
    for at in range(0, tokens, 64):
        sl = slice(at, at + 64)
        hat = hat_ref[sl, :]
        grad = df2_ref[sl, :] * slope_ref[sl, :]
        sum_gain = sum_gain + rowsum(grad * hat)
        sum_shift = sum_shift + rowsum(grad)
        low = norm_back(grad * p384_ref[1:2, :], hat, inv_ref[sl, 0:1]).astype(BF)
        sum_bias = sum_bias + rowsum(low.astype(F32))
        df1_ref[sl, :] = low
    s384_ref[0:1, :] += sum_bias
    s384_ref[1:2, :] += sum_gain
    s384_ref[2:3, :] += sum_shift
    dcol_ref[0, step] = mm(yt_ref[...], df1_ref[...]).astype(BF)
    col_copy(step, 0).start()
    dy_ref[...] += mt(df1_ref[...], ff_ref[...])

    middle = (mm(y_ref[...], mu_ref[...]) + p384_ref[3:4, :]).astype(BF)
    product = mm(middle, lm_ref[...])
    sg, ss = lateral_back(
        product,
        lambda at: dzm_ref[0, 0, at : at + 64, :].astype(F32),
        p256_ref[1:2, :],
        dl_ref,
    )
    s256_ref[1:2, :] += sg
    s256_ref[9:10, :] += ss
    lm_acc[...] += tm(middle, dl_ref[...])
    dmiddle = mt(dl_ref[...], lm_ref[...]).astype(BF)
    s384_ref[3:4, :] += rowsum(dmiddle.astype(F32))
    dcol_ref[1, step] = mm(yt_ref[...], dmiddle).astype(BF)
    col_copy(step, 1).start()
    dy_ref[...] += mt(dmiddle, mu_ref[...])

    @pl.when(step == pl.num_programs(0) - 1)
    def _():
        drest_ref[:, 0:half] = fs_acc[...].astype(BF)
        laterals = jnp.concatenate([lf_acc[...], lm_acc[...]], axis=0).astype(BF)
        drest_ref[:, half + 2 * chan : half + 3 * chan] = mm(place_ref[...], laterals).astype(BF)
        rest_copy.start()
        for which in (0, 1):
            for at in range(4):
                col_copy(at, which).wait()
        rest_copy.wait()


def pyramid_back_call(
    y, lr, cols, ff, fs, mu, lf, lm, lc0, lc1, p384, fsb, p256, dzf, dzm, dzb, dzc, place, lanes
):
    tokens, width = y.shape
    half = fs.shape[1]
    quart = fsb.shape[1]
    outs = lf.shape[1]
    col_block = pl.BlockSpec((width, half), lambda s: (0, s))
    return call(
        functools.partial(pyramid_back_kernel, lr, cols),
        [
            sds((tokens, width), F32),
            sds((width, lanes), BF),
            sds((8, half), F32),
            sds((8, quart), F32),
            sds((16, outs), F32),
        ],
        grid=(4,),
        in_specs=[
            whole(y.shape),
            col_block,
            whole(fs.shape),
            col_block,
            whole(lf.shape),
            whole(lm.shape),
            whole(lc0.shape),
            whole(lc1.shape),
            whole(p384.shape),
            whole(fsb.shape),
            whole(p256.shape),
            pl.BlockSpec((1, 2, 1, 2, tokens, outs), lambda s: (s // 2, 0, s % 2, 0, 0, 0)),
            pl.BlockSpec((1, 1, tokens, outs), lambda s: (s // 2, s % 2, 0, 0)),
            whole(dzb.shape),
            whole(dzc.shape),
            whole(place.shape),
        ],
        out_specs=[
            whole((tokens, width)),
            pl.BlockSpec(memory_space=pl.ANY),
            whole((8, half)),
            whole((8, quart)),
            whole((16, outs)),
        ],
        scratch=[
            pltpu.VMEM((width, tokens), BF),
            pltpu.VMEM((tokens, half), F32),
            pltpu.VMEM((tokens, half), F32),
            pltpu.VMEM((tokens, 128), F32),
            pltpu.VMEM((tokens, half), BF),
            pltpu.VMEM((tokens, half), F32),
            pltpu.VMEM((tokens, half), BF),
            pltpu.VMEM((tokens, outs), BF),
            pltpu.VMEM(fs.shape, F32),
            pltpu.VMEM(lf.shape, F32),
            pltpu.VMEM(lm.shape, F32),
            pltpu.VMEM((2, 4, width, half), BF),
            pltpu.VMEM((width, half + 3 * outs), BF),
            pltpu.SemaphoreType.DMA((9,)),
        ],
        flops=20e9,
        name="pyramid_back",
    )(
        y, ff, fs, mu, lf, lm, lc0, lc1, p384, fsb, p256,
        dzf.reshape(2, 2, 2, 2, tokens, outs), dzm, dzb, dzc, place,
    )


def mlp_back_kernel(
    shards, offset,
    dy_ref, g_ref, gp_ref, w1_ref, w2_ref, x1_ref, o_ref, wp_ref, p_ref, s384_ref, s192_ref, s256_ref, levels_ref,
    hot256_ref, hot384_ref, hot192_ref, old_ref,
    pack_ref, dx1_ref, do_ref,
    n2t_ref, d2_ref, dn2_ref, low_ref, sums_ref, vec_ref, dw1_ref, dw2f_ref, dw2_ref, dwp_ref, vlow_ref, sem,
):
    step = pl.program_id(0)
    steps = pl.num_programs(0)
    tokens, width = dy_ref.shape
    unit = width // shards
    hidden = 4 * width

    def w1_copy(at):
        return pltpu.make_async_copy(
            dw1_ref.at[at], pack_ref.at[:, pl.ds(offset + at * width, width)], sem.at[at]
        )

    def w2_copy(at):
        rows = width // 4
        return pltpu.make_async_copy(
            dw2_ref.at[at],
            pack_ref.at[pl.ds(at * rows, rows), pl.ds(offset + hidden, hidden)],
            sem.at[4 + at],
        )

    wp_copy = pltpu.make_async_copy(
        dwp_ref, pack_ref.at[:, pl.ds(offset + 2 * hidden, width)], sem.at[8]
    )
    vec_copy = pltpu.make_async_copy(
        vlow_ref, pack_ref.at[:, pl.ds(offset + 2 * hidden + width, 128)], sem.at[9]
    )

    @pl.when(step == 0)
    def _():
        sums_ref[...] = jnp.zeros_like(sums_ref)
        vec_ref[...] = jnp.zeros_like(vec_ref)
        total = jnp.zeros((1, width), F32)
        for at in range(0, tokens, 32):
            sl = slice(at, at + 32)
            hat, _ = stats(x1_ref[sl, :])
            low_ref[sl, :] = (hat * p_ref[1:2, :] + p_ref[3:4, :]).astype(BF)
            low = dy_ref[sl, :].astype(BF)
            d2_ref[sl, :] = low
            total = total + rowsum(low.astype(F32))
        sums_ref[7:8, :] = total
        n2t_ref[...] = low_ref[...].T

    dw2 = tm(g_ref[...], d2_ref[...])
    dg = mt(d2_ref[...], w2_ref[...])
    for at in range(0, tokens, 32):
        sl = slice(at, at + 32)
        low_ref[sl, :] = (dg[sl] * gp_ref[sl, :].astype(F32)).astype(BF)
    db1 = tm(low_ref[...], jnp.ones((tokens, 128), BF))
    lane = lax.broadcasted_iota(jnp.int32, (unit, 128), 1)
    rows4 = width // 4
    for q in range(shards // 4):
        entry = jnp.zeros((unit, 128), F32)
        for k in range(4):
            sl = slice((4 * q + k) * unit, (4 * q + k + 1) * unit)
            dw2f_ref[q * unit : q * unit + unit, k * width : (k + 1) * width] = dw2[sl]
            entry = jnp.where(lane == 40 + k, db1[sl], entry)
        vec_ref[pl.ds(pl.multiple_of(step * rows4 + q * unit, 8), unit), :] += entry
    dw2_ref[step] = dw2f_ref[...].astype(BF)
    w2_copy(step).start()
    dw1_ref[step] = mm(n2t_ref[...], low_ref[...]).astype(BF)
    w1_copy(step).start()
    part = mt(low_ref[...], w1_ref[...])

    @pl.when(step == 0)
    def _():
        dn2_ref[...] = part

    @pl.when(step > 0)
    def _():
        dn2_ref[...] += part

    @pl.when(step == steps - 1)
    def _():
        zero = jnp.zeros((1, width), F32)
        sum_gain, sum_shift, sum_bias = zero, zero, zero
        for at in range(0, tokens, 32):
            sl = slice(at, at + 32)
            hat, inverse = stats(x1_ref[sl, :])
            grad = dn2_ref[sl, :]
            sum_gain = sum_gain + rowsum(grad * hat)
            sum_shift = sum_shift + rowsum(grad)
            dx1 = dy_ref[sl, :] + norm_back(grad * p_ref[1:2, :], hat, inverse)
            dx1_ref[sl, :] = dx1
            low = dx1.astype(BF)
            sum_bias = sum_bias + rowsum(low.astype(F32))
            d2_ref[sl, :] = low
        sums_ref[1:2, :] = sum_gain
        sums_ref[3:4, :] = sum_shift
        sums_ref[6:7, :] = sum_bias
        dwp_ref[...] = tm(o_ref[...], d2_ref[...]).astype(BF)
        wp_copy.start()
        do_ref[...] = mt(d2_ref[...], wp_ref[...]).astype(BF)

        def lanes_of(rows, before):
            after = 128 - before - rows.shape[0]
            parts = [jnp.zeros((before, rows.shape[1]), F32)] if before else []
            parts += [rows, jnp.zeros((after, rows.shape[1]), F32)]
            return jnp.concatenate(parts, axis=0)

        spread = mt(hot256_ref[...], lanes_of(s256_ref[...], 8).astype(BF))
        spread = spread + mt(hot256_ref[...], lanes_of(levels_ref[...], 24).astype(BF))
        spread = spread + mt(hot384_ref[...], lanes_of(s384_ref[...], 32).astype(BF))
        spread = spread + mt(hot192_ref[...], lanes_of(s192_ref[...], 48).astype(BF))
        spread = spread + lanes_of(sums_ref[...], 0).T
        vlow_ref[...] = (vec_ref[...] + spread).astype(BF)
        vec_copy.start()
        for at in range(4):
            w1_copy(at).wait()
            w2_copy(at).wait()
        wp_copy.wait()
        vec_copy.wait()


def mlp_back_call(
    dy, g, gp, w1, w2, x1, attended, wp, p768, s384, s192, s256, levels, hots, packed, offset, shards
):
    rows, width = dy.shape
    hidden = g.shape[1]
    full = whole((rows, width))
    column = pl.BlockSpec((rows, width), lambda s: (0, s))
    smalls = [p768, s384, s192, s256, levels, *hots]
    return call(
        functools.partial(mlp_back_kernel, shards, offset),
        [
            sds(packed.shape, BF),
            sds((rows, width), F32),
            sds((rows, width), BF),
        ],
        grid=(hidden // width,),
        in_specs=[
            full,
            column,
            column,
            pl.BlockSpec((width, width), lambda s: (0, s)),
            pl.BlockSpec((width, width), lambda s: (s, 0)),
            full,
            full,
            whole((width, width)),
        ]
        + [whole(a.shape) for a in smalls]
        + [pl.BlockSpec(memory_space=pl.ANY)],
        out_specs=[pl.BlockSpec(memory_space=pl.ANY), full, full],
        scratch=[
            pltpu.VMEM((width, rows), BF),
            pltpu.VMEM((rows, width), BF),
            pltpu.VMEM((rows, width), F32),
            pltpu.VMEM((rows, width), BF),
            pltpu.VMEM((8, width), F32),
            pltpu.VMEM((width, 128), F32),
            pltpu.VMEM((4, width, width), BF),
            pltpu.VMEM((width // 4, hidden), F32),
            pltpu.VMEM((4, width // 4, hidden), BF),
            pltpu.VMEM((width, width), BF),
            pltpu.VMEM((width, 128), BF),
            pltpu.SemaphoreType.DMA((10,)),
        ],
        flops=22e9,
        name="mlp_back",
        aliases={16: 0},
    )(dy, g, gp, w1, w2, x1, attended, wp, *smalls, packed)


def roll_back(values, amount):
    moved = jnp.concatenate(
        [
            pltpu.roll(values[8 * g : 8 * g + 8], (amount - 7 - 8 * g) % 128, 1)
            for g in range(values.shape[0] // 8)
        ],
        axis=0,
    )
    left = 7 - lax.rem(lax.broadcasted_iota(jnp.int32, values.shape, 0), 8)
    for step in (1, 2, 4):
        moved = jnp.where((left & step) > 0, pltpu.roll(moved, step, 1), moved)
    return moved


def attend_back_kernel(total_rows, scale, others, *refs):
    first_ref, q_ref, qaug_ref, do_ref, o_ref, lse_ref, tab_ref, oh1_ref, oh2_ref = refs[:9]
    k_refs = refs[9 : 9 + others]
    v_refs = refs[9 + others : 9 + 2 * others]
    rest = refs[9 + 2 * others :]
    dq_ref, dtab_ref = rest[:2]
    dk_refs = rest[2 : 2 + others]
    dv_refs = rest[2 + others : 2 + 2 * others]
    kaug_ref, v_ref, p_ref, ds_ref, dqt_ref, df_ref = rest[2 + 2 * others :]
    first_row = first_ref[0]
    tokens = q_ref.shape[0]
    keys = kaug_ref.shape[0]

    @pl.when(pl.program_id(0) == 0)
    def _():
        kaug_ref[:, 128:] = oh2_ref[...]
        dtab_ref[...] = jnp.zeros_like(dtab_ref)

    at = 0
    for ref in v_refs:
        v_ref[at : at + ref.shape[0], :] = ref[...]
        at += ref.shape[0]
    lane_all = lax.broadcasted_iota(jnp.int32, (tokens, 128), 1)
    lane = lax.broadcasted_iota(jnp.int32, (64, 128), 1)
    qf = q_ref[...].astype(F32)
    dof = do_ref[...].astype(F32)
    delta_t = (dof * o_ref[...].astype(F32)).T
    dk = None
    dv = None
    dq = None
    for odd in (0, 1):
        mine_all = (lane_all >= 64) if odd else (lane_all < 64)
        other = (lane < 64) if odd else (lane >= 64)
        build_kaug(kaug_ref, k_refs, oh1_ref, oh2_ref, odd)
        qm = jnp.where(mine_all, qf, 0.0).astype(BF)
        dom = jnp.where(mine_all, dof, 0.0).astype(BF)
        delta = rowsum(delta_t[64 * odd : 64 * odd + 64])
        for t in range(0, tokens, 256):
            sl = slice(t, t + 256)
            scores = mt(kaug_ref[...], qaug_ref[odd, sl, :])
            dweight = mt(v_ref[...], dom[sl])
            lse = lse_ref[0, odd : odd + 1, sl]
            for c in range(0, keys, 128):
                weight = jnp.exp(scores[c : c + 128] - lse)
                p_ref[c : c + 128, :] = weight.astype(BF)
                ds_ref[c : c + 128, :] = (weight * (dweight[c : c + 128] - delta[:, sl])).astype(BF)
            dk_part = mm(ds_ref[...], qm[sl])
            dv_part = mm(p_ref[...], dom[sl])
            dk = dk_part if dk is None else dk + dk_part
            dv = dv_part if dv is None else dv + dv_part
            dqt_ref[:, sl] = tm(kaug_ref[...], ds_ref[...])
        dqa = dqt_ref[0:256, :].T
        for i in range(tokens // 64):
            sl = slice(64 * i, 64 * i + 64)
            cols = roll_back(jnp.where(other, dqa[sl, 0:128], 0.0), 63 if odd else 127)
            shift = lax.rem(63 + total_rows - (first_row + i) + 128, 128)
            rows = pltpu.roll(
                jnp.where((lane >= 64) & (lane < 64 + total_rows), dqa[sl, 128:256], 0.0), shift, 1
            )
            df_ref[sl, 0:128] = cols.astype(BF)
            df_ref[sl, 128:256] = rows.astype(BF)
        from_tables = mt(df_ref[...], tab_ref[...])
        part = jnp.where(mine_all, dqa[:, 0:128] * scale + from_tables, 0.0)
        dq = part if dq is None else dq + part
        dtab_ref[...] += tm(qm, df_ref[...])
    dq_ref[...] = dq.astype(BF)
    at = 0
    for dk_ref, dv_ref in zip(dk_refs, dv_refs):
        count = dk_ref.shape[0]
        dk_ref[...] = (dk[at : at + count] * scale).astype(BF)
        dv_ref[...] = dv[at : at + count].astype(BF)
        at += count


def attend_back_call(first, qkv_own, kv_others, qaug, dout, attended, lse, tab, oh1, oh2, total_rows, heads):
    tokens = qkv_own.shape[0]
    width = qkv_own.shape[1] // 3
    keys = oh1.shape[0]
    aug = 128 + oh2.shape[1]
    pairs = width // 128
    parts = 1 + (1 if kv_others is not None else 0)
    own = pl.BlockSpec((tokens, 128), lambda h: (0, h))
    far = pl.BlockSpec((max(keys - tokens, 16), 128), lambda h: (0, h))
    in_specs = [
        pl.BlockSpec(memory_space=pltpu.SMEM),
        own,
        pl.BlockSpec((2, tokens, aug), lambda h: (h, 0, 0)),
        own,
        own,
        pl.BlockSpec((1, 2, tokens), lambda h: (h, 0, 0)),
        whole(tab.shape),
        whole(oh1.shape),
        whole(oh2.shape),
    ]
    k_args, v_args, k_specs, v_specs = [qkv_own], [qkv_own], [], []
    k_specs.append(pl.BlockSpec((tokens, 128), lambda h: (0, h + pairs)))
    v_specs.append(pl.BlockSpec((tokens, 128), lambda h: (0, h + 2 * pairs)))
    g_shapes, g_specs = [sds((tokens, width), BF)], [own]
    if kv_others is not None:
        k_args.append(kv_others)
        v_args.append(kv_others)
        k_specs.append(far)
        v_specs.append(pl.BlockSpec((keys - tokens, 128), lambda h: (0, h + pairs)))
        g_shapes.append(sds((keys - tokens, width), BF))
        g_specs.append(far)
    scale = (width // heads) ** -0.5
    return call(
        functools.partial(attend_back_kernel, total_rows, scale, parts),
        [sds((tokens, width), BF), sds((128, 256), F32)] + g_shapes + g_shapes,
        grid=(pairs,),
        in_specs=in_specs + k_specs + v_specs,
        out_specs=[own, whole((128, 256))] + g_specs + g_specs,
        scratch=[
            pltpu.VMEM((keys, aug), BF),
            pltpu.VMEM((keys, 128), BF),
            pltpu.VMEM((keys, 256), BF),
            pltpu.VMEM((keys, 256), BF),
            pltpu.VMEM((aug, tokens), F32),
            pltpu.VMEM((tokens, 256), BF),
        ],
        flops=30e9,
        name="attend_back",
    )(first, qkv_own, qaug, dout, attended, lse, tab, oh1, oh2, *k_args, *v_args)


def qkv_back_kernel(
    x_ref, dq_ref, dk_ref, dv_ref, rk_ref, rv_ref, w_ref, dx1_ref, p_ref, dtab_ref, hot_ref,
    pack_ref, dx_ref, nt_ref, low_ref, dn_ref, sums_ref, dw_ref, extra_ref, sem,
):
    step = pl.program_id(0)
    tokens, width = x_ref.shape

    def w_copy(at):
        return pltpu.make_async_copy(
            dw_ref.at[at], pack_ref.at[:, pl.ds(at * width, width)], sem.at[at]
        )

    extra_copy = pltpu.make_async_copy(extra_ref, pack_ref.at[:, pl.ds(3 * width, 384)], sem.at[3])

    @pl.when(step == 0)
    def _():
        sums_ref[...] = jnp.zeros_like(sums_ref)
        for at in range(0, tokens, 32):
            sl = slice(at, at + 32)
            hat, _ = stats(x_ref[sl, :].astype(F32))
            low_ref[sl, :] = (hat * p_ref[0:1, :] + p_ref[2:3, :]).astype(BF)
        nt_ref[...] = low_ref[...].T
        low_ref[...] = dq_ref[...]
        sums_ref[4:5, :] = rowsum(dq_ref[...].astype(F32))
        both = dtab_ref[...]
        tables = (both[0:64] + both[64:128]).astype(BF)
        extra_ref[:, 128:384] = mm(hot_ref[...], tables).astype(BF)

    def gather(own_ref, recv_ref):
        total = own_ref[...].astype(F32)
        for d in range(recv_ref.shape[0]):
            total = total + recv_ref[d].astype(F32)
        low_ref[...] = total.astype(BF)

    @pl.when(step == 1)
    def _():
        gather(dk_ref, rk_ref)

    @pl.when(step == 2)
    def _():
        gather(dv_ref, rv_ref)
        sums_ref[5:6, :] = rowsum(low_ref[...].astype(F32))

    dw_ref[step] = mm(nt_ref[...], low_ref[...]).astype(BF)
    w_copy(step).start()
    part = mt(low_ref[...], w_ref[...])

    @pl.when(step == 0)
    def _():
        dn_ref[...] = part

    @pl.when(step > 0)
    def _():
        dn_ref[...] += part

    @pl.when(step == 2)
    def _():
        zero = jnp.zeros((1, width), F32)
        sum_gain, sum_shift = zero, zero
        for at in range(0, tokens, 32):
            sl = slice(at, at + 32)
            hat, inverse = stats(x_ref[sl, :].astype(F32))
            grad = dn_ref[sl, :]
            sum_gain = sum_gain + rowsum(grad * hat)
            sum_shift = sum_shift + rowsum(grad)
            dx_ref[sl, :] = dx1_ref[sl, :] + norm_back(grad * p_ref[0:1, :], hat, inverse)
        sums_ref[0:1, :] = sum_gain
        sums_ref[2:3, :] = sum_shift
        padded = jnp.concatenate([sums_ref[...], jnp.zeros((120, width), F32)], axis=0)
        extra_ref[:, 0:128] = padded.T.astype(BF)
        extra_copy.start()
        for at in range(3):
            w_copy(at).wait()
        extra_copy.wait()


def qkv_back_call(tokens, dq, dk, dv, recv_k, recv_v, weight, dx1, p768, dtab, hot):
    rows, width = tokens.shape
    full = whole((rows, width))
    return call(
        qkv_back_kernel,
        [sds((width, 3 * width + 384), BF), sds((rows, width), F32)],
        grid=(3,),
        in_specs=[
            full,
            full,
            full,
            full,
            whole(recv_k.shape),
            whole(recv_v.shape),
            pl.BlockSpec((width, width), lambda s: (0, s)),
            full,
            whole(p768.shape),
            whole(dtab.shape),
            whole(hot.shape),
        ],
        out_specs=[pl.BlockSpec(memory_space=pl.ANY), full],
        scratch=[
            pltpu.VMEM((width, rows), BF),
            pltpu.VMEM((rows, width), BF),
            pltpu.VMEM((rows, width), F32),
            pltpu.VMEM((8, width), F32),
            pltpu.VMEM((3, width, width), BF),
            pltpu.VMEM((width, 384), BF),
            pltpu.SemaphoreType.DMA((4,)),
        ],
        flops=4e9,
        name="qkv_back",
    )(tokens, dq, dk, dv, recv_k, recv_v, weight, dx1, p768, dtab, hot)


def rim_exchange(levels, axis):
    peers = lax.axis_size(axis)
    chan = levels[0].shape[-1]
    counts = [level.shape[1] for level in levels]
    lasts = jnp.concatenate([level[-1] for level in levels], axis=0)
    firsts = jnp.concatenate([level[0] for level in levels], axis=0)
    if peers == 2:
        me = lax.axis_index(axis)
        got = lax.ppermute(jnp.where(me == 0, lasts, firsts), axis, [(0, 1), (1, 0)])
        nothing = jnp.zeros_like(got)
        before = jnp.where(me == 1, got, nothing)
        after = jnp.where(me == 0, got, nothing)
    else:
        before = lax.ppermute(lasts, axis, [(i, i + 1) for i in range(peers - 1)])
        after = lax.ppermute(firsts, axis, [(i + 1, i) for i in range(peers - 1)])
    both = jnp.stack([before, after])
    rims, at = [], 0
    for count in counts:
        rims.append(both[:, at : at + count])
        at += count
    return rims


def seq_total(part):
    peers = lax.axis_size("seq")
    if peers == 2:
        other = lax.ppermute(part, "seq", [(0, 1), (1, 0)])
        return part.astype(F32) + other.astype(F32)
    return lax.psum(part, "seq").astype(F32)


def per_device(
    tokens, valid_rows, valid_cols, block_gains, block_shifts, qkv_weight, qv_bias, table_rows, table_cols,
    proj_weight, proj_bias, fc1_weight, fc1_bias, fc2_weight, fc2_bias, fine_first, fine_first_bias,
    fine_norm_gain, fine_norm_shift, fine_second, fine_second_bias, middle_up, middle_up_bias, lateral_fine,
    lateral_middle, lateral_coarse, level_gains, level_shifts, output_convs, cotan_fine, cotan_middle,
    cotan_base, cotan_coarse,
):
    lr, cols, width = tokens.shape[1:]
    head = table_rows.shape[0]
    heads = width // head
    peers = lax.axis_size("seq")
    shards = lax.axis_size("img")
    me = lax.axis_index("seq")
    total_rows = lr * peers
    count = lr * cols
    chan = lateral_fine.shape[1]
    first_row = me * lr
    first = first_row.astype(jnp.int32).reshape(1)
    flat = tokens[0].reshape(count, width)

    far = [
        lax.ppermute(flat, "seq", [(i, (i + d) % peers) for i in range(peers)])
        for d in range(1, peers)
    ]
    far_tokens = jnp.concatenate(far, axis=0) if len(far) > 1 else (far[0] if far else None)

    p768 = jnp.stack(
        [
            block_gains[:, 0], block_gains[:, 1], block_shifts[:, 0], block_shifts[:, 1],
            qv_bias[:, 0], qv_bias[:, 1], proj_bias, fc2_bias,
        ]
    ).astype(F32)
    bias3 = jnp.stack([qv_bias[:, 0], jnp.zeros_like(proj_bias), qv_bias[:, 1]]).astype(F32)[:, None, :]
    b1 = fc1_bias.astype(F32)[None]
    p384 = jnp.stack([fine_first_bias, fine_norm_gain, fine_norm_shift, middle_up_bias]).astype(F32)
    fsb = fine_second_bias.astype(F32)[None]
    p256 = jnp.concatenate([level_gains.T, level_shifts.T]).astype(F32)
    conv_weights = output_convs.transpose(1, 0, 2).reshape(4, 3, 3 * chan, chan)
    lc0, lc1 = lateral_coarse[:, 0, :], lateral_coarse[:, 1, :]

    def turned(table):
        back = table[:, ::-1]
        back = jnp.pad(back, ((0, 0), (0, 128 - back.shape[1])))
        return jnp.concatenate([back, back], axis=0)

    tw, tr = turned(table_cols), turned(table_rows)

    low_at, aug = aug_layout(total_rows)
    ranks = jnp.stack([(me - d) % peers for d in range(peers)])
    key_rows = (ranks[:, None] * lr + jnp.arange(lr)[None, :])[:, :, None]
    key_rows = jnp.broadcast_to(key_rows, (peers, lr, cols)).reshape(-1, 1)
    key_cols = jnp.broadcast_to(jnp.arange(cols)[None, None, :], (peers, lr, cols)).reshape(-1, 1)
    lane = jnp.arange(128)[None, :]
    oh1 = (lane % 64 == key_cols).astype(BF)
    lane = jnp.arange(aug - 128)[None, :]
    hot = (lane < 64) & (lane == key_cols)
    hot = hot | ((lane >= 64) & (lane < 64 + total_rows) & (lane - 64 == key_rows))
    off = low_at
    hot = hot | ((lane >= off) & (lane < off + total_rows) & (lane - off == key_rows))
    bad = (key_rows >= valid_rows[0]) | (key_cols >= valid_cols[0])
    oh2 = jnp.where(bad & (lane == off + total_rows), NEG, hot.astype(F32)).astype(BF)

    qkv_own = qkv_call(flat, qkv_weight, bias3, p768, 0)
    kv_far = qkv_call(far_tokens, qkv_weight, bias3, p768, 1) if far else None
    attended, qaug, lse = attend_call(
        first, qkv_own, kv_far, (tw, tr), oh1, oh2, total_rows, heads
    )
    x1, hidden, slope, y = mlp_call(flat, attended, proj_weight, fc1_weight, b1, fc2_weight, p768)

    zf, zm, zb, zc = pyramid_call(
        y, lr, cols, fine_first, fine_second, middle_up, lateral_fine, lateral_middle, lc0, lc1, p384, fsb, p256
    )
    levels = [
        zf.reshape(4 * lr, 4 * cols, chan),
        zm.reshape(2 * lr, 2 * cols, chan),
        zb.reshape(lr, cols, chan),
        zc.reshape(lr // 2, cols // 2, chan),
    ]
    rims = rim_exchange(levels, "seq")
    cots = [c[0] for c in (cotan_fine, cotan_middle, cotan_base, cotan_coarse)]
    maps, drs, level_sums = [None] * 4, [None] * 4, [None] * 4
    packed = None
    for level in (3, 2, 1, 0):
        z = levels[level]
        block = min(z.shape[0], max(1, 2048 // z.shape[1]))
        maps[level], drs[level], packed, level_sums[level] = conv_call(
            level, z, rims[level], conv_weights, cots[level], p256, block, shards, packed
        )

    conv_low = lax.psum_scatter(packed, "img", scatter_dimension=0, tiled=True)
    drims = rim_exchange(drs, "seq")
    dzs = []
    for level, ways in enumerate((4, 2, 1, 1)):
        dr = drs[level]
        block = min(dr.shape[0], max(1, 2048 // dr.shape[1]))
        dzs.append(conv_back_call(level, dr, drims[level], conv_weights, ways, block))

    unit = width // shards
    packed_row = jnp.arange(width)[:, None]
    shard_at, within = packed_row // unit, packed_row % unit

    def placed(size):
        own = size // shards
        at = jnp.arange(size)[None, :]
        return ((within < own) & (at == shard_at * own + within)).astype(BF)

    quart, half = lateral_fine.shape[0], lateral_middle.shape[0]
    own_q, own_h = quart // shards, half // shards
    at = jnp.arange(quart + half)[None, :]
    source = jnp.where(
        within < own_q,
        shard_at * own_q + within,
        jnp.where(within < own_q + own_h, quart + shard_at * own_h + within - own_q, -1),
    )
    place = (at == source).astype(BF)
    hots = (placed(chan), placed(half), placed(quart))
    offset = 9 * half + 3 * chan
    lanes = offset + 9 * width + 128
    dy, wide, s384, s192, s256 = pyramid_back_call(
        y, lr, cols, fine_first, fine_second, middle_up, lateral_fine, lateral_middle, lc0, lc1, p384, fsb, p256,
        *dzs, place, lanes,
    )

    level_rows = jnp.concatenate(
        [level_sums[k][0:1] for k in range(4)] + [level_sums[k][1:2] for k in range(4)]
    )
    wide, dx1, dout = mlp_back_call(
        dy, hidden, slope, fc1_weight, fc2_weight, x1, attended, proj_weight, p768,
        s384, s192, s256, level_rows, hots, wide, offset, shards,
    )
    wide_low = lax.psum_scatter(wide, "img", scatter_dimension=0, tiled=True)
    back = attend_back_call(
        first, qkv_own, kv_far, qaug, dout, attended, lse,
        jnp.concatenate([tw, tr], axis=1), oh1, oh2, total_rows, heads,
    )
    dq, dtab = back[:2]
    if far:
        dk, dk_far, dv, dv_far = back[2:]

        def send(parts):
            return jnp.stack(
                [
                    lax.ppermute(
                        parts[(d - 1) * count : d * count],
                        "seq",
                        [(i, (i - d) % peers) for i in range(peers)],
                    )
                    for d in range(1, peers)
                ]
            )

        recv_k, recv_v = send(dk_far), send(dv_far)
    else:
        dk, dv = back[2:]
        recv_k = recv_v = jnp.zeros((1, count, width), BF)
    last, dx = qkv_back_call(
        flat, dq, dk, dv, recv_k, recv_v, qkv_weight, dx1, p768, dtab, placed(head)
    )
    last, wide_low = lax.optimization_barrier((last, wide_low))
    last_low = lax.psum_scatter(last, "img", scatter_dimension=0, tiled=True)
    conv_total = seq_total(conv_low)
    wide_total = seq_total(wide_low)
    last_total = seq_total(last_low)

    def taken(total, start, size):
        return total[:, start : start + size]

    g_ff = taken(wide_total, 0, 4 * half)
    g_mu = taken(wide_total, 4 * half, 4 * half)
    g_fs = taken(wide_total, 8 * half, half)
    g_lc = jnp.stack(
        [taken(wide_total, 9 * half, chan), taken(wide_total, 9 * half + chan, chan)], axis=1
    )
    laterals = taken(wide_total, 9 * half + 2 * chan, chan)
    g_lf, g_lm = laterals[:own_q], laterals[own_q : own_q + own_h]
    g_w1 = taken(wide_total, offset, 4 * width)
    g_w2 = (
        taken(wide_total, offset + 4 * width, 4 * width)
        .reshape(unit, 4, width).transpose(1, 0, 2).reshape(4 * unit, width)
    )
    g_wp = taken(wide_total, offset + 8 * width, width)
    vec = taken(wide_total, offset + 9 * width, 128)
    own_c = chan // shards
    g_lg = jnp.concatenate([vec[:own_c, 8:12], vec[:own_c, 24:28]], axis=1)
    g_ls = jnp.concatenate([vec[:own_c, 16:20], vec[:own_c, 28:32]], axis=1)
    g_ffb, g_fng, g_fns, g_mub = (vec[:own_h, 32 + k] for k in range(4))
    g_fsb = vec[:own_q, 48]
    g_b1 = vec[:, 40:44].T.reshape(-1)
    g_pb, g_b2 = vec[:, 6], vec[:, 7]
    g_qkv = last_total[:, : 3 * width]
    late = last_total[:, 3 * width : 3 * width + 128]
    g_bg = jnp.stack([late[:, 0], vec[:, 1]], axis=1)
    g_bs = jnp.stack([late[:, 2], vec[:, 3]], axis=1)
    g_qvb = late[:, 4:6]
    own_t = head // shards
    tabs = last_total[:own_t, 3 * width + 128 :]
    g_tc = tabs[:, : 2 * cols - 1][:, ::-1]
    g_tr = tabs[:, 128 : 128 + 2 * total_rows - 1][:, ::-1]
    g_conv = (
        conv_total.reshape(unit, 4, 3, chan).transpose(2, 0, 1, 3).reshape(3 * unit, 4, chan)
    )
    return (
        maps[0][None], maps[1][None], maps[2][None], maps[3][None],
        dx.reshape(1, lr, cols, width),
        g_bg, g_bs, g_qkv, g_qvb, g_tr, g_tc, g_wp, g_pb, g_w1, g_b1, g_w2, g_b2, g_ff, g_ffb, g_fng, g_fns,
        g_fs, g_fsb, g_mu, g_mub, g_lf, g_lm, g_lc, g_lg, g_ls, g_conv,
    )


def solution(mesh):
    image = P("img", "seq", None, None)
    in_specs = (image, P("img"), P("img")) + (P(),) * 26 + (image,) * 4
    ranks = (2, 2, 2, 2, 2, 2, 2, 1, 2, 1, 2, 1, 2, 1, 1, 1, 2, 1, 2, 1, 2, 2, 3, 2, 2, 3)
    out_specs = (image,) * 5 + tuple(P(*(("img",) + (None,) * (r - 1))) for r in ranks)
    return jax.shard_map(
        per_device, mesh=mesh, in_specs=in_specs, out_specs=out_specs, check_vma=False
    )
```

time: 2230 us -> 725 us (0.33)
  matrix products: 501 us -> 0 us
  local copies, waits for them, and re-layouts: 490 us -> 44.1 us
  waiting for transfers between devices: 686 us -> 289 us
  Pallas kernels: 0 us -> 331 us
  other arithmetic: 349 us -> 24.8 us
  blocking collectives: 94.5 us -> 0 us
  starting transfers between devices: 62.3 us -> 10.1 us
    dot_general x171 -> x0, matrix products: 501 us -> none  [the longest x94 252 us: narrow_product(): return multiply(left, right)]
    reduce_scatter x12 -> x3, waiting for transfers between devices: 637 us -> 241 us  [the longest x1 104 us: per_device(): wide_low = lax.psum_scatter(wide, 'img', scatter_dimension=0, tiled=True)]
    pallas_call x0 -> x17, Pallas kernels: none -> 331 us  [the longest x4 99.1 us: conv_call(): call(functools.partial(conv_kernel, level, block, shards), [sds((rows, co...]
    slice x42 -> x26, local copies, waits for them, and re-layouts: 128 us -> 13.4 us  [the longest x4 3.1 us: per_device(): level_sums[k][1:2]]
    reduce_sum x52 -> x0, other arithmetic: 112 us -> none  [the longest x21 58.4 us: normalize(): return centred * lax.rsqrt(spread + 1e-06) * gain_vec + shift_vec]
    convert_element_type x72 -> x11, other arithmetic: 114 us -> 10.2 us  [the longest x4 4.06 us: placed(): return ((within < own) & (at == shard_at * own + within)).astype(BF)]
    unnamed x2 -> x0, blocking collectives: 94.5 us -> none
    unnamed x561 -> x20, local copies, waits for them, and re-layouts: 82.6 us -> 7.69 us
  transfers between devices with their start and end apart: 41 -> 11, of which waited for: 12 -> 8; matrix products, arithmetic and copies ran while one was open for 41% -> 7% of each run, Pallas kernels for 0% -> 7%
where the time goes in v1:
time: 725 us; the launch traced here: 714 us
  Pallas kernels  331 us (46%)
  waiting for transfers between devices  289 us (40%)
  local copies, waits for them, and re-layouts  44.1 us (6%)
  other arithmetic  24.8 us (3%)
  between operations  15.6 us (2%)
  starting transfers between devices  10.1 us (1%)
    reduce_scatter x1, waiting for transfers between devices, per_device(): wide_low = lax.psum_scatter(wide, 'img', scatter_dimension=0, tiled=True)  104 us
    pallas_call x4, Pallas kernels, conv_call(): call(functools.partial(conv_kernel, level, block, shards), [sds((rows, co...  99.1 us
    reduce_scatter x1, waiting for transfers between devices, per_device(): conv_low = lax.psum_scatter(packed, 'img', scatter_dimension=0, tiled=True)  75.7 us
    reduce_scatter x1, waiting for transfers between devices, per_device(): last_low = lax.psum_scatter(last, 'img', scatter_dimension=0, tiled=True)  60.5 us
    pallas_call x1, Pallas kernels, pyramid_back_call(): call(functools.partial(pyramid_back_kernel, lr, cols), [sds((tokens, widt...  53.2 us
    pallas_call x4, Pallas kernels, conv_back_call(): call(functools.partial(conv_back_kernel, ways, block), out, grid=(rows //...  40 us
    ppermute x2, waiting for transfers between devices, send(): lax.ppermute(parts[(d - 1) * count:d * count], 'seq', [(i, (i - d) % peer...  31.2 us
    pallas_call x1, Pallas kernels, attend_back_call(): call(functools.partial(attend_back_kernel, total_rows, scale, parts), [sd...  29.7 us
  transfers between devices with their start and end apart: 11, of which 8 were waited for; matrix products, arithmetic and copies ran while one was open for 7% of the time, Pallas kernels for 7%

profile of v1, /device:TPU:0, one launch (start us, length us, event | category | flops | bytes accessed | tf_op | source)
XLA Modules:
  0.0 714.1 jit_solution(4522297732361757801)
XLA Ops:
  22.7 5.1 copy.109
  32.9 6.2 qkv.2.refs_1_.refs_6_.refs_8_.refs_9_.refs_11_
  45.1 4.6 qkv.3.refs_7_.refs_9_.refs_10_.refs_12_
  49.7 24.5 %attend.1 = (bf16[512,768]{1,0:T(8,128)(2,1)}, bf16[12,512,256]{2,1,0:T(8,128)(2,1)}, f32[6,2,512]{2,1,0:T(2,128)}) custom-call(s32[1]{0:T(128)} %bitcast.1.refs_0_, bf16[512,2304]{1,0:T(8,128)(2,1)} %qkv.2.refs_1_.refs_6_.refs_8_.refs_9_.refs_11_, bf16[128,128]{1,0:T(8,128)(2,1)} %get-tuple-element.311.refs_2_, ...), custom_call_target="tpu_custom_call" | custom-call | flops 12000000000 | tf_op jit(solution)/shard_map/attend/pallas_call | solution.py:248
  74.2 14.3 %mlp.1 = (f32[512,768]{1,0:T(8,128)}, bf16[512,3072]{1,0:T(8,128)(2,1)}, bf16[512,3072]{1,0:T(8,128)(2,1)}, bf16[512,768]{1,0:T(8,128)(2,1)}) custom-call(bf16[512,768]{1,0:T(8,128)(2,1)} %bitcast.107, bf16[512,768]{1,0:T(8,128)(2,1)} %get-tuple-element.76.o_ref.refs_4_, bf16[768,768]{1,0:T(8,128)(2,1)} %wp_ref.3, bf16[768,3072]{1,0:T(8,128)(2,1)} %w1_ref.3, ...), custom_call_target="tpu_custom_call" | custom-call | flops 11000000512 | tf_op jit(solution)/shard_map/mlp/pallas_call | solution.py:313
  88.5 21.0 %pyramid.1 = (bf16[8,4,256,256]{3,2,1,0:T(8,128)(2,1)}, bf16[8,2,128,256]{3,2,1,0:T(8,128)(2,1)}, bf16[512,256]{1,0:T(8,128)(2,1)}, bf16[128,256]{1,0:T(8,128)(2,1)}) custom-call(bf16[512,768]{1,0:T(8,128)(2,1)} %get-tuple-element.77.y_ref, bf16[768,1536]{1,0:T(8,128)(2,1)} %ff_ref.3, bf16[768,384]{1,0:T(8,128)(2,1)} %fs_ref.3, bf16[768,1536]{1,0:T(8,128)(2,1)} %mu_ref.3, ...), custom_call_target="tpu_custom_call" | custom-call | flops 8000000000 | tf_op jit(solution)/shard_map/pyramid/pallas_call | solution.py:422
  114.3 6.1 collective-permute-done.1
  123.1 5.2 conv3.1
  129.9 8.7 %conv2.1 = (bf16[8,64,256]{2,1,0:T(8,128)(2,1)}, bf16[8,64,256]{2,1,0:T(8,128)(2,1)}, bf16[768,3072]{1,0:T(8,128)(2,1)}, f32[8,256]{1,0:T(8,128)}) custom-call(bf16[8,64,256]{2,1,0:T(8,128)(2,1)} %bitcast.110, bf16[2,64,256]{2,1,0:T(8,128)(2,1)} %fusion.17.rim_ref, bf16[4,3,768,256]{3,2,1,0:T(8,128)(2,1)} %bitcast.94, ...), custom_call_target="tpu_custom_call", output_to_operand_aliasing={{2}: (5, {})} | custom-call | flops 1207959552 | tf_op jit(solution)/shard_map/conv2/pallas_call | solution.py:555
  140.1 21.0 %conv1.1 = (bf16[16,128,256]{2,1,0:T(8,128)(2,1)}, bf16[16,128,256]{2,1,0:T(8,128)(2,1)}, bf16[768,3072]{1,0:T(8,128)(2,1)}, f32[8,256]{1,0:T(8,128)}) custom-call(bf16[16,128,256]{2,1,0:T(8,128)(2,1)} %bitcast.117, bf16[2,128,256]{2,1,0:T(8,128)(2,1)} %fusion.15.rim_ref, bf16[4,3,768,256]{3,2,1,0:T(8,128)(2,1)} %bitcast.95, ...), custom_call_target="tpu_custom_call", output_to_operand_aliasing={{2}: (5, {})} | custom-call | flops 4831838208 | tf_op jit(solution)/shard_map/conv1/pallas_call | solution.py:555
  162.0 64.1 %conv0.1 = (bf16[32,256,256]{2,1,0:T(8,128)(2,1)}, bf16[32,256,256]{2,1,0:T(8,128)(2,1)}, bf16[768,3072]{1,0:T(8,128)(2,1)}, f32[8,256]{1,0:T(8,128)}) custom-call(bf16[32,256,256]{2,1,0:T(8,128)(2,1)} %bitcast.115, bf16[2,256,256]{2,1,0:T(8,128)(2,1)} %fusion.13.rim_ref, bf16[4,3,768,256]{3,2,1,0:T(8,128)(2,1)} %bitcast.96, ...), custom_call_target="tpu_custom_call", output_to_operand_aliasing={{2}: (5, {})} | custom-call | flops 19327352832 | tf_op jit(solution)/shard_map/conv0/pallas_call | solution.py:555
  239.5 4.1 conv_back2.1.dzb_ref
  243.6 24.3 %conv_back0.1 = bf16[4,4,512,256]{3,2,1,0:T(8,128)(2,1)} custom-call(bf16[32,256,256]{2,1,0:T(8,128)(2,1)} %get-tuple-element.90.dr_ref, bf16[2,256,256]{2,1,0:T(8,128)(2,1)} %fusion.12.rim_ref, bf16[4,3,768,256]{3,2,1,0:T(8,128)(2,1)} %bitcast.99), custom_call_target="tpu_custom_call" | custom-call | flops 9663676416 | tf_op jit(solution)/shard_map/conv_back0/pallas_call | solution.py:631
  267.9 8.6 %conv_back1.1.dzm_ref = bf16[2,2,512,256]{3,2,1,0:T(8,128)(2,1)} custom-call(bf16[16,128,256]{2,1,0:T(8,128)(2,1)} %get-tuple-element.91.dr_ref, bf16[2,128,256]{2,1,0:T(8,128)(2,1)} %fusion.14.rim_ref, bf16[4,3,768,256]{3,2,1,0:T(8,128)(2,1)} %bitcast.100), custom_call_target="tpu_custom_call" | custom-call | flops 2415919104 | tf_op jit(solution)/shard_map/conv_back1/pallas_call | solution.py:631
  276.5 53.2 %pyramid_back.1 = (f32[512,768]{1,0:T(8,128)}, bf16[768,11264]{1,0:T(8,128)(2,1)}, f32[8,384]{1,0:T(8,128)}, f32[8,192]{1,0:T(8,128)}, f32[16,256]{1,0:T(8,128)}) custom-call(bf16[512,768]{1,0:T(8,128)(2,1)} %get-tuple-element.77.y_ref, bf16[768,1536]{1,0:T(8,128)(2,1)} %ff_ref.3, bf16[768,384]{1,0:T(8,128)(2,1)} %fs_ref.3, bf16[768,1536]{1,0:T(8,128)(2,1)} %mu_ref.3, ...), custom_call_target="tpu_custom_call" | custom-call | flops 20000000000 | tf_op jit(solution)/shard_map/pyramid_back/pallas_call | solution.py:804
  329.7 24.4 %mlp_back.1 = (bf16[768,11264]{1,0:T(8,128)(2,1)}, f32[512,768]{1,0:T(8,128)}, bf16[512,768]{1,0:T(8,128)(2,1)}) custom-call(f32[512,768]{1,0:T(8,128)} %get-tuple-element.94.dy_ref, bf16[512,3072]{1,0:T(8,128)(2,1)} %get-tuple-element.95.g_ref, bf16[512,3072]{1,0:T(8,128)(2,1)} %get-tuple-element.96.gp_ref, ...), custom_call_target="tpu_custom_call", output_to_operand_aliasing={{0}: (16, {})} | custom-call | flops 22000001024 | tf_op jit(solution)/shard_map/mlp_back/pallas_call | solution.py:990
  355.6 29.7 %attend_back.1 = (bf16[512,768]{1,0:T(8,128)(2,1)}, f32[128,256]{1,0:T(8,128)}, bf16[512,768]{1,0:T(8,128)(2,1)}, bf16[512,768]{1,0:T(8,128)(2,1)}, bf16[512,768]{1,0:T(8,128)(2,1)}, /*index=5*/bf16[512,768]{1,0:T(8,128)(2,1)}) custom-call(s32[1]{0:T(128)} %bitcast.1.refs_0_, bf16[512,2304]{1,0:T(8,128)(2,1)} %qkv.2.refs_1_.refs_6_.refs_8_.refs_9_.refs_11_, ...), custom_call_target="tpu_custom_call" | custom-call | flops 30000001024 | tf_op jit(solution)/shard_map/attend_back/pallas_call | solution.py:1151
  388.4 17.7 %collective-permute-done.3 = bf16[512,768]{1,0:T(8,128)(2,1)S(1)} collective-permute-done((bf16[512,768]{1,0:T(8,128)(2,1)}, bf16[512,768]{1,0:T(8,128)(2,1)S(1)}, u32[]{:S(2)}, u32[]{:S(2)}) %collective-permute-start.3) | collective-permute-done | bytes 786464 | tf_op jit(solution)/shard_map/ppermute | solution.py:1454
  406.1 13.5 %collective-permute-done.4 = bf16[512,768]{1,0:T(8,128)(2,1)S(1)} collective-permute-done((bf16[512,768]{1,0:T(8,128)(2,1)}, bf16[512,768]{1,0:T(8,128)(2,1)S(1)}, u32[]{:S(2)}, u32[]{:S(2)}) %collective-permute-start.4) | collective-permute-done | bytes 786464 | tf_op jit(solution)/shard_map/ppermute | solution.py:1454
  420.5 13.6 %qkv_back.1 = (bf16[768,2688]{1,0:T(8,128)(2,1)}, f32[512,768]{1,0:T(8,128)}) custom-call(bf16[512,768]{1,0:T(8,128)(2,1)} %bitcast.108, bf16[512,768]{1,0:T(8,128)(2,1)} %get-tuple-element.108.dq_ref, bf16[512,768]{1,0:T(8,128)(2,1)} %get-tuple-element.109.dk_ref, bf16[512,768]{1,0:T(8,128)(2,1)} %get-tuple-element.110.dv_ref, ...), custom_call_target="tpu_custom_call" | custom-call | flops 4000000000 | tf_op jit(solution)/shard_map/qkv_back/pallas_call | solution.py:1249
  434.1 104.4 %reduce-scatter.4.cloned.1.call-done = bf16[48,11264]{1,0:T(8,128)(2,1)} async-done(((bf16[768,11264]{1,0:T(8,128)(2,1)}), bf16[48,11264]{1,0:T(8,128)(2,1)}) %reduce-scatter.4.cloned.1.call-update) | async-done | bytes 1081360 | tf_op jit(solution)/shard_map/reduce_scatter | solution.py:1442
  541.2 75.7 %reduce-scatter.8.cloned.1.call-done = bf16[48,3072]{1,0:T(8,128)(2,1)} async-done(((bf16[768,3072]{1,0:T(8,128)(2,1)}), bf16[48,3072]{1,0:T(8,128)(2,1)}) %reduce-scatter.8.cloned.1.call-update) | async-done | bytes 294928 | tf_op jit(solution)/shard_map/reduce_scatter | solution.py:1401
  618.4 6.4 collective-permute-done.7
  632.0 60.5 %reduce-scatter.6.cloned.1.call-done = bf16[48,2688]{1,0:T(8,128)(2,1)} async-done(((bf16[768,2688]{1,0:T(8,128)(2,1)}), bf16[48,2688]{1,0:T(8,128)(2,1)}) %reduce-scatter.6.cloned.1.call-update) | async-done | bytes 258064 | tf_op jit(solution)/shard_map/reduce_scatter | solution.py:1471
  (152 shorter events, 81.7 us)
Async XLA Ops:
  7.2 531.3 %reduce-scatter.4.cloned.1.call-start = ((), (), s32[]{:S(2)}) async-start(), calls=%async_computation.3 | async-start | bytes 18382848 | tf_op jit(solution)/shard_map/reduce_scatter | solution.py:1442
  7.2 37.0 %collective-permute-start = (bf16[512,768]{1,0:T(8,128)(2,1)}, bf16[512,768]{1,0:T(8,128)(2,1)S(1)}, u32[]{:S(2)}, u32[]{:S(2)}) collective-permute-start(bf16[512,768]{1,0:T(8,128)(2,1)} %bitcast.105), channel_id=1, source_target_pairs={{0,1},{1,0},{2,3},{3,2},{4,5},{5,4},{6,7},{7,6},{8,9},{9,8},{10,11... | collective-permute-start | bytes 2359304 | tf_op jit(solution)/shard_map/ppermute | solution.py:1333
  22.7 5.2 copy-start.3
  22.7 5.2 copy-start.4
  32.9 9.2 %copy-start = (bf16[768,2,256]{2,1,0:T(2,128)(2,1)S(1)}, bf16[768,2,256]{2,1,0:T(2,128)(2,1)}, u32[]{:S(2)}) copy-start(bf16[768,2,256]{2,1,0:T(2,128)(2,1)} %param.58) | copy-start | bytes 2359300
  44.2 0.9 copy-start.2
  113.0 7.5 %collective-permute-start.1 = (bf16[480,256]{1,0:T(8,128)(2,1)S(1)}, bf16[480,256]{1,0:T(8,128)(2,1)S(1)}, u32[]{:S(2)}, u32[]{:S(2)}) collective-permute-start(bf16[480,256]{1,0:T(8,128)(2,1)S(1)} %maximum_select_fusion), channel_id=1, source_target_pairs={{0,1},{1,0},{2,3},{3,2},{4,5},{5,4},{6,7},{7,6},{8,9},{9,8},{10,11... | collective-permute-start | bytes 737288 | tf_op jit(solution)/shard_map/ppermute | solution.py:1289
  227.2 6.6 collective-permute-start.2
  354.1 262.7 %reduce-scatter.8.cloned.1.call-start = ((), (), s32[]{:S(2)}) async-start(), calls=%async_computation.5 | async-start | bytes 5013504 | tf_op jit(solution)/shard_map/reduce_scatter | solution.py:1401
  354.9 337.7 %reduce-scatter.6.cloned.1.call-start = ((), (), s32[]{:S(2)}) async-start(), calls=%async_computation.4 | async-start | bytes 4386816 | tf_op jit(solution)/shard_map/reduce_scatter | solution.py:1471
  385.3 20.8 %collective-permute-start.3 = (bf16[512,768]{1,0:T(8,128)(2,1)}, bf16[512,768]{1,0:T(8,128)(2,1)S(1)}, u32[]{:S(2)}, u32[]{:S(2)}) collective-permute-start(bf16[512,768]{1,0:T(8,128)(2,1)} %get-tuple-element.111), channel_id=1, source_target_pairs={{0,1},{1,0},{2,3},{3,2},{4,5},{5,4},{6,7},{7,6},{8,9},{9,8},{10,11... | collective-permute-start | bytes 2359304 | tf_op jit(solution)/shard_map/ppermute | solution.py:1454
  386.1 33.6 %collective-permute-start.4 = (bf16[512,768]{1,0:T(8,128)(2,1)}, bf16[512,768]{1,0:T(8,128)(2,1)S(1)}, u32[]{:S(2)}, u32[]{:S(2)}) collective-permute-start(bf16[512,768]{1,0:T(8,128)(2,1)} %get-tuple-element.112), channel_id=1, source_target_pairs={{0,1},{1,0},{2,3},{3,2},{4,5},{5,4},{6,7},{7,6},{8,9},{9,8},{10,11... | collective-permute-start | bytes 2359304 | tf_op jit(solution)/shard_map/ppermute | solution.py:1454
  406.1 13.5 %copy-start.5 = (bf16[512,768]{1,0:T(8,128)(2,1)}, bf16[512,768]{1,0:T(8,128)(2,1)S(1)}, u32[]{:S(2)}) copy-start(bf16[512,768]{1,0:T(8,128)(2,1)S(1)} %collective-permute-done.3) | copy-start | bytes 2359300
  419.6 0.9 copy-start.6
  538.5 1.2 copy-start.1
  539.7 88.2 %collective-permute-start.6 = (bf16[48,11264]{1,0:T(8,128)(2,1)S(1)}, bf16[48,11264]{1,0:T(8,128)(2,1)}, u32[]{:S(2)}, u32[]{:S(2)}) collective-permute-start(bf16[48,11264]{1,0:T(8,128)(2,1)S(1)} %copy-done.1), channel_id=1, source_target_pairs={{0,1},{1,0},{2,3},{3,2},{4,5},{5,4},{6,7},{7,6},{8,9},{9,8},{10,11... | collective-permute-start | bytes 3244040 | tf_op jit(solution)/shard_map/ppermute | solution.py:1307
  616.9 8.0 %collective-permute-start.7 = (bf16[48,3072]{1,0:T(8,128)(2,1)}, bf16[48,3072]{1,0:T(8,128)(2,1)S(1)}, u32[]{:S(2)}, u32[]{:S(2)}) collective-permute-start(bf16[48,3072]{1,0:T(8,128)(2,1)} %reduce-scatter.8.cloned.1.call-done), channel_id=1, source_target_pairs={{0,1},{1,0},{2,3},{3,2},{4,5},{5,4},{6,7},{7,6},{8,9},{9,8},{10,11... | collective-permute-start | bytes 884744 | tf_op jit(solution)/shard_map/ppermute | solution.py:1307
  692.5 9.5 %collective-permute-start.5 = (bf16[48,2688]{1,0:T(8,128)(2,1)}, bf16[48,2688]{1,0:T(8,128)(2,1)}, u32[]{:S(2)}, u32[]{:S(2)}) collective-permute-start(bf16[48,2688]{1,0:T(8,128)(2,1)} %reduce-scatter.6.cloned.1.call-done), channel_id=1, source_target_pairs={{0,1},{1,0},{2,3},{3,2},{4,5},{5,4},{6,7},{7,6},{8,9},{9,8},{10,11... | collective-permute-start | bytes 774152 | tf_op jit(solution)/shard_map/ppermute | solution.py:1307
Sparse Core Ops, SparseCore 0:
  354.3 184.1 reduce-scatter.3
  542.3 74.5 reduce-scatter.7
  621.3 71.1 reduce-scatter.5

commit v2 on v1

v2 whole, which is shorter than its diff:
```python
import functools

import jax
import jax.numpy as jnp
from jax import lax
from jax.experimental import pallas as pl
from jax.experimental.pallas import tpu as pltpu
from jax.sharding import PartitionSpec as P

F32 = jnp.float32
BF = jnp.bfloat16
NEG = -1e30
EPS = 1e-6
SQRT_HALF = 0.7071067811865476
INV_SQRT_2PI = 0.3989422804014327
VMEM_LIMIT = 60 * 1024 * 1024


def mm(left, right):
    return lax.dot_general(left, right, (((1,), (0,)), ((), ())), preferred_element_type=F32)


def mt(left, right):
    return lax.dot_general(left, right, (((1,), (1,)), ((), ())), preferred_element_type=F32)


def tm(left, right):
    return lax.dot_general(left, right, (((0,), (0,)), ((), ())), preferred_element_type=F32)


def call(
    kernel, outs, grid=(), in_specs=None, out_specs=None, scratch=(), flops=0, name=None, aliases=None
):
    return pl.pallas_call(
        kernel,
        out_shape=outs,
        grid=grid,
        in_specs=in_specs,
        out_specs=out_specs,
        scratch_shapes=scratch,
        name=name,
        input_output_aliases=aliases or {},
        cost_estimate=pl.CostEstimate(flops=int(flops) // COST_SHARE, bytes_accessed=0, transcendentals=0),
        compiler_params=pltpu.CompilerParams(vmem_limit_bytes=VMEM_LIMIT),
    )


def whole(shape):
    return pl.BlockSpec(shape, lambda *_: (0,) * len(shape))


def sds(shape, dtype):
    return jax.ShapeDtypeStruct(shape, dtype)


def stats(values):
    average = jnp.mean(values, axis=-1, keepdims=True)
    centred = values - average
    spread = jnp.mean(centred * centred, axis=-1, keepdims=True)
    inverse = lax.rsqrt(spread + EPS)
    return centred * inverse, inverse


def norm_back(grad_hat, hat, inverse):
    first = jnp.mean(grad_hat, axis=-1, keepdims=True)
    second = jnp.mean(grad_hat * hat, axis=-1, keepdims=True)
    return inverse * (grad_hat - first - hat * second)


def rowsum(values):
    return jnp.sum(values, axis=0, keepdims=True)


UNROLL = 64
COST_SHARE = 100
CONV_PIXELS = 1024
MOVE_ROWS = 8
BACK_PIXELS = 2048


def by_chunks(total, size, body, carry=0, unroll=None):
    unroll = max(1, min(unroll or UNROLL, total // size))

    def step(k, inner):
        for u in range(unroll):
            out = body(pl.ds(pl.multiple_of((k * unroll + u) * size, size), size), inner)
            inner = inner if out is None else out
        return inner

    if unroll == total // size:
        return step(0, carry)
    return lax.fori_loop(0, total // size // unroll, step, carry)


def put_shards(source, keep_ref, send_ref, lanes, shards, first, core, sem):
    unit = source.shape[0] // shards
    for s in range(shards):
        at = first + s
        rows = pl.ds(pl.multiple_of(lax.div(at, 2) * unit, unit), unit)
        piece = source.at[pl.ds(s * unit, unit)]

        @pl.when(lax.rem(at, 2) == core)
        def _():
            pltpu.make_async_copy(piece, keep_ref.at[rows, lanes], sem).start()

        @pl.when(lax.rem(at, 2) != core)
        def _():
            pltpu.make_async_copy(piece, send_ref.at[rows, lanes], sem).start()


def wait_shards(source, sem):
    pltpu.make_async_copy(source, source, sem).wait()


def repeat(count, body):
    for k in range(count):
        body(k, 0)


def gelu_pair(values):
    half = 0.5 * (1.0 + lax.erf(values * SQRT_HALF))
    slope = half + values * (jnp.exp(-0.5 * values * values) * INV_SQRT_2PI)
    return values * half, slope


def shift_matrix(size, amount):
    out_at = lax.broadcasted_iota(jnp.int32, (size, size), 0)
    in_at = lax.broadcasted_iota(jnp.int32, (size, size), 1)
    return jnp.where(in_at == out_at + amount, 1.0, 0.0).astype(BF)


def weave_matrix(size, ways, inverse=False):
    out_at = lax.broadcasted_iota(jnp.int32, (size, size), 1 if inverse else 0)
    in_at = lax.broadcasted_iota(jnp.int32, (size, size), 0 if inverse else 1)
    source = lax.rem(out_at, ways) * (size // ways) + lax.div(out_at, ways)
    return jnp.where(in_at == source, 1.0, 0.0).astype(BF)


def qkv_kernel(x_ref, w_ref, b_ref, p_ref, out_ref, n1_ref):
    @pl.when(pl.program_id(1) == 0)
    def _():
        def norm(sl, carry):
            hat, _ = stats(x_ref[sl, :].astype(F32))
            n1_ref[sl, :] = (hat * p_ref[0:1, :] + p_ref[2:3, :]).astype(BF)

        by_chunks(x_ref.shape[0], 32, norm)

    out_ref[...] = (mm(n1_ref[...], w_ref[...]) + b_ref[0]).astype(BF)


def qkv_call(tokens, weight, bias3, p768, first):
    rows, width = tokens.shape
    block = 512
    count = 3 - first
    return call(
        qkv_kernel,
        sds((rows, count * width), BF),
        grid=(rows // block, count),
        in_specs=[
            pl.BlockSpec((block, width), lambda i, j: (i, 0)),
            pl.BlockSpec((width, width), lambda i, j: (0, j + first)),
            pl.BlockSpec((1, 1, width), lambda i, j: (j + first, 0, 0)),
            whole(p768.shape),
        ],
        out_specs=pl.BlockSpec((block, width), lambda i, j: (i, j)),
        scratch=[pltpu.VMEM((block, width), BF)],
        flops=2 * rows * width * width * count,
        name="qkv",
    )(tokens, weight, bias3, p768)


def aug_layout(total_rows):
    low_at = 64 + total_rows
    if low_at + total_rows + 1 > 128:
        low_at = 128
    width = 128 * (2 + (low_at + total_rows) // 128)
    return low_at, width


def build_kaug(kaug_ref, k_refs, oh1_ref, oh2_ref, odd):
    lane = lax.broadcasted_iota(jnp.int32, (512, 128), 1)
    mine = (lane >= 64) if odd else (lane < 64)
    at = 0
    for k_ref in k_refs:
        for row in range(0, k_ref.shape[0], 512):
            keys = k_ref[row : row + 512, :].astype(F32)
            hot = oh1_ref[at : at + 512, :].astype(F32)
            kaug_ref[at : at + 512, 0:128] = jnp.where(mine, keys, hot).astype(BF)
            at += 512


def build_qaug(first_row, qp, tw_ref, tr_ref, qaug_ref, odd, total_rows, scale):
    low_at, width = aug_layout(total_rows)
    tokens = qp.shape[0]
    lane = lax.broadcasted_iota(jnp.int32, (64, 128), 1)
    mine = (lane >= 64) if odd else (lane < 64)
    lane_all = lax.broadcasted_iota(jnp.int32, (tokens, 128), 1)
    mine_all = (lane_all >= 64) if odd else (lane_all < 64)
    qf = qp.astype(F32)
    qm = jnp.where(mine_all, qf, 0.0).astype(BF)
    cols = mm(qm, tw_ref[...])
    rows = mm(qm, tr_ref[...])
    for i in range(tokens // 64):
        sl = slice(64 * i, 64 * i + 64)
        upper = pltpu.roll(cols[sl], 1, 1, stride=1, stride_axis=0)
        lower = pltpu.roll(cols[sl], 65, 1, stride=1, stride_axis=0)
        first = jnp.where(mine, qf[sl] * scale, lower if odd else upper)
        col_low = lower - lower.astype(BF).astype(F32)
        shift = lax.rem(first_row + i + (65 - total_rows + 128), 128)
        row_part = pltpu.roll(rows[sl], shift, 1)
        row_low = row_part - row_part.astype(BF).astype(F32)
        qaug_ref[sl, 0:128] = first.astype(BF)
        one_at = low_at + total_rows
        if low_at < 128:
            rest = jnp.where(lane == one_at, 1.0, 0.0)
            rest = jnp.where(
                (lane >= low_at) & (lane < one_at), pltpu.roll(row_low, total_rows, 1), rest
            )
            second = jnp.where(lane < 64, col_low, jnp.where(lane < low_at, row_part, rest))
            qaug_ref[sl, 128:256] = second.astype(BF)
        else:
            second = jnp.where(
                lane < 64, col_low, jnp.where(lane < 64 + total_rows, row_part, 0.0)
            )
            third = jnp.where(
                lane < total_rows,
                pltpu.roll(row_low, 64, 1),
                jnp.where(lane == total_rows, 1.0, 0.0),
            )
            qaug_ref[sl, 128:256] = second.astype(BF)
            qaug_ref[sl, 256:384] = third.astype(BF)


def attend_kernel(total_rows, scale, others, *refs):
    first_ref, q_ref, tw_ref, tr_ref, oh1_ref, oh2_ref = refs[:6]
    k_refs = refs[6 : 6 + others]
    v_refs = refs[6 + others : 6 + 2 * others]
    o_ref, qaug_out, lse_ref, kaug_ref, v_ref, p_ref, ot_ref, scores_ref = refs[6 + 2 * others :]
    first_row = first_ref[0]
    tokens = q_ref.shape[0]
    keys = kaug_ref.shape[0]

    @pl.when(pl.program_id(0) == 0)
    def _():
        kaug_ref[:, 128:] = oh2_ref[...]

    at = 0
    for ref in v_refs:
        v_ref[at : at + ref.shape[0], :] = ref[...]
        at += ref.shape[0]
    qp = q_ref[...]
    for odd in (0, 1):
        build_kaug(kaug_ref, k_refs, oh1_ref, oh2_ref, odd)
        build_qaug(first_row, qp, tw_ref, tr_ref, qaug_out.at[odd], odd, total_rows, scale)

        def queries(t, carry):
            sl = pl.ds(pl.multiple_of(t * 256, 256), 256)
            scores_ref[...] = mt(kaug_ref[...], qaug_out[odd, sl, :])

            def highest(rows, top):
                return jnp.maximum(top, jnp.max(scores_ref[rows, :], axis=0, keepdims=True))

            top = by_chunks(keys, 128, highest, jnp.full((1, 256), NEG, F32))

            def weigh(rows, total):
                weight = jnp.exp(scores_ref[rows, :] - top)
                p_ref[rows, :] = weight.astype(BF)
                return total + rowsum(weight)

            total = by_chunks(keys, 128, weigh, jnp.zeros((1, 256), F32))
            lse_ref[0, odd : odd + 1, sl] = top + jnp.log(total)
            out_t = tm(v_ref[...], p_ref[...])
            ot_ref[64 * odd : 64 * odd + 64, sl] = out_t[64 * odd : 64 * odd + 64] / total
            return carry

        repeat(tokens // 256, queries)
    o_ref[...] = ot_ref[...].T.astype(BF)


def attend_call(first, qkv_own, kv_others, tables, oh1, oh2, total_rows, heads):
    tokens = qkv_own.shape[0]
    width = qkv_own.shape[1] // 3
    keys = oh1.shape[0]
    aug = 128 + oh2.shape[1]
    pairs = width // 128
    tw, tr = tables
    parts = 1 + (1 if kv_others is not None else 0)
    in_specs = [
        pl.BlockSpec(memory_space=pltpu.SMEM),
        pl.BlockSpec((tokens, 128), lambda h: (0, h)),
        whole(tw.shape),
        whole(tr.shape),
        whole(oh1.shape),
        whole(oh2.shape),
    ]
    k_args, v_args, k_specs, v_specs = [qkv_own], [qkv_own], [], []
    k_specs.append(pl.BlockSpec((tokens, 128), lambda h: (0, h + pairs)))
    v_specs.append(pl.BlockSpec((tokens, 128), lambda h: (0, h + 2 * pairs)))
    if kv_others is not None:
        k_args.append(kv_others)
        v_args.append(kv_others)
        k_specs.append(pl.BlockSpec((keys - tokens, 128), lambda h: (0, h)))
        v_specs.append(pl.BlockSpec((keys - tokens, 128), lambda h: (0, h + pairs)))
    scale = (width // heads) ** -0.5
    return call(
        functools.partial(attend_kernel, total_rows, scale, parts),
        [
            sds((tokens, width), BF),
            sds((heads, tokens, aug), BF),
            sds((pairs, 2, tokens), F32),
        ],
        grid=(pairs,),
        in_specs=in_specs + k_specs + v_specs,
        out_specs=[
            pl.BlockSpec((tokens, 128), lambda h: (0, h)),
            pl.BlockSpec((2, tokens, aug), lambda h: (h, 0, 0)),
            pl.BlockSpec((1, 2, tokens), lambda h: (h, 0, 0)),
        ],
        scratch=[
            pltpu.VMEM((keys, aug), BF),
            pltpu.VMEM((keys, 128), BF),
            pltpu.VMEM((keys, 256), BF),
            pltpu.VMEM((128, tokens), F32),
            pltpu.VMEM((keys, 256), F32),
        ],
        flops=25e9,
        name="attend",
    )(first, qkv_own, tw, tr, oh1, oh2, *k_args, *v_args)


def mlp_kernel(
    x_ref, o_ref, wp_ref, w1_ref, b1_ref, w2_ref, p_ref, x1_ref, g_ref, gp_ref, y_ref, n2_ref, acc_ref,
    hidden_ref,
):
    step = pl.program_id(0)
    tokens = x_ref.shape[0]

    @pl.when(step == 0)
    def _():
        product = mm(o_ref[...], wp_ref[...])
        acc_ref[...] = product

        def norm(sl, carry):
            middle = x_ref[sl, :].astype(F32) + (acc_ref[sl, :] + p_ref[6:7, :])
            x1_ref[sl, :] = middle
            acc_ref[sl, :] = jnp.zeros_like(middle)
            hat, _ = stats(middle)
            n2_ref[sl, :] = (hat * p_ref[1:2, :] + p_ref[3:4, :]).astype(BF)

        by_chunks(tokens, 32, norm)

    hidden_ref[...] = mm(n2_ref[...], w1_ref[...])

    def act(sl, carry):
        value, slope = gelu_pair(hidden_ref[sl, :] + b1_ref[...])
        g_ref[sl, :] = value.astype(BF)
        gp_ref[sl, :] = slope.astype(BF)

    by_chunks(tokens, 32, act)
    acc_ref[...] += mm(g_ref[...], w2_ref[...])

    @pl.when(step == pl.num_programs(0) - 1)
    def _():
        y_ref[...] = (x1_ref[...] + (acc_ref[...] + p_ref[7:8, :])).astype(BF)


def mlp_call(tokens, attended, wp, w1, b1, w2, p768):
    rows, width = tokens.shape
    hidden = w1.shape[1]
    return call(
        mlp_kernel,
        [sds((rows, width), F32), sds((rows, hidden), BF), sds((rows, hidden), BF), sds((rows, width), BF)],
        grid=(hidden // width,),
        in_specs=[
            whole((rows, width)),
            whole((rows, width)),
            whole(wp.shape),
            pl.BlockSpec((width, width), lambda s: (0, s)),
            pl.BlockSpec((1, width), lambda s: (0, s)),
            pl.BlockSpec((width, width), lambda s: (s, 0)),
            whole(p768.shape),
        ],
        out_specs=[
            whole((rows, width)),
            pl.BlockSpec((rows, width), lambda s: (0, s)),
            pl.BlockSpec((rows, width), lambda s: (0, s)),
            whole((rows, width)),
        ],
        scratch=[
            pltpu.VMEM((rows, width), BF),
            pltpu.VMEM((rows, width), F32),
            pltpu.VMEM((rows, width), F32),
        ],
        flops=14e9,
        name="mlp",
    )(tokens, attended, wp, w1, b1, w2, p768)


def pool_matrix(a, b, rows, cols):
    count = rows * cols // 4
    out_at = lax.broadcasted_iota(jnp.int32, (count, rows * cols), 0)
    in_at = lax.broadcasted_iota(jnp.int32, (count, rows * cols), 1)
    half = cols // 2
    source = (2 * lax.div(out_at, half) + a) * cols + 2 * lax.rem(out_at, half) + b
    return jnp.where(in_at == source, 1.0, 0.0).astype(BF)


def lateral_norm(product_ref, count, gain, shift, write):
    def norm(sl, carry):
        hat, _ = stats(product_ref[sl, :])
        write(sl, (hat * gain + shift).astype(BF))

    by_chunks(count, 64, norm)


def pyramid_kernel(
    lr, cols, y_ref, ff_ref, fs_ref, mu_ref, lf_ref, lm_ref, lc0_ref, lc1_ref, p384_ref, fsb_ref, p256_ref,
    zf_ref, zm_ref, zb_ref, zc_ref, plane_ref, mplane_ref, f2_ref, first_ref, product_ref,
    third_ref, stack_ref,
):
    tokens = lr * cols
    half = mu_ref.shape[1] // 2
    quart = fs_ref.shape[0] // 4

    def offset(b, carry):
        columns = pl.ds(pl.multiple_of(b * half, half), half)
        first_ref[...] = mm(y_ref[...], ff_ref[:, columns])

        def norm(sl, inner):
            hat, _ = stats(first_ref[sl, :] + p384_ref[0:1, :])
            value = hat * p384_ref[1:2, :] + p384_ref[2:3, :]
            f2_ref[sl, :] = (0.5 * value * (1.0 + lax.erf(value * SQRT_HALF))).astype(BF)

        by_chunks(tokens, 64, norm)

        for k in range(4):
            third_ref[k * tokens : (k + 1) * tokens, :] = (
                mt(f2_ref[...], fs_ref[k * quart : (k + 1) * quart, :]) + fsb_ref[...]
            ).astype(BF)
        stack_ref[...] = mm(third_ref[...], lf_ref[...])
        for k in range(4):

            def write(sl, values):
                plane_ref[k // 2, 2 * b + k % 2, sl, :] = values

            part = stack_ref.at[k * tokens : (k + 1) * tokens]
            lateral_norm(part, tokens, p256_ref[0:1, :], p256_ref[8:9, :], write)
        middle = (mm(y_ref[...], mu_ref[:, columns]) + p384_ref[3:4, :]).astype(BF)
        product_ref[...] = mm(middle, lm_ref[...])

        def write_middle(sl, values):
            mplane_ref[b, sl, :] = values

        lateral_norm(product_ref, tokens, p256_ref[1:2, :], p256_ref[9:10, :], write_middle)
        return carry

    repeat(2, offset)
    weave4 = weave_matrix(4 * cols, 4)
    weave2 = weave_matrix(2 * cols, 2)

    def weave(i, carry):
        sl = pl.ds(pl.multiple_of(i * cols, cols), cols)
        for c in (0, 1):
            planes = jnp.concatenate([plane_ref[c, k, sl, :] for k in range(4)], axis=0)
            zf_ref[i, c] = mm(weave4, planes).astype(BF)
        planes = jnp.concatenate([mplane_ref[k, sl, :] for k in range(2)], axis=0)
        zm_ref[i, 0] = mm(weave2, planes).astype(BF)
        return carry

    repeat(lr, weave)

    @pl.when(pl.program_id(0) == 0)
    def _():
        product_ref[...] = mm(y_ref[...], lc0_ref[...])

        def write_base(sl, values):
            zb_ref[sl, :] = values

        lateral_norm(product_ref, tokens, p256_ref[2:3, :], p256_ref[10:11, :], write_base)
        pooled = pool_picks(y_ref, pick_ref=None, rows=lr, cols=cols)
        product_ref[0 : tokens // 4, :] = mm(pooled.astype(BF), lc1_ref[...])

        def write_coarse(sl, values):
            zc_ref[sl, :] = values

        lateral_norm(product_ref, tokens // 4, p256_ref[3:4, :], p256_ref[11:12, :], write_coarse)


def pool_picks(y_ref, pick_ref, rows, cols):
    def pick(k, top):
        values = mm(pool_matrix(k // 2, k % 2, rows, cols), y_ref[...])
        if pick_ref is not None:
            pick_ref[k] = values
        return jnp.maximum(top, values)

    low = jnp.full((rows * cols // 4, y_ref.shape[1]), -jnp.inf, F32)
    for k in range(4):
        low = pick(k, low)
    return low


def pyramid_call(y, lr, cols, ff, fs, mu, lf, lm, lc0, lc1, p384, fsb, p256):
    tokens, width = y.shape
    outs = lf.shape[1]
    half2 = ff.shape[1] // 2
    return call(
        functools.partial(pyramid_kernel, lr, cols),
        [
            sds((lr, 4, 4 * cols, outs), BF),
            sds((lr, 2, 2 * cols, outs), BF),
            sds((tokens, outs), BF),
            sds((tokens // 4, outs), BF),
        ],
        grid=(2,),
        in_specs=[
            whole(y.shape),
            pl.BlockSpec((width, half2), lambda a: (0, a)),
            whole(fs.shape),
            pl.BlockSpec((width, half2), lambda a: (0, a)),
            whole(lf.shape),
            whole(lm.shape),
            whole(lc0.shape),
            whole(lc1.shape),
            whole(p384.shape),
            whole(fsb.shape),
            whole(p256.shape),
        ],
        out_specs=[
            pl.BlockSpec((lr, 2, 4 * cols, outs), lambda a: (0, a, 0, 0)),
            pl.BlockSpec((lr, 1, 2 * cols, outs), lambda a: (0, a, 0, 0)),
            whole((tokens, outs)),
            whole((tokens // 4, outs)),
        ],
        scratch=[
            pltpu.VMEM((2, 4, tokens, outs), BF),
            pltpu.VMEM((2, tokens, outs), BF),
            pltpu.VMEM((tokens, half2 // 2), BF),
            pltpu.VMEM((tokens, half2 // 2), F32),
            pltpu.VMEM((tokens, outs), F32),
            pltpu.VMEM((4 * tokens, fs.shape[0] // 4), BF),
            pltpu.VMEM((4 * tokens, outs), F32),
        ],
        flops=20e9,
        name="pyramid",
    )(y, ff, fs, mu, lf, lm, lc0, lc1, p384, fsb, p256)


def fill_padded(step, block, src_ref, rim_ref, pad_ref, left, right):
    rows, cols, chan = src_ref.shape

    @pl.when(step == 0)
    def _():
        pad_ref[0, :, chan : 2 * chan] = rim_ref[0]
        pad_ref[rows + 1, :, chan : 2 * chan] = rim_ref[1]

        def copy(row, carry):
            pad_ref[row + 1, :, chan : 2 * chan] = src_ref[row]
            return carry

        lax.fori_loop(0, rows, copy, 0)

    def move(at):
        row = pad_ref[at, :, chan : 2 * chan]
        pad_ref[at, :, 0:chan] = mm(left, row).astype(BF)
        pad_ref[at, :, 2 * chan :] = mm(right, row).astype(BF)

    start = step * block
    group = min(block, MOVE_ROWS)

    @pl.when(step == 0)
    def _():
        move(0)
        move(1)

    def move_group(k, carry):
        for q in range(group):
            move(start + 2 + k * group + q)
        return carry

    lax.fori_loop(0, block // group, move_group, 0)


def conv_kernel(level, block, z_ref, rim_ref, w_ref, cot_ref, p_ref, *refs):
    map_ref, dr_ref, dw_ref, sums_ref, pad_ref, dwt_ref, gradt_ref = refs[-7:]
    step = pl.program_id(0)
    rows, cols, chan = z_ref.shape
    fill_padded(
        step, block, z_ref, rim_ref, pad_ref, shift_matrix(cols, -1), shift_matrix(cols, 1)
    )
    gain = p_ref[4 + level : 5 + level, :]
    shift = p_ref[12 + level : 13 + level, :]
    few = min(block, max(1, (CONV_PIXELS if rows * cols > 4096 else CONV_PIXELS // 2) // cols))
    pixels = few * cols

    @pl.when(step == 0)
    def _():
        sums_ref[...] = jnp.zeros_like(sums_ref)
        dwt_ref[...] = jnp.zeros_like(dwt_ref)

    def forward(k, carry):
        sum_gain, sum_shift = carry
        row = step * block + k * few
        result = None
        for a in range(3):
            part = mm(pad_ref[pl.ds(row + a, few)].reshape(pixels, 3 * chan), w_ref[0, a])
            result = part if result is None else result + part
        base = pl.multiple_of(k * pixels, pixels)
        for q in range(0, pixels, 64):
            sl = pl.ds(base + q, 64)
            hat, inverse = stats(result[q : q + 64])
            map_ref[sl, :] = (hat * gain + shift).astype(BF)
            cot = cot_ref[sl, :].astype(F32)
            sum_gain = sum_gain + rowsum(cot * hat)
            sum_shift = sum_shift + rowsum(cot)
            dr_ref[sl, :] = norm_back(cot * gain, hat, inverse).astype(BF)
        gradt_ref[:, pl.ds(base, pixels)] = dr_ref[pl.ds(base, pixels), :].T
        return sum_gain, sum_shift

    zero = jnp.zeros((1, chan), F32)
    sum_gain, sum_shift = lax.fori_loop(0, block // few, forward, (zero, zero))
    sums_ref[0:1, :] += sum_gain
    sums_ref[1:2, :] += sum_shift

    def add_grad(k, carry):
        a, b = lax.div(k, 3), lax.rem(k, 3)
        lanes = pl.ds(pl.multiple_of(b * chan, chan), chan)
        window = pad_ref[pl.ds(step * block + a, block), :, lanes].reshape(block * cols, chan)
        dwt_ref[k] += mm(gradt_ref[...], window)
        return carry

    lax.fori_loop(0, 9, add_grad, 0)

    @pl.when(step == pl.num_programs(0) - 1)
    def _():
        def turn(k, carry):
            dw_ref[pl.ds(pl.multiple_of(k * chan, chan), chan), :] = dwt_ref[k].T.astype(BF)
            return carry

        lax.fori_loop(0, 9, turn, 0)


def conv_call(level, z, rims, weights, cot, p256, block, packed):
    rows, cols, chan = z.shape
    before = [] if packed is None else [packed]
    spec = pl.BlockSpec((block * cols, chan), lambda s: (s, 0))
    return call(
        functools.partial(conv_kernel, level, block),
        [
            sds((rows * cols, chan), BF),
            sds((rows * cols, chan), BF),
            sds((9 * chan, 4 * chan), BF),
            sds((8, chan), F32),
        ],
        grid=(rows // block,),
        in_specs=[
            whole(z.shape),
            whole(rims.shape),
            pl.BlockSpec((1, 3, 3 * chan, chan), lambda s: (level, 0, 0, 0)),
            spec,
            whole(p256.shape),
        ]
        + [pl.BlockSpec(memory_space=pl.ANY)] * len(before),
        out_specs=[
            spec,
            spec,
            pl.BlockSpec((9 * chan, chan), lambda s: (0, level)),
            whole((8, chan)),
        ],
        scratch=[
            pltpu.VMEM((rows + 2, cols, 3 * chan), BF),
            pltpu.VMEM((9, chan, chan), F32),
            pltpu.VMEM((chan, block * cols), BF),
        ],
        flops=5 * 9 * rows * cols * chan * chan,
        name=f"conv{level}",
        aliases={5: 2} if before else {},
    )(z, rims, weights, cot.reshape(rows * cols, chan), p256, *before)


def conv_back_kernel(ways, block, dr_ref, rim_ref, w_ref, dz_ref, pad_ref):
    step = pl.program_id(0)
    rows, cols, chan = dr_ref.shape
    fill_padded(
        step, block, dr_ref, rim_ref, pad_ref, shift_matrix(cols, 1), shift_matrix(cols, -1)
    )
    few = min(block, max(1, BACK_PIXELS // cols))
    pixels = few * cols
    base = cols // ways
    unweave = weave_matrix(cols, ways, inverse=True)

    def back(k, carry):
        row = step * block + k * few
        result = None
        for a in range(3):
            for b in range(3):
                window = pad_ref[pl.ds(row + 2 - a, few), :, b * chan : (b + 1) * chan]
                part = mt(
                    window.reshape(pixels, chan), w_ref[0, a, b * chan : (b + 1) * chan, :]
                )
                result = part if result is None else result + part
        low = result.astype(BF)
        if ways == 1:
            dz_ref[pl.ds(pl.multiple_of(k * pixels, pixels), pixels), :] = low
            return carry
        for q in range(few):
            planes = mm(unweave, low[q * cols : (q + 1) * cols]).astype(BF)
            inner = k * few + q
            at = pl.ds(pl.multiple_of(lax.div(inner, ways) * base, base), base)
            for w in range(ways):
                dz_ref[lax.rem(inner, ways), w, at, :] = planes[w * base : (w + 1) * base]
        return carry

    lax.fori_loop(0, block // few, back, 0)


def conv_back_call(level, dr, rims, weights, ways, block):
    rows, cols, chan = dr.shape
    if ways == 1:
        out = sds((rows * cols, chan), BF)
        spec = pl.BlockSpec((block * cols, chan), lambda s: (s, 0))
    else:
        tokens = rows * cols // (ways * ways)
        out = sds((ways, ways, tokens, chan), BF)
        spec = pl.BlockSpec(
            (ways, ways, block * cols // (ways * ways), chan), lambda s: (0, 0, s, 0)
        )
    return call(
        functools.partial(conv_back_kernel, ways, block),
        out,
        grid=(rows // block,),
        in_specs=[
            whole(dr.shape),
            whole(rims.shape),
            pl.BlockSpec((1, 3, 3 * chan, chan), lambda s: (level, 0, 0, 0)),
        ],
        out_specs=spec,
        scratch=[pltpu.VMEM((rows + 2, cols, 3 * chan), BF)],
        flops=3 * 9 * rows * cols * chan * chan,
        name=f"conv_back{level}",
    )(dr, rims, weights)


def lateral_back(product_ref, count, read, gain, dl_ref):
    zero = jnp.zeros((1, product_ref.shape[1]), F32)

    def chunk(sl, carry):
        hat, inverse = stats(product_ref[sl, :])
        grad = read(sl)
        dl_ref[sl, :] = norm_back(grad * gain, hat, inverse).astype(BF)
        return carry[0] + rowsum(grad * hat), carry[1] + rowsum(grad)

    return by_chunks(count, 64, chunk, (zero, zero))


def pyramid_back_kernel(
    lr, cols, shards, core_ref, y_ref, ff_ref, fs_ref, mu_ref, lf_ref, lm_ref, lc0_ref, lc1_ref, p384_ref,
    fsb_ref, p256_ref, dzf_ref, dzm_ref, dzb_ref, dzc_ref, place_ref,
    dy_ref, keep_ref, send_ref, s384_ref, s192_ref, s256_ref,
    yt_ref, hat_ref, slope_ref, inv_ref, f2_ref, df2_ref, df1_ref, dl_ref, fs_acc, lf_acc, lm_acc,
    dcol_ref, drest_ref, product_ref, pick_ref, third_ref, stack_ref, dls_ref, sem,
):
    step = pl.program_id(0)
    tokens = lr * cols
    quart = fs_ref.shape[0] // 4
    half = ff_ref.shape[1]
    chan = lf_ref.shape[1]

    core = core_ref[0]
    rest = drest_ref.shape[1]

    @pl.when(step == 0)
    def _():
        yt_ref[...] = y_ref[...].T
        for ref in (fs_acc, lf_acc, lm_acc, s384_ref, s192_ref, s256_ref):
            ref[...] = jnp.zeros_like(ref)
        product_ref[...] = mm(y_ref[...], lc0_ref[...])
        sg, ss = lateral_back(
            product_ref, tokens, lambda sl: dzb_ref[sl, :].astype(F32), p256_ref[2:3, :], dl_ref
        )
        s256_ref[2:3, :] = sg
        s256_ref[10:11, :] = ss
        drest_ref[:, half : half + chan] = mm(yt_ref[...], dl_ref[...]).astype(BF)
        dy_ref[...] = mt(dl_ref[...], lc0_ref[...])
        top = pool_picks(y_ref, pick_ref, lr, cols)
        low = top.astype(BF)
        product_ref[0 : tokens // 4, :] = mm(low, lc1_ref[...])
        sg, ss = lateral_back(
            product_ref, tokens // 4, lambda sl: dzc_ref[sl, :].astype(F32), p256_ref[3:4, :], dl_ref
        )
        s256_ref[3:4, :] = sg
        s256_ref[11:12, :] = ss
        grad = dl_ref[0 : tokens // 4, :]
        drest_ref[:, half + chan : half + 2 * chan] = tm(low, grad).astype(BF)
        dtop = mt(grad, lc1_ref[...])
        hits = jnp.zeros_like(top)
        for k in range(4):
            hits = hits + jnp.where(pick_ref[k] == top, 1.0, 0.0)
        dtop = dtop / hits

        def share_out(k, carry):
            share = jnp.where(pick_ref[k] == top, dtop, 0.0)
            upper = share.astype(BF)
            lower = (share - upper.astype(F32)).astype(BF)
            spread = pool_matrix(k // 2, k % 2, lr, cols)
            dy_ref[...] += tm(spread, upper) + tm(spread, lower)
            return carry

        repeat(4, share_out)

    df2_ref[...] = mm(y_ref[...], ff_ref[...])

    def norm(sl, carry):
        hat, inverse = stats(df2_ref[sl, :] + p384_ref[0:1, :])
        hat_ref[sl, :] = hat
        inv_ref[sl, :] = jnp.broadcast_to(inverse, (64, 128))
        value, slope = gelu_pair(hat * p384_ref[1:2, :] + p384_ref[2:3, :])
        f2_ref[sl, :] = value.astype(BF)
        slope_ref[sl, :] = slope
        df2_ref[sl, :] = jnp.zeros_like(hat)

    by_chunks(tokens, 64, norm)

    for k in range(4):
        third_ref[k * tokens : (k + 1) * tokens, :] = (
            mt(f2_ref[...], fs_ref[k * quart : (k + 1) * quart, :]) + fsb_ref[...]
        ).astype(BF)
    stack_ref[...] = mm(third_ref[...], lf_ref[...])
    for k in range(4):
        sg, ss = lateral_back(
            stack_ref.at[k * tokens : (k + 1) * tokens],
            tokens,
            lambda sl: dzf_ref[0, k // 2, 0, k % 2, sl, :].astype(F32),
            p256_ref[0:1, :],
            dls_ref.at[k * tokens : (k + 1) * tokens],
        )
        s256_ref[0:1, :] += sg
        s256_ref[8:9, :] += ss
    lf_acc[...] += tm(third_ref[...], dls_ref[...])
    third_ref[...] = mt(dls_ref[...], lf_ref[...]).astype(BF)
    s192_ref[0:1, :] += rowsum(third_ref[...].astype(F32))
    for k in range(4):
        rows = slice(k * quart, (k + 1) * quart)
        fs_acc[rows, :] += tm(third_ref[k * tokens : (k + 1) * tokens, :], f2_ref[...])
        df2_ref[...] += mm(third_ref[k * tokens : (k + 1) * tokens, :], fs_ref[rows, :])
    zero = jnp.zeros((1, half), F32)

    def first_back(sl, carry):
        sum_gain, sum_shift, sum_bias = carry
        hat = hat_ref[sl, :]
        grad = df2_ref[sl, :] * slope_ref[sl, :]
        low = norm_back(grad * p384_ref[1:2, :], hat, inv_ref[sl, 0:1]).astype(BF)
        df1_ref[sl, :] = low
        return (
            sum_gain + rowsum(grad * hat),
            sum_shift + rowsum(grad),
            sum_bias + rowsum(low.astype(F32)),
        )

    sum_gain, sum_shift, sum_bias = by_chunks(tokens, 64, first_back, (zero, zero, zero))
    s384_ref[0:1, :] += sum_bias
    s384_ref[1:2, :] += sum_gain
    s384_ref[2:3, :] += sum_shift
    dcol_ref[step, :, 0:half] = mm(yt_ref[...], df1_ref[...]).astype(BF)
    dy_ref[...] += mt(df1_ref[...], ff_ref[...])

    f2_ref[...] = (mm(y_ref[...], mu_ref[...]) + p384_ref[3:4, :]).astype(BF)
    product_ref[...] = mm(f2_ref[...], lm_ref[...])
    sg, ss = lateral_back(
        product_ref, tokens, lambda sl: dzm_ref[0, 0, sl, :].astype(F32), p256_ref[1:2, :], dl_ref
    )
    s256_ref[1:2, :] += sg
    s256_ref[9:10, :] += ss
    lm_acc[...] += tm(f2_ref[...], dl_ref[...])
    df1_ref[...] = mt(dl_ref[...], lm_ref[...]).astype(BF)
    s384_ref[3:4, :] += rowsum(df1_ref[...].astype(F32))
    dcol_ref[step, :, half:] = mm(yt_ref[...], df1_ref[...]).astype(BF)
    lanes = pl.ds(pl.multiple_of(step * 2 * half, 2 * half), 2 * half)
    put_shards(dcol_ref.at[step], keep_ref, send_ref, lanes, shards, 0, core, sem.at[step])
    dy_ref[...] += mt(df1_ref[...], mu_ref[...])

    @pl.when(step == pl.num_programs(0) - 1)
    def _():
        drest_ref[:, 0:half] = fs_acc[...].astype(BF)
        laterals = jnp.concatenate([lf_acc[...], lm_acc[...]], axis=0).astype(BF)
        drest_ref[:, half + 2 * chan : half + 3 * chan] = mm(place_ref[...], laterals).astype(BF)
        put_shards(
            drest_ref, keep_ref, send_ref, pl.ds(8 * half, rest), shards, 0, core, sem.at[4]
        )
        for at in range(4):
            wait_shards(dcol_ref.at[at], sem.at[at])
        wait_shards(drest_ref, sem.at[4])


def pyramid_back_call(
    y, lr, cols, ff, fs, mu, lf, lm, lc0, lc1, p384, fsb, p256, dzf, dzm, dzb, dzc, place, core, shards
):
    tokens, width = y.shape
    half = fs.shape[1]
    quart = fsb.shape[1]
    outs = lf.shape[1]
    col_block = pl.BlockSpec((width, half), lambda s: (0, s))
    return call(
        functools.partial(pyramid_back_kernel, lr, cols, shards),
        [
            sds((tokens, width), F32),
            sds((width // 2, 9 * half + 3 * outs), BF),
            sds((width // 2, 9 * half + 3 * outs), BF),
            sds((8, half), F32),
            sds((8, quart), F32),
            sds((16, outs), F32),
        ],
        grid=(4,),
        in_specs=[
            pl.BlockSpec(memory_space=pltpu.SMEM),
            whole(y.shape),
            col_block,
            whole(fs.shape),
            col_block,
            whole(lf.shape),
            whole(lm.shape),
            whole(lc0.shape),
            whole(lc1.shape),
            whole(p384.shape),
            whole(fsb.shape),
            whole(p256.shape),
            pl.BlockSpec((1, 2, 1, 2, tokens, outs), lambda s: (s // 2, 0, s % 2, 0, 0, 0)),
            pl.BlockSpec((1, 1, tokens, outs), lambda s: (s // 2, s % 2, 0, 0)),
            whole(dzb.shape),
            whole(dzc.shape),
            whole(place.shape),
        ],
        out_specs=[
            whole((tokens, width)),
            pl.BlockSpec(memory_space=pl.ANY),
            pl.BlockSpec(memory_space=pl.ANY),
            whole((8, half)),
            whole((8, quart)),
            whole((16, outs)),
        ],
        scratch=[
            pltpu.VMEM((width, tokens), BF),
            pltpu.VMEM((tokens, half), F32),
            pltpu.VMEM((tokens, half), F32),
            pltpu.VMEM((tokens, 128), F32),
            pltpu.VMEM((tokens, half), BF),
            pltpu.VMEM((tokens, half), F32),
            pltpu.VMEM((tokens, half), BF),
            pltpu.VMEM((tokens, outs), BF),
            pltpu.VMEM(fs.shape, F32),
            pltpu.VMEM(lf.shape, F32),
            pltpu.VMEM(lm.shape, F32),
            pltpu.VMEM((4, width, 2 * half), BF),
            pltpu.VMEM((width, half + 3 * outs), BF),
            pltpu.VMEM((tokens, outs), F32),
            pltpu.VMEM((4, tokens // 4, width), F32),
            pltpu.VMEM((4 * tokens, quart), BF),
            pltpu.VMEM((4 * tokens, outs), F32),
            pltpu.VMEM((4 * tokens, outs), BF),
            pltpu.SemaphoreType.DMA((5,)),
        ],
        flops=45e9,
        name="pyramid_back",
    )(
        core, y, ff, fs, mu, lf, lm, lc0, lc1, p384, fsb, p256,
        dzf.reshape(2, 2, 2, 2, tokens, outs), dzm, dzb, dzc, place,
    )


def mlp_back_kernel(
    shards,
    core_ref, dy_ref, g_ref, gp_ref, w1_ref, w2_ref, x1_ref, o_ref, wp_ref, p_ref, s384_ref, s192_ref, s256_ref, levels_ref,
    hot256_ref, hot384_ref, hot192_ref,
    keep_ref, send_ref, keep2_ref, send2_ref, dx1_ref, do_ref,
    n2t_ref, d2_ref, dn2_ref, low_ref, sums_ref, vec_ref, dw1_ref, dw2_ref, rest_ref, temp_ref, sem,
):
    step = pl.program_id(0)
    steps = pl.num_programs(0)
    tokens, width = dy_ref.shape
    unit = width // shards
    hidden = 4 * width

    core = core_ref[0]

    @pl.when(step == 0)
    def _():
        sums_ref[...] = jnp.zeros_like(sums_ref)
        vec_ref[...] = jnp.zeros_like(vec_ref)
        dn2_ref[...] = jnp.zeros_like(dn2_ref)

        def norm(sl, total):
            hat, _ = stats(x1_ref[sl, :])
            low_ref[sl, :] = (hat * p_ref[1:2, :] + p_ref[3:4, :]).astype(BF)
            low = dy_ref[sl, :].astype(BF)
            d2_ref[sl, :] = low
            return total + rowsum(low.astype(F32))

        sums_ref[7:8, :] = by_chunks(tokens, 32, norm, jnp.zeros((1, width), F32))
        n2t_ref[...] = low_ref[...].T

    dw2_ref[step] = tm(g_ref[...], d2_ref[...]).astype(BF)
    put_shards(
        dw2_ref.at[step], keep2_ref, send2_ref, pl.ds(0, width), shards // 4, step * (shards // 4), core,
        sem.at[5 + step],
    )
    temp_ref[...] = mt(d2_ref[...], w2_ref[...])

    def act(sl, carry):
        low_ref[sl, :] = (temp_ref[sl, :] * gp_ref[sl, :].astype(F32)).astype(BF)

    by_chunks(tokens, 32, act)
    db1 = tm(low_ref[...], jnp.ones((tokens, 128), BF))
    lane = lax.broadcasted_iota(jnp.int32, (unit, 128), 1)
    for q in range(shards // 4):
        entry = jnp.zeros((unit, 128), F32)
        for k in range(4):
            sl = slice((4 * q + k) * unit, (4 * q + k + 1) * unit)
            entry = jnp.where(lane == 40 + k, db1[sl], entry)
        vec_ref[pl.ds(pl.multiple_of(step * (width // 4) + q * unit, 8), unit), :] += entry
    dw1_ref[step] = mm(n2t_ref[...], low_ref[...]).astype(BF)
    lanes = pl.ds(pl.multiple_of(step * width, width), width)
    put_shards(dw1_ref.at[step], keep_ref, send_ref, lanes, shards, 0, core, sem.at[step])
    dn2_ref[...] += mt(low_ref[...], w1_ref[...])

    @pl.when(step == steps - 1)
    def _():
        zero = jnp.zeros((1, width), F32)

        def back(sl, carry):
            hat, inverse = stats(x1_ref[sl, :])
            grad = dn2_ref[sl, :]
            dx1 = dy_ref[sl, :] + norm_back(grad * p_ref[1:2, :], hat, inverse)
            dx1_ref[sl, :] = dx1
            low = dx1.astype(BF)
            d2_ref[sl, :] = low
            return (
                carry[0] + rowsum(grad * hat),
                carry[1] + rowsum(grad),
                carry[2] + rowsum(low.astype(F32)),
            )

        sum_gain, sum_shift, sum_bias = by_chunks(tokens, 32, back, (zero, zero, zero))
        sums_ref[1:2, :] = sum_gain
        sums_ref[3:4, :] = sum_shift
        sums_ref[6:7, :] = sum_bias
        rest_ref[:, 0:width] = tm(o_ref[...], d2_ref[...]).astype(BF)
        do_ref[...] = mt(d2_ref[...], wp_ref[...]).astype(BF)

        def lanes_of(rows, before):
            after = 128 - before - rows.shape[0]
            parts = [jnp.zeros((before, rows.shape[1]), F32)] if before else []
            parts += [rows, jnp.zeros((after, rows.shape[1]), F32)]
            return jnp.concatenate(parts, axis=0)

        spread = mt(hot256_ref[...], lanes_of(s256_ref[...], 8).astype(BF))
        spread = spread + mt(hot256_ref[...], lanes_of(levels_ref[...], 24).astype(BF))
        spread = spread + mt(hot384_ref[...], lanes_of(s384_ref[...], 32).astype(BF))
        spread = spread + mt(hot192_ref[...], lanes_of(s192_ref[...], 48).astype(BF))
        spread = spread + lanes_of(sums_ref[...], 0).T
        rest_ref[:, width:] = (vec_ref[...] + spread).astype(BF)
        put_shards(
            rest_ref, keep_ref, send_ref, pl.ds(hidden, width + 128), shards, 0, core, sem.at[4]
        )
        for at in range(4):
            wait_shards(dw1_ref.at[at], sem.at[at])
            wait_shards(dw2_ref.at[at], sem.at[5 + at])
        wait_shards(rest_ref, sem.at[4])


def mlp_back_call(
    dy, g, gp, w1, w2, x1, attended, wp, p768, s384, s192, s256, levels, hots, core, shards
):
    rows, width = dy.shape
    hidden = g.shape[1]
    full = whole((rows, width))
    column = pl.BlockSpec((rows, width), lambda s: (0, s))
    smalls = [p768, s384, s192, s256, levels, *hots]
    return call(
        functools.partial(mlp_back_kernel, shards),
        [
            sds((width // 2, hidden + width + 128), BF),
            sds((width // 2, hidden + width + 128), BF),
            sds((hidden // 2, width), BF),
            sds((hidden // 2, width), BF),
            sds((rows, width), F32),
            sds((rows, width), BF),
        ],
        grid=(hidden // width,),
        in_specs=[
            pl.BlockSpec(memory_space=pltpu.SMEM),
            full,
            column,
            column,
            pl.BlockSpec((width, width), lambda s: (0, s)),
            pl.BlockSpec((width, width), lambda s: (s, 0)),
            full,
            full,
            whole((width, width)),
        ]
        + [whole(a.shape) for a in smalls],
        out_specs=[
            pl.BlockSpec(memory_space=pl.ANY),
            pl.BlockSpec(memory_space=pl.ANY),
            pl.BlockSpec(memory_space=pl.ANY),
            pl.BlockSpec(memory_space=pl.ANY),
            full,
            full,
        ],
        scratch=[
            pltpu.VMEM((width, rows), BF),
            pltpu.VMEM((rows, width), BF),
            pltpu.VMEM((rows, width), F32),
            pltpu.VMEM((rows, width), BF),
            pltpu.VMEM((8, width), F32),
            pltpu.VMEM((width, 128), F32),
            pltpu.VMEM((4, width, width), BF),
            pltpu.VMEM((4, width, width), BF),
            pltpu.VMEM((width, width + 128), BF),
            pltpu.VMEM((rows, width), F32),
            pltpu.SemaphoreType.DMA((9,)),
        ],
        flops=25e9,
        name="mlp_back",
    )(core, dy, g, gp, w1, w2, x1, attended, wp, *smalls)


def roll_back(values, amount):
    moved = jnp.concatenate(
        [
            pltpu.roll(values[8 * g : 8 * g + 8], (amount - 7 - 8 * g) % 128, 1)
            for g in range(values.shape[0] // 8)
        ],
        axis=0,
    )
    left = 7 - lax.rem(lax.broadcasted_iota(jnp.int32, values.shape, 0), 8)
    for step in (1, 2, 4):
        moved = jnp.where((left & step) > 0, pltpu.roll(moved, step, 1), moved)
    return moved


def attend_back_kernel(total_rows, scale, others, *refs):
    first_ref, q_ref, qaug_ref, do_ref, o_ref, lse_ref, tab_ref, oh1_ref, oh2_ref, before_ref = refs[:10]
    k_refs = refs[10 : 10 + others]
    v_refs = refs[10 + others : 10 + 2 * others]
    rest = refs[-15:]
    (
        dqkv_ref, dtab_ref, kaug_ref, v_ref, p_ref, ds_ref, dqt_ref, df_ref, qm_ref, dom_ref, delta_ref,
        scores_ref, dweight_ref, dk_acc, dv_acc,
    ) = rest
    first_row = first_ref[0]
    tokens = q_ref.shape[0]
    keys = kaug_ref.shape[0]

    @pl.when(pl.program_id(0) == 0)
    def _():
        kaug_ref[:, 128:] = oh2_ref[...]
        dtab_ref[...] = before_ref[...]

    at = 0
    for ref in v_refs:
        v_ref[at : at + ref.shape[0], :] = ref[...]
        at += ref.shape[0]
    lane_all = lax.broadcasted_iota(jnp.int32, (tokens, 128), 1)
    lane = lax.broadcasted_iota(jnp.int32, (64, 128), 1)
    qf = q_ref[...].astype(F32)
    dof = do_ref[...].astype(F32)
    delta_t = (dof * o_ref[...].astype(F32)).T
    dk_acc[...] = jnp.zeros_like(dk_acc)
    dv_acc[...] = jnp.zeros_like(dv_acc)
    dq = None
    for odd in (0, 1):
        mine_all = (lane_all >= 64) if odd else (lane_all < 64)
        other = (lane < 64) if odd else (lane >= 64)
        build_kaug(kaug_ref, k_refs, oh1_ref, oh2_ref, odd)
        qm = jnp.where(mine_all, qf, 0.0).astype(BF)
        dom = jnp.where(mine_all, dof, 0.0).astype(BF)
        delta = rowsum(delta_t[64 * odd : 64 * odd + 64])
        qm_ref[...] = qm
        dom_ref[...] = dom
        delta_ref[...] = delta

        def queries(t, carry):
            sl = pl.ds(pl.multiple_of(t * 256, 256), 256)
            scores_ref[...] = mt(kaug_ref[...], qaug_ref[odd, sl, :])
            dweight_ref[...] = mt(v_ref[...], dom_ref[sl, :])
            lse = lse_ref[0, odd : odd + 1, sl]
            shift = delta_ref[:, sl]

            def weigh(rows, inner):
                weight = jnp.exp(scores_ref[rows, :] - lse)
                p_ref[rows, :] = weight.astype(BF)
                ds_ref[rows, :] = (weight * (dweight_ref[rows, :] - shift)).astype(BF)

            by_chunks(keys, 128, weigh)
            dk_acc[...] += mm(ds_ref[...], qm_ref[sl, :])
            dv_acc[...] += mm(p_ref[...], dom_ref[sl, :])
            dqt_ref[:, sl] = tm(kaug_ref[...], ds_ref[...])
            return carry

        repeat(tokens // 256, queries)
        dqa = dqt_ref[0:256, :].T
        for i in range(tokens // 64):
            sl = slice(64 * i, 64 * i + 64)
            cols = roll_back(jnp.where(other, dqa[sl, 0:128], 0.0), 63 if odd else 127)
            shift = lax.rem(63 + total_rows - (first_row + i) + 128, 128)
            rows = pltpu.roll(
                jnp.where((lane >= 64) & (lane < 64 + total_rows), dqa[sl, 128:256], 0.0), shift, 1
            )
            df_ref[sl, 0:128] = cols.astype(BF)
            df_ref[sl, 128:256] = rows.astype(BF)
        from_tables = mt(df_ref[...], tab_ref[...])
        part = jnp.where(mine_all, dqa[:, 0:128] * scale + from_tables, 0.0)
        dq = part if dq is None else dq + part
        dtab_ref[...] += tm(qm, df_ref[...])
    dqkv_ref[0, 0:tokens, :] = dq.astype(BF)
    dqkv_ref[1] = (dk_acc[...] * scale).astype(BF)
    dqkv_ref[2] = dv_acc[...].astype(BF)


def attend_back_call(
    first, qkv_own, kv_others, qaug, dout, attended, lse, tab, oh1, oh2, dtab, total_rows, heads, part, parts, grads
):
    tokens = qkv_own.shape[0]
    width = qkv_own.shape[1] // 3
    keys = oh1.shape[0]
    aug = 128 + oh2.shape[1]
    pairs = width // 128
    count = pairs // parts
    base = part * count
    sources = 1 + (1 if kv_others is not None else 0)
    own = pl.BlockSpec((tokens, 128), lambda h: (0, h + base))
    in_specs = [
        pl.BlockSpec(memory_space=pltpu.SMEM),
        own,
        pl.BlockSpec((2, tokens, aug), lambda h: (h + base, 0, 0)),
        own,
        own,
        pl.BlockSpec((1, 2, tokens), lambda h: (h + base, 0, 0)),
        whole(tab.shape),
        whole(oh1.shape),
        whole(oh2.shape),
        whole(dtab.shape),
    ]
    k_args, v_args, k_specs, v_specs = [qkv_own], [qkv_own], [], []
    k_specs.append(pl.BlockSpec((tokens, 128), lambda h: (0, h + base + pairs)))
    v_specs.append(pl.BlockSpec((tokens, 128), lambda h: (0, h + base + 2 * pairs)))
    if kv_others is not None:
        k_args.append(kv_others)
        v_args.append(kv_others)
        k_specs.append(pl.BlockSpec((keys - tokens, 128), lambda h: (0, h + base)))
        v_specs.append(pl.BlockSpec((keys - tokens, 128), lambda h: (0, h + base + pairs)))
    scale = (width // heads) ** -0.5
    earlier = [] if grads is None else [grads]
    return call(
        functools.partial(attend_back_kernel, total_rows, scale, sources),
        [sds((3, keys, width), BF), sds((128, 256), F32)],
        grid=(count,),
        in_specs=in_specs + k_specs + v_specs + [pl.BlockSpec(memory_space=pl.ANY)] * len(earlier),
        out_specs=[pl.BlockSpec((3, keys, 128), lambda h: (0, 0, h + base)), whole((128, 256))],
        scratch=[
            pltpu.VMEM((keys, aug), BF),
            pltpu.VMEM((keys, 128), BF),
            pltpu.VMEM((keys, 256), BF),
            pltpu.VMEM((keys, 256), BF),
            pltpu.VMEM((aug, tokens), F32),
            pltpu.VMEM((tokens, 256), BF),
            pltpu.VMEM((tokens, 128), BF),
            pltpu.VMEM((tokens, 128), BF),
            pltpu.VMEM((1, tokens), F32),
            pltpu.VMEM((keys, 256), F32),
            pltpu.VMEM((keys, 256), F32),
            pltpu.VMEM((keys, 128), F32),
            pltpu.VMEM((keys, 128), F32),
        ],
        flops=30e9 / parts,
        name="attend_back",
        aliases={10 + 2 * sources: 0} if earlier else {},
    )(first, qkv_own, qaug, dout, attended, lse, tab, oh1, oh2, dtab, *k_args, *v_args, *earlier)


def qkv_back_kernel(
    x_ref, dqkv_ref, w_ref, dx1_ref, p_ref, dtab_ref, hot_ref,
    pack_ref, dx_ref, far_ref, nt_ref, low_ref, dn_ref, sums_ref, dw_ref, out_ref, extra_ref, sem,
):
    step = pl.program_id(0)
    tokens, width = x_ref.shape

    def w_copy(at):
        return pltpu.make_async_copy(
            out_ref.at[at], pack_ref.at[:, pl.ds(at * width, width)], sem.at[at]
        )

    extra_copy = pltpu.make_async_copy(extra_ref, pack_ref.at[:, pl.ds(3 * width, 384)], sem.at[3])

    def norm_chunk(sl, carry):
        hat, _ = stats(x_ref[sl, :].astype(F32))
        low_ref[sl, :] = (hat * p_ref[0:1, :] + p_ref[2:3, :]).astype(BF)

    by_chunks(tokens, 32, norm_chunk)
    nt_ref[...] = low_ref[...].T

    @pl.when(step == 0)
    def _():
        sums_ref[...] = jnp.zeros_like(sums_ref)
        sums_ref[4:5, :] = rowsum(dqkv_ref[0].astype(F32))
        both = dtab_ref[...]
        tables = (both[0:64] + both[64:128]).astype(BF)
        extra_ref[:, 128:384] = mm(hot_ref[...], tables).astype(BF)
        dw_ref[...] = jnp.zeros_like(dw_ref)

    dn_ref[...] = jnp.zeros_like(dn_ref)

    def product(at, carry):
        lanes = pl.ds(pl.multiple_of(at * width, width), width)
        dw_ref[at] += mm(nt_ref[...], dqkv_ref[at])
        dn_ref[...] += mt(dqkv_ref[at], w_ref[:, lanes])
        return carry

    lax.fori_loop(jnp.where(step == 0, 0, 1), 3, product, 0)
    sums_ref[5:6, :] += rowsum(dqkv_ref[2].astype(F32))

    def back_chunk(sl, carry):
        sum_gain, sum_shift = carry
        hat, inverse = stats(x_ref[sl, :].astype(F32))
        grad = dn_ref[sl, :]
        dn_ref[sl, :] = norm_back(grad * p_ref[0:1, :], hat, inverse)
        return sum_gain + rowsum(grad * hat), sum_shift + rowsum(grad)

    zero = jnp.zeros((1, width), F32)
    sum_gain, sum_shift = by_chunks(tokens, 32, back_chunk, (zero, zero))
    sums_ref[0:1, :] += sum_gain
    sums_ref[2:3, :] += sum_shift

    @pl.when(step == 0)
    def _():
        dx_ref[...] = dx1_ref[...] + dn_ref[...]

    far_ref[...] = dn_ref[...].astype(BF)

    @pl.when(step == pl.num_programs(0) - 1)
    def _():
        def put(at, carry):
            out_ref[at] = dw_ref[at].astype(BF)
            w_copy(at).start()
            return carry

        lax.fori_loop(0, 3, put, 0)
        padded = jnp.concatenate([sums_ref[...], jnp.zeros((120, width), F32)], axis=0)
        extra_ref[:, 0:128] = padded.T.astype(BF)
        extra_copy.start()
        for at in range(3):
            w_copy(at).wait()
        extra_copy.wait()


def qkv_back_call(tokens, dqkv, weight, dx1, p768, dtab, hot):
    rows, width = dx1.shape
    blocks = tokens.shape[0] // rows
    full = whole((rows, width))
    block = pl.BlockSpec((rows, width), lambda s: (s, 0))
    return call(
        qkv_back_kernel,
        [
            sds((width, 3 * width + 384), BF),
            sds((rows, width), F32),
            sds(((max(blocks, 2) - 1) * rows, width), BF),
        ],
        grid=(blocks,),
        in_specs=[
            block,
            pl.BlockSpec((3, rows, width), lambda s: (0, s, 0)),
            whole(weight.shape),
            full,
            whole(p768.shape),
            whole(dtab.shape),
            whole(hot.shape),
        ],
        out_specs=[
            pl.BlockSpec(memory_space=pl.ANY),
            full,
            pl.BlockSpec((rows, width), lambda s: (jnp.maximum(s - 1, 0), 0)),
        ],
        scratch=[
            pltpu.VMEM((width, rows), BF),
            pltpu.VMEM((rows, width), BF),
            pltpu.VMEM((rows, width), F32),
            pltpu.VMEM((8, width), F32),
            pltpu.VMEM((3, width, width), F32),
            pltpu.VMEM((3, width, width), BF),
            pltpu.VMEM((width, 384), BF),
            pltpu.SemaphoreType.DMA((4,)),
        ],
        flops=8e9,
        name="qkv_back",
    )(tokens, dqkv, weight, dx1, p768, dtab, hot)


def rim_exchange(levels, axis):
    peers = lax.axis_size(axis)
    chan = levels[0].shape[-1]
    counts = [level.shape[1] for level in levels]
    lasts = jnp.concatenate([level[-1] for level in levels], axis=0)
    firsts = jnp.concatenate([level[0] for level in levels], axis=0)
    if peers == 2:
        me = lax.axis_index(axis)
        got = lax.ppermute(jnp.where(me == 0, lasts, firsts), axis, [(0, 1), (1, 0)])
        nothing = jnp.zeros_like(got)
        before = jnp.where(me == 1, got, nothing)
        after = jnp.where(me == 0, got, nothing)
    else:
        before = lax.ppermute(lasts, axis, [(i, i + 1) for i in range(peers - 1)])
        after = lax.ppermute(firsts, axis, [(i + 1, i) for i in range(peers - 1)])
    both = jnp.stack([before, after])
    rims, at = [], 0
    for count in counts:
        rims.append(both[:, at : at + count])
        at += count
    return rims


class Halving:
    def __init__(self, keep, send):
        bits = lax.axis_size("img").bit_length() - 1
        self.left = list(range(1, bits))[::-1]
        self.shape = (2,) * (bits - 1) + (keep.shape[0] >> (bits - 1), keep.shape[1])
        self.keep, self.first = keep.reshape(self.shape), send.reshape(self.shape)

    def lanes(self):
        first, second = Halving.__new__(Halving), Halving.__new__(Halving)
        middle = self.shape[-1] // 256 * 128
        for part, cut in ((first, slice(0, middle)), (second, slice(middle, None))):
            part.left = list(self.left)
            part.terms = [term[..., cut] for term in self.terms]
        return first, second

    def split(self, step):
        if step == 0:
            self.route = ("img", [(i, i ^ 1) for i in range(lax.axis_size("img"))])
            return self.first
        terms = self.terms
        if step == "y":
            at, mine, axis, pairs = len(self.left), lax.axis_index("seq"), "seq", [(0, 1), (1, 0)]
            shape = terms[0].shape
            terms = [t.reshape(shape[:-2] + (2, shape[-2] // 2, shape[-1])) for t in terms]
        else:
            at, mine, axis = self.left.index(step), (lax.axis_index("img") >> step) & 1, "img"
            pairs = [(i, i ^ (1 << step)) for i in range(lax.axis_size("img"))]
            self.left.remove(step)
        self.route = (axis, pairs)

        def half(which):
            parts = [lax.dynamic_index_in_dim(t, which, at, keepdims=False) for t in terms]
            return (parts[0].astype(F32) + parts[1].astype(F32)).astype(BF)

        self.keep = half(mine)
        return half(1 - mine)


def swap(steps, after=()):
    if lax.axis_size("seq") != 2:
        steps = [(h, step) for h, step in steps if step != "y"]
    sends = [h.split(step) for h, step in steps]
    keeps = [h.keep for h, _ in steps]
    sends, keeps, after = lax.optimization_barrier((sends, keeps, after))
    for (h, _), send, keep in zip(steps, sends, keeps):
        h.terms = [keep, lax.ppermute(flat(send), *h.route).reshape(send.shape)]
    return [h for h, _ in steps], after


def flat(values):
    return values.reshape(-1, values.shape[-1])


def last_swap(group):
    left = group[0].left
    count = 1 << len(left)
    base = left[-1]
    mine = (lax.axis_index("img") >> base) & (count - 1)
    shards = lax.axis_size("img")
    terms = [
        jnp.concatenate(
            [h.terms[k].reshape((count,) + h.terms[k].shape[len(left) :]) for h in group], axis=-1
        )
        for k in (0, 1)
    ]

    def part(which):
        parts = [lax.dynamic_index_in_dim(t, which, 0, keepdims=False) for t in terms]
        return (parts[0].astype(F32) + parts[1].astype(F32)).astype(BF)

    total = part(mine).astype(F32)
    for d in range(1, count):
        pairs = [(i, i ^ (d << base)) for i in range(shards)]
        total = total + lax.ppermute(part(mine ^ d), "img", pairs).astype(F32)
    grad = total.astype(BF)
    if lax.axis_size("seq") != 2:
        return lax.psum(grad, "seq").astype(F32)
    row = lax.axis_index("seq")
    other = lax.ppermute(grad, "seq", [(0, 1), (1, 0)])
    first = jnp.where(row == 0, grad, other)
    second = jnp.where(row == 0, other, grad)
    return jnp.concatenate([first, second], axis=0).astype(F32)


def settle(moving, done=()):
    terms, _ = lax.optimization_barrier(([h.terms for h in moving], done))
    for h, arrived in zip(moving, terms):
        h.terms = arrived


def seq_total(part):
    peers = lax.axis_size("seq")
    if peers == 2:
        other = lax.ppermute(part, "seq", [(0, 1), (1, 0)])
        return part.astype(F32) + other.astype(F32)
    return lax.psum(part, "seq").astype(F32)


def per_device(
    tokens, valid_rows, valid_cols, block_gains, block_shifts, qkv_weight, qv_bias, table_rows, table_cols,
    proj_weight, proj_bias, fc1_weight, fc1_bias, fc2_weight, fc2_bias, fine_first, fine_first_bias,
    fine_norm_gain, fine_norm_shift, fine_second, fine_second_bias, middle_up, middle_up_bias, lateral_fine,
    lateral_middle, lateral_coarse, level_gains, level_shifts, output_convs, cotan_fine, cotan_middle,
    cotan_base, cotan_coarse,
):
    lr, cols, width = tokens.shape[1:]
    head = table_rows.shape[0]
    heads = width // head
    peers = lax.axis_size("seq")
    shards = lax.axis_size("img")
    me = lax.axis_index("seq")
    total_rows = lr * peers
    count = lr * cols
    chan = lateral_fine.shape[1]
    first_row = me * lr
    first = first_row.astype(jnp.int32).reshape(1)
    own_tokens = tokens[0].reshape(count, width)

    far = [
        lax.ppermute(own_tokens, "seq", [(i, (i + d) % peers) for i in range(peers)])
        for d in range(1, peers)
    ]
    far_tokens = jnp.concatenate(far, axis=0) if len(far) > 1 else (far[0] if far else None)
    all_tokens = jnp.concatenate([own_tokens] + far, axis=0)

    p768 = jnp.stack(
        [
            block_gains[:, 0], block_gains[:, 1], block_shifts[:, 0], block_shifts[:, 1],
            qv_bias[:, 0], qv_bias[:, 1], proj_bias, fc2_bias,
        ]
    ).astype(F32)
    bias3 = jnp.stack([qv_bias[:, 0], jnp.zeros_like(proj_bias), qv_bias[:, 1]]).astype(F32)[:, None, :]
    qkv_own = qkv_call(own_tokens, qkv_weight, bias3, p768, 0)
    (
        fc1_bias, fine_first_bias, fine_norm_gain, fine_norm_shift, middle_up_bias, fine_second_bias, level_gains,
        level_shifts, table_cols, table_rows, valid_rows, qkv_own,
    ) = lax.optimization_barrier(
        (
            fc1_bias, fine_first_bias, fine_norm_gain, fine_norm_shift, middle_up_bias, fine_second_bias,
            level_gains, level_shifts, table_cols, table_rows, valid_rows, qkv_own,
        )
    )
    b1 = fc1_bias.astype(F32)[None]
    p384 = jnp.stack([fine_first_bias, fine_norm_gain, fine_norm_shift, middle_up_bias]).astype(F32)
    fsb = fine_second_bias.astype(F32)[None]
    p256 = jnp.concatenate([level_gains.T, level_shifts.T]).astype(F32)
    lc0, lc1 = lateral_coarse[:, 0, :], lateral_coarse[:, 1, :]

    def turned(table):
        back = table[:, ::-1]
        back = jnp.pad(back, ((0, 0), (0, 128 - back.shape[1])))
        return jnp.concatenate([back, back], axis=0)

    tw, tr = turned(table_cols), turned(table_rows)

    low_at, aug = aug_layout(total_rows)
    ranks = jnp.stack([(me - d) % peers for d in range(peers)])
    key_rows = (ranks[:, None] * lr + jnp.arange(lr)[None, :])[:, :, None]
    key_rows = jnp.broadcast_to(key_rows, (peers, lr, cols)).reshape(-1, 1)
    key_cols = jnp.broadcast_to(jnp.arange(cols)[None, None, :], (peers, lr, cols)).reshape(-1, 1)
    lane = jnp.arange(128)[None, :]
    oh1 = (lane % 64 == key_cols).astype(BF)
    lane = jnp.arange(aug - 128)[None, :]
    hot = (lane < 64) & (lane == key_cols)
    hot = hot | ((lane >= 64) & (lane < 64 + total_rows) & (lane - 64 == key_rows))
    off = low_at
    hot = hot | ((lane >= off) & (lane < off + total_rows) & (lane - off == key_rows))
    bad = (key_rows >= valid_rows[0]) | (key_cols >= valid_cols[0])
    oh2 = jnp.where(bad & (lane == off + total_rows), NEG, hot.astype(F32)).astype(BF)

    kv_far = qkv_call(far_tokens, qkv_weight, bias3, p768, 1) if far else None
    attended, qaug, lse = attend_call(
        first, qkv_own, kv_far, (tw, tr), oh1, oh2, total_rows, heads
    )
    x1, hidden, slope, y = mlp_call(own_tokens, attended, proj_weight, fc1_weight, b1, fc2_weight, p768)

    zf, zm, zb, zc = pyramid_call(
        y, lr, cols, fine_first, fine_second, middle_up, lateral_fine, lateral_middle, lc0, lc1, p384, fsb, p256
    )
    levels = [
        zf.reshape(4 * lr, 4 * cols, chan),
        zm.reshape(2 * lr, 2 * cols, chan),
        zb.reshape(lr, cols, chan),
        zc.reshape(lr // 2, cols // 2, chan),
    ]
    later, _ = lax.optimization_barrier((output_convs, zc))
    conv_weights = later.transpose(1, 0, 2).reshape(4, 3, 3 * chan, chan)
    rims = rim_exchange(levels, "seq")
    cots = [c[0] for c in (cotan_fine, cotan_middle, cotan_base, cotan_coarse)]
    maps, drs, level_sums = [None] * 4, [None] * 4, [None] * 4
    packed = None
    for level in (3, 2, 1, 0):
        z = levels[level]
        block = min(z.shape[0], max(1, 2048 // z.shape[1]))
        map_low, dr, packed, level_sums[level] = conv_call(
            level, z, rims[level], conv_weights, cots[level], p256, block, packed
        )
        maps[level], drs[level] = map_low.reshape(z.shape), dr.reshape(z.shape)

    conv_low = lax.psum_scatter(packed, "img", scatter_dimension=0, tiled=True)
    drims = rim_exchange(drs, "seq")
    dzs = []
    for level, ways in enumerate((4, 2, 1, 1)):
        dr = drs[level]
        block = min(dr.shape[0], max(1, 2048 // dr.shape[1]))
        dzs.append(conv_back_call(level, dr, drims[level], conv_weights, ways, block))

    unit = width // shards
    packed_row, _ = lax.optimization_barrier((jnp.arange(width)[:, None], level_sums[0]))
    shard_at, within = packed_row // unit, packed_row % unit

    def placed(size):
        own = size // shards
        at = jnp.arange(size)[None, :]
        return ((within < own) & (at == shard_at * own + within)).astype(BF)

    quart, half = lateral_fine.shape[0], lateral_middle.shape[0]
    own_q, own_h = quart // shards, half // shards
    at = jnp.arange(quart + half)[None, :]
    source = jnp.where(
        within < own_q,
        shard_at * own_q + within,
        jnp.where(within < own_q + own_h, quart + shard_at * own_h + within - own_q, -1),
    )
    place = (at == source).astype(BF)
    hots = (placed(chan), placed(half), placed(quart))
    core = (lax.axis_index("img") & 1).astype(jnp.int32).reshape(1)
    dy, low_keep, low_send, s384, s192, s256 = pyramid_back_call(
        y, lr, cols, fine_first, fine_second, middle_up, lateral_fine, lateral_middle, lc0, lc1, p384, fsb, p256,
        *dzs, place, core, shards,
    )
    pyramid_sum = Halving(low_keep, low_send)
    moving, dy = swap([(pyramid_sum, 0)], dy)

    level_rows = jnp.concatenate(
        [level_sums[k][0:1] for k in range(4)] + [level_sums[k][1:2] for k in range(4)]
    )
    high_keep, high_send, keep2, send2, dx1, dout = mlp_back_call(
        dy, hidden, slope, fc1_weight, fc2_weight, x1, attended, proj_weight, p768,
        s384, s192, s256, level_rows, hots, core, shards,
    )
    settle(moving, dout)
    one, two = pyramid_sum.lanes()
    three, four = Halving(high_keep, high_send), Halving(keep2, send2)
    tables = jnp.concatenate([tw, tr], axis=1)

    def attend_part(dout_now, dtab, part, grads):
        return attend_back_call(
            first, qkv_own, kv_far, qaug, dout_now, attended, lse, tables, oh1, oh2, dtab,
            total_rows, heads, part, 2, grads,
        )

    _, (dout, conv_low) = swap([(one, 1), (two, "y"), (three, 0), (four, 0)], (dout, conv_low))
    dqkv, dtab = attend_part(dout, jnp.zeros((128, 256), F32), 0, None)
    settle([three, four], dtab)
    _, dtab = swap([(three, 1), (four, "y")], dtab)
    dqkv, dtab = attend_part(dout, dtab, 1, dqkv)
    settle([one, two], dtab)
    _, dtab = swap([(one, "y"), (two, 1)], dtab)
    last, dx, dx_far = qkv_back_call(
        all_tokens, dqkv, qkv_weight, dx1, p768, dtab, placed(head)
    )
    last_low = lax.psum_scatter(last, "img", scatter_dimension=0, tiled=True)
    for d in range(1, peers):
        part = dx_far[(d - 1) * count : d * count]
        dx = dx + lax.ppermute(part, "seq", [(i, (i - d) % peers) for i in range(peers)])
    conv_low, _ = lax.optimization_barrier((conv_low, last))
    conv_total = seq_total(conv_low)
    settle([one, two, three, four], last)
    swap([(three, "y"), (four, 1)])
    settle([three, four])
    low_total, high_total = last_swap([one, two]), last_swap([three])
    g_w2 = last_swap([four])
    last_low, low_total, high_total, g_w2 = lax.optimization_barrier(
        (last_low, low_total, high_total, g_w2)
    )
    last_total = seq_total(last_low)

    def taken(total, start, size):
        return total[:, start : start + size]

    g_ff = jnp.concatenate([taken(low_total, 2 * k * half, half) for k in range(4)], axis=1)
    g_mu = jnp.concatenate([taken(low_total, (2 * k + 1) * half, half) for k in range(4)], axis=1)
    g_fs = taken(low_total, 8 * half, half)
    g_lc = jnp.stack(
        [taken(low_total, 9 * half, chan), taken(low_total, 9 * half + chan, chan)], axis=1
    )
    laterals = taken(low_total, 9 * half + 2 * chan, chan)
    g_lf, g_lm = laterals[:own_q], laterals[own_q : own_q + own_h]
    g_w1 = taken(high_total, 0, 4 * width)
    g_wp = taken(high_total, 4 * width, width)
    vec = taken(high_total, 5 * width, 128)
    own_c = chan // shards
    g_lg = jnp.concatenate([vec[:own_c, 8:12], vec[:own_c, 24:28]], axis=1)
    g_ls = jnp.concatenate([vec[:own_c, 16:20], vec[:own_c, 28:32]], axis=1)
    g_ffb, g_fng, g_fns, g_mub = (vec[:own_h, 32 + k] for k in range(4))
    g_fsb = vec[:own_q, 48]
    g_b1 = vec[:, 40:44].T.reshape(-1)
    g_pb, g_b2 = vec[:, 6], vec[:, 7]
    g_qkv = last_total[:, : 3 * width]
    late = last_total[:, 3 * width : 3 * width + 128]
    g_bg = jnp.stack([late[:, 0], vec[:, 1]], axis=1)
    g_bs = jnp.stack([late[:, 2], vec[:, 3]], axis=1)
    g_qvb = late[:, 4:6]
    own_t = head // shards
    tabs = last_total[:own_t, 3 * width + 128 :]
    g_tc = tabs[:, : 2 * cols - 1][:, ::-1]
    g_tr = tabs[:, 128 : 128 + 2 * total_rows - 1][:, ::-1]
    g_conv = conv_total.reshape(-1, 4, chan)
    return (
        maps[0][None], maps[1][None], maps[2][None], maps[3][None],
        dx.reshape(1, lr, cols, width),
        g_bg, g_bs, g_qkv, g_qvb, g_tr, g_tc, g_wp, g_pb, g_w1, g_b1, g_w2, g_b2, g_ff, g_ffb, g_fng, g_fns,
        g_fs, g_fsb, g_mu, g_mub, g_lf, g_lm, g_lc, g_lg, g_ls, g_conv,
    )


def solution(mesh):
    image = P("img", "seq", None, None)
    in_specs = (image, P("img"), P("img")) + (P(),) * 26 + (image,) * 4
    ranks = (2, 2, 2, 2, 2, 2, 2, 1, 2, 1, 2, 1, 2, 1, 1, 1, 2, 1, 2, 1, 2, 2, 3, 2, 2, 3)
    out_specs = (image,) * 5 + tuple(P(*(("img",) + (None,) * (r - 1))) for r in ranks)
    return jax.shard_map(
        per_device, mesh=mesh, in_specs=in_specs, out_specs=out_specs, check_vma=False
    )
```

time: 725 us -> 524 us (0.72)
  waiting for transfers between devices: 289 us -> 67.1 us
  Pallas kernels: 331 us -> 296 us
  starting transfers between devices: 10.1 us -> 44.2 us
  other arithmetic: 24.8 us -> 47.9 us
    reduce_scatter x1 -> x0, waiting for transfers between devices: 104 us -> none  [per_device(): wide_low = lax.psum_scatter(wide, 'img', scatter_dimension=0, tiled=True)]
    reduce_scatter x1, waiting for transfers between devices: 75.7 us -> 0.01 us  [per_device(): conv_low = lax.psum_scatter(packed, 'img', scatter_dimension=0, tiled=True)]
    reduce_scatter x1, waiting for transfers between devices: 60.5 us -> 0.02 us  [per_device(): last_low = lax.psum_scatter(last, 'img', scatter_dimension=0, tiled=True)]
    ppermute x3 -> x25, starting transfers between devices: 5.12 us -> 41.3 us  [the longest x9 23.3 us: last_swap(): total = total + lax.ppermute(part(mine ^ d), 'img', pairs).astype(F32)]
    pallas_call x7 -> x8, Pallas kernels: 206 us -> 174 us  [the longest x4 71.1 us: conv_call(): call(functools.partial(conv_kernel, level, block), [sds((rows * cols, cha...]
    ppermute x3 -> x25, waiting for transfers between devices: 31.2 us -> 53.2 us  [the longest x9 25 us: last_swap(): total = total + lax.ppermute(part(mine ^ d), 'img', pairs).astype(F32)]
    convert_element_type x0 -> x17, other arithmetic: none -> 20.2 us  [the longest x8 16.2 us: half(): return (parts[0].astype(F32) + parts[1].astype(F32)).astype(BF)]
    pallas_call x4, Pallas kernels: 40 us -> 31.8 us  [conv_back_call(): call(functools.partial(conv_back_kernel, ways, block), out, grid=(rows //...]
  transfers between devices with their start and end apart: 11 -> 31, of which waited for: 8 -> 14; matrix products, arithmetic and copies ran while one was open for 7% -> 14% of each run, Pallas kernels for 7% -> 31%
where the time goes in v2:
time: 524 us; the launch traced here: 515 us
  Pallas kernels  296 us (56%)
  waiting for transfers between devices  67.1 us (13%)
  other arithmetic  47.9 us (9%)
  starting transfers between devices  44.2 us (8%)
  local copies, waits for them, and re-layouts  42.7 us (8%)
  between operations  16.4 us (3%)
    pallas_call x4, Pallas kernels, conv_call(): call(functools.partial(conv_kernel, level, block), [sds((rows * cols, cha...  71.1 us
    pallas_call x1, Pallas kernels, pyramid_back_call(): call(functools.partial(pyramid_back_kernel, lr, cols, shards), [sds((toke...  45.6 us
    pallas_call x2, Pallas kernels, attend_back_call(): call(functools.partial(attend_back_kernel, total_rows, scale, sources), [...  33.1 us
    pallas_call x4, Pallas kernels, conv_back_call(): call(functools.partial(conv_back_kernel, ways, block), out, grid=(rows //...  31.8 us
    ppermute x9, waiting for transfers between devices, last_swap(): total = total + lax.ppermute(part(mine ^ d), 'img', pairs).astype(F32)  25 us
    pallas_call x1, Pallas kernels, attend_call(): call(functools.partial(attend_kernel, total_rows, scale, parts), [sds((to...  24.5 us
    pallas_call x1, Pallas kernels, mlp_back_call(): call(functools.partial(mlp_back_kernel, shards), [sds((width // 2, hidden...  24.5 us
    ppermute x9, starting transfers between devices, last_swap(): total = total + lax.ppermute(part(mine ^ d), 'img', pairs).astype(F32)  23.3 us
  transfers between devices with their start and end apart: 31, of which 14 were waited for; matrix products, arithmetic and copies ran while one was open for 14% of the time, Pallas kernels for 31%

profile of v2, /device:TPU:0, one launch (start us, length us, event | category | flops | bytes accessed | tf_op | source)
XLA Modules:
  0.0 514.7 jit_solution(2595167986154389093)
XLA Ops:
  16.4 6.2 %qkv.2.refs_1_.refs_6_.refs_8_.refs_10_.refs_12_ = bf16[512,2304]{1,0:T(8,128)(2,1)} custom-call(bf16[512,768]{1,0:T(8,128)(2,1)} %bitcast.195, bf16[768,2304]{1,0:T(8,128)(2,1)} %w_ref.5, f32[3,1,768]{2,1,0:T(1,128)} %maximum_convert_fusion.3.b_ref, f32[8,768]{1,0:T(8,128)} %convert_element_type.518.p_ref), custom_call_target="tpu_custom_call" | custom-call | flops 18119392 | tf_op jit(solution)/shard_map/qkv/pallas_call | solution.py:155
  36.7 24.5 %attend.1 = (bf16[512,768]{1,0:T(8,128)(2,1)}, bf16[12,512,256]{2,1,0:T(8,128)(2,1)}, f32[6,2,512]{2,1,0:T(2,128)}) custom-call(s32[1]{0:T(128)} %bitcast.1.refs_0_, bf16[512,2304]{1,0:T(8,128)(2,1)} %qkv.2.refs_1_.refs_6_.refs_8_.refs_10_.refs_12_, bf16[128,128]{1,0:T(8,128)(2,1)} %pad_maximum_fusion.6.refs_2_, bf16[128,128]{1,0:T(8,128)(2,1)} %pad_maximum_fusion.7.refs_3_, ...), custom_call_target="tpu_custom_call" | custom-call | flops 250000000 | tf_op jit(solution)/shard_map/attend/pallas_call | solution.py:305
  61.2 14.1 %mlp.1 = (f32[512,768]{1,0:T(8,128)}, bf16[512,3072]{1,0:T(8,128)(2,1)}, bf16[512,3072]{1,0:T(8,128)(2,1)}, bf16[512,768]{1,0:T(8,128)(2,1)}) custom-call(bf16[512,768]{1,0:T(8,128)(2,1)} %bitcast.196, bf16[512,768]{1,0:T(8,128)(2,1)} %get-tuple-element.149.o_ref.refs_4_, bf16[768,768]{1,0:T(8,128)(2,1)} %wp_ref.3, bf16[768,3072]{1,0:T(8,128)(2,1)} %w1_ref.3, ...), custom_call_target="tpu_custom_call" | custom-call | flops 140000000 | tf_op jit(solution)/shard_map/mlp/pallas_call | solution.py:370
  75.3 20.4 %pyramid.1 = (bf16[8,4,256,256]{3,2,1,0:T(8,128)(2,1)}, bf16[8,2,128,256]{3,2,1,0:T(8,128)(2,1)}, bf16[512,256]{1,0:T(8,128)(2,1)}, bf16[128,256]{1,0:T(8,128)(2,1)}) custom-call(bf16[512,768]{1,0:T(8,128)(2,1)} %get-tuple-element.151.y_ref, bf16[768,1536]{1,0:T(8,128)(2,1)} %ff_ref.3, bf16[768,384]{1,0:T(8,128)(2,1)} %fs_ref.3, bf16[768,1536]{1,0:T(8,128)(2,1)} %mu_ref.3, ...), custom_call_target="tpu_custom_call" | custom-call | flops 200000000 | tf_op jit(solution)/shard_map/pyramid/pallas_call | solution.py:506
  99.3 5.1 copy.126
  109.4 5.8 %conv3.1 = (bf16[128,256]{1,0:T(8,128)(2,1)}, bf16[128,256]{1,0:T(8,128)(2,1)}, bf16[2304,1024]{1,0:T(8,128)(2,1)}, f32[8,256]{1,0:T(8,128)}) custom-call(bf16[4,32,256]{2,1,0:T(8,128)(2,1)} %bitcast.239, bf16[2,32,256]{2,1,0:T(8,128)(2,1)} %pad_maximum_fusion.5.rim_ref, bf16[4,3,768,256]{3,2,1,0:T(8,128)(2,1)} %bitcast.185, bf16[128,256]{1,0:T(8,128)(2,1)} %bitcast.240, ...), custom_call_target="tpu_custom_call" | custom-call | flops 3774873 | tf_op jit(solution)/shard_map/conv3/pallas_call | solution.py:646
  115.2 7.3 %conv2.1 = (bf16[512,256]{1,0:T(8,128)(2,1)}, bf16[512,256]{1,0:T(8,128)(2,1)}, bf16[2304,1024]{1,0:T(8,128)(2,1)}, f32[8,256]{1,0:T(8,128)}) custom-call(bf16[8,64,256]{2,1,0:T(8,128)(2,1)} %bitcast.234, bf16[2,64,256]{2,1,0:T(8,128)(2,1)} %fusion.62.rim_ref, bf16[4,3,768,256]{3,2,1,0:T(8,128)(2,1)} %bitcast.186, ...), custom_call_target="tpu_custom_call", output_to_operand_aliasing={{2}: (5, {})} | custom-call | flops 15099494 | tf_op jit(solution)/shard_map/conv2/pallas_call | solution.py:646
  122.4 15.1 %conv1.1 = (bf16[2048,256]{1,0:T(8,128)(2,1)}, bf16[2048,256]{1,0:T(8,128)(2,1)}, bf16[2304,1024]{1,0:T(8,128)(2,1)}, f32[8,256]{1,0:T(8,128)}) custom-call(bf16[16,128,256]{2,1,0:T(8,128)(2,1)} %bitcast.222, bf16[2,128,256]{2,1,0:T(8,128)(2,1)} %fusion.60.rim_ref, bf16[4,3,768,256]{3,2,1,0:T(8,128)(2,1)} %bitcast.187, ...), custom_call_target="tpu_custom_call", output_to_operand_aliasing={{2}: (5, {})} | custom-call | flops 60397976 | tf_op jit(solution)/shard_map/conv1/pallas_call | solution.py:646
  137.6 42.9 %conv0.1 = (bf16[8192,256]{1,0:T(8,128)(2,1)}, bf16[8192,256]{1,0:T(8,128)(2,1)}, bf16[2304,1024]{1,0:T(8,128)(2,1)}, f32[8,256]{1,0:T(8,128)}) custom-call(bf16[32,256,256]{2,1,0:T(8,128)(2,1)} %bitcast.203, bf16[2,256,256]{2,1,0:T(8,128)(2,1)} %fusion.38.rim_ref, bf16[4,3,768,256]{3,2,1,0:T(8,128)(2,1)} %bitcast.188, ...), custom_call_target="tpu_custom_call", output_to_operand_aliasing={{2}: (5, {})} | custom-call | flops 241591904 | tf_op jit(solution)/shard_map/conv0/pallas_call | solution.py:646
  185.7 4.9 collective-permute-done.2
  198.5 7.0 %conv_back1.1.dzm_ref = bf16[2,2,512,256]{3,2,1,0:T(8,128)(2,1)} custom-call(bf16[16,128,256]{2,1,0:T(8,128)(2,1)} %bitcast.223, bf16[2,128,256]{2,1,0:T(8,128)(2,1)} %fusion.59.rim_ref, bf16[4,3,768,256]{3,2,1,0:T(8,128)(2,1)} %bitcast.191), custom_call_target="tpu_custom_call" | custom-call | flops 36238784 | tf_op jit(solution)/shard_map/conv_back1/pallas_call | solution.py:727
  206.2 18.9 %conv_back0.1 = bf16[4,4,512,256]{3,2,1,0:T(8,128)(2,1)} custom-call(bf16[32,256,256]{2,1,0:T(8,128)(2,1)} %bitcast.201, bf16[2,256,256]{2,1,0:T(8,128)(2,1)} %fusion.37.rim_ref, bf16[4,3,768,256]{3,2,1,0:T(8,128)(2,1)} %bitcast.192), custom_call_target="tpu_custom_call" | custom-call | flops 144955152 | tf_op jit(solution)/shard_map/conv_back0/pallas_call | solution.py:727
  225.1 45.6 %pyramid_back.1 = (f32[512,768]{1,0:T(8,128)}, bf16[384,4224]{1,0:T(8,128)(2,1)}, bf16[384,4224]{1,0:T(8,128)(2,1)}, f32[8,384]{1,0:T(8,128)}, f32[8,192]{1,0:T(8,128)}, /*index=5*/f32[16,256]{1,0:T(8,128)}) custom-call(s32[1]{0:T(128)} %bitcast.40.core_ref, bf16[512,768]{1,0:T(8,128)(2,1)} %get-tuple-element.151.y_ref, bf16[768,1536]{1,0:T(8,128)(2,1)} %ff_ref.3, ...), custom_call_target="tpu_custom_call" | custom-call | flops 450000000 | tf_op jit(solution)/shard_map/pyramid_back/pallas_call | solution.py:902
  277.7 24.5 %mlp_back.1 = (bf16[384,3968]{1,0:T(8,128)(2,1)}, bf16[384,3968]{1,0:T(8,128)(2,1)}, bf16[1536,768]{1,0:T(8,128)(2,1)}, bf16[1536,768]{1,0:T(8,128)(2,1)}, f32[512,768]{1,0:T(8,128)}, /*index=5*/bf16[512,768]{1,0:T(8,128)(2,1)}) custom-call(s32[1]{0:T(128)} %bitcast.40.core_ref, f32[512,768]{1,0:T(8,128)} %get-tuple-element.183.dy_ref, ...), custom_call_target="tpu_custom_call" | custom-call | flops 250000000 | tf_op jit(solution)/shard_map/mlp_back/pallas_call | solution.py:1077
  312.9 16.7 %attend_back.2 = (bf16[3,1024,768]{2,1,0:T(8,128)(2,1)}, f32[128,256]{1,0:T(8,128)}) custom-call(s32[1]{0:T(128)} %bitcast.1.refs_0_, bf16[512,2304]{1,0:T(8,128)(2,1)} %qkv.2.refs_1_.refs_6_.refs_8_.refs_10_.refs_12_, bf16[12,512,256]{2,1,0:T(8,128)(2,1)} %get-tuple-element.171.refs_2_, bf16[512,768]{1,0:T(8,128)(2,1)} %get-tuple-element.201.refs_3_, ...), custom_call_target="tpu_custom_call" | custom-call | flops 150000000 | tf_op jit(solution)/shard_map/attend_back/pallas_call | solution.py:1253
  341.7 16.4 %attend_back.3 = (bf16[3,1024,768]{2,1,0:T(8,128)(2,1)}, f32[128,256]{1,0:T(8,128)}) custom-call(s32[1]{0:T(128)} %bitcast.1.refs_0_, bf16[512,2304]{1,0:T(8,128)(2,1)} %qkv.2.refs_1_.refs_6_.refs_8_.refs_10_.refs_12_, bf16[12,512,256]{2,1,0:T(8,128)(2,1)} %get-tuple-element.171.refs_2_, ...), custom_call_target="tpu_custom_call", output_to_operand_aliasing={{0}: (14, {})} | custom-call | flops 150000000 | tf_op jit(solution)/shard_map/attend_back/pallas_call | solution.py:1253
  362.5 20.5 %qkv_back.1 = (bf16[768,2688]{1,0:T(8,128)(2,1)}, f32[512,768]{1,0:T(8,128)}, bf16[512,768]{1,0:T(8,128)(2,1)}) custom-call(bf16[1024,768]{1,0:T(8,128)(2,1)} %pad_maximum_fusion.x_ref, bf16[3,1024,768]{2,1,0:T(8,128)(2,1)} %get-tuple-element.214.dqkv_ref, bf16[768,2304]{1,0:T(8,128)(2,1)} %w_ref.5, f32[512,768]{1,0:T(8,128)} %get-tuple-element.215.dx1_ref, ...), custom_call_target="tpu_custom_call" | custom-call | flops 80000000 | tf_op jit(solution)/shard_map/qkv_back/pallas_call | solution.py:1360
  386.5 6.8 %collective-permute-done.28 = bf16[144,1024]{1,0:T(8,128)(2,1)} collective-permute-done((bf16[144,1024]{1,0:T(8,128)(2,1)}, bf16[144,1024]{1,0:T(8,128)(2,1)}, u32[]{:S(2)}, u32[]{:S(2)}) %collective-permute-start.28) | collective-permute-done | bytes 294944 | tf_op jit(solution)/shard_map/ppermute | solution.py:1513
  407.6 9.4 %collective-permute-done.8 = bf16[512,768]{1,0:T(8,128)(2,1)} collective-permute-done((bf16[512,768]{1,0:T(8,128)(2,1)}, bf16[512,768]{1,0:T(8,128)(2,1)}, u32[]{:S(2)}, u32[]{:S(2)}) %collective-permute-start.8) | collective-permute-done | bytes 786464 | tf_op jit(solution)/shard_map/ppermute | solution.py:1685
  419.4 5.7 %collective-permute-done.14 = bf16[24,4224]{1,0:T(8,128)(2,1)S(1)} collective-permute-done((bf16[24,4224]{1,0:T(8,128)(2,1)S(1)}, bf16[24,4224]{1,0:T(8,128)(2,1)S(1)}, u32[]{:S(2)}, u32[]{:S(2)}) %collective-permute-start.14) | collective-permute-done | bytes 202784 | tf_op jit(solution)/shard_map/ppermute | solution.py:1493
  434.3 6.0 %collective-permute-done.18 = bf16[384,768]{1,0:T(8,128)(2,1)S(1)} collective-permute-done((bf16[384,768]{1,0:T(8,128)(2,1)S(1)}, bf16[384,768]{1,0:T(8,128)(2,1)S(1)}, u32[]{:S(2)}, u32[]{:S(2)}) %collective-permute-start.18) | collective-permute-done | bytes 589856 | tf_op jit(solution)/shard_map/ppermute | solution.py:1465
  440.3 4.8 collective-permute-done.17
  445.3 9.7 %collective-permute-start.23 = (bf16[96,768]{1,0:T(8,128)(2,1)S(1)}, bf16[96,768]{1,0:T(8,128)(2,1)S(1)}, u32[]{:S(2)}, u32[]{:S(2)}) collective-permute-start(bf16[96,768]{1,0:T(8,128)(2,1)S(1)} %get-tuple-element.456), channel_id=1, source_target_pairs={{0,8},{2,10},{4,12},{6,14},{8,0},{10,2},{12,4},{14,6},{16,24},{18,... | collective-permute-start | bytes 442376 | tf_op jit(solution)/shard_map/ppermute | solution.py:1493
  467.7 12.0 %collective-permute-done.24 = bf16[96,768]{1,0:T(8,128)(2,1)S(1)} collective-permute-done((bf16[96,768]{1,0:T(8,128)(2,1)S(1)}, bf16[96,768]{1,0:T(8,128)(2,1)S(1)}, u32[]{:S(2)}, u32[]{:S(2)}) %collective-permute-start.24) | collective-permute-done | bytes 147488 | tf_op jit(solution)/shard_map/ppermute | solution.py:1493
  (244 shorter events, 147.9 us)
Async XLA Ops:
  7.2 301.9 %reduce-scatter.3.cloned.1.call-start = ((), (), s32[]{:S(2)}) async-start(), calls=%async_computation.2 | async-start | bytes 5013504 | tf_op jit(solution)/shard_map/reduce_scatter | solution.py:1619
  7.2 24.0 %collective-permute-start = (bf16[512,768]{1,0:T(8,128)(2,1)}, bf16[512,768]{1,0:T(8,128)(2,1)S(1)}, u32[]{:S(2)}, u32[]{:S(2)}) collective-permute-start(bf16[512,768]{1,0:T(8,128)(2,1)} %bitcast.194), channel_id=1, source_target_pairs={{0,1},{1,0},{2,3},{3,2},{4,5},{5,4},{6,7},{7,6},{8,9},{9,8},{10,11... | collective-permute-start | bytes 2359304 | tf_op jit(solution)/shard_map/ppermute | solution.py:1539
  180.5 310.8 %reduce-scatter.5.cloned.1.call-start = ((), (), s32[]{:S(2)}) async-start(), calls=%async_computation.3 | async-start | bytes 4386816 | tf_op jit(solution)/shard_map/reduce_scatter | solution.py:1682
  270.8 31.5 %collective-permute-start.3 = (bf16[384,4224]{1,0:T(8,128)(2,1)}, bf16[384,4224]{1,0:T(8,128)(2,1)}, u32[]{:S(2)}, u32[]{:S(2)}) collective-permute-start(bf16[384,4224]{1,0:T(8,128)(2,1)} %get-tuple-element.178), channel_id=1, source_target_pairs={{0,2},{2,0},{4,6},{6,4},{8,10},{10,8},{12,14},{14,12},{16,18},{18,... | collective-permute-start | bytes 9732104 | tf_op jit(solution)/shard_map/ppermute | solution.py:1465
  309.1 20.5 %collective-permute-start.4 = (bf16[384,3968]{1,0:T(8,128)(2,1)}, bf16[384,3968]{1,0:T(8,128)(2,1)S(1)}, u32[]{:S(2)}, u32[]{:S(2)}) collective-permute-start(bf16[384,3968]{1,0:T(8,128)(2,1)} %get-tuple-element.196), channel_id=1, source_target_pairs={{0,2},{2,0},{4,6},{6,4},{8,10},{10,8},{12,14},{14,12},{16,18},{18,... | collective-permute-start | bytes 9142280 | tf_op jit(solution)/shard_map/ppermute | solution.py:1465
  309.6 20.0 %collective-permute-start.5 = (bf16[1536,768]{1,0:T(8,128)(2,1)}, bf16[1536,768]{1,0:T(8,128)(2,1)}, u32[]{:S(2)}, u32[]{:S(2)}) collective-permute-start(bf16[1536,768]{1,0:T(8,128)(2,1)} %get-tuple-element.197), channel_id=1, source_target_pairs={{0,2},{2,0},{4,6},{6,4},{8,10},{10,8},{12,14},{14,12},{16,18},{18,... | collective-permute-start | bytes 7077896 | tf_op jit(solution)/shard_map/ppermute | solution.py:1465
  310.2 47.9 %collective-permute-start.6 = (bf16[192,2048]{1,0:T(8,128)(2,1)}, bf16[192,2048]{1,0:T(8,128)(2,1)}, u32[]{:S(2)}, u32[]{:S(2)}) collective-permute-start(bf16[192,2048]{1,0:T(8,128)(2,1)} %bitcast.72), channel_id=1, source_target_pairs={{0,4},{2,6},{4,0},{6,2},{8,12},{10,14},{12,8},{14,10},{16,20},{18,... | collective-permute-start | bytes 2359304 | tf_op jit(solution)/shard_map/ppermute | solution.py:1465
  311.6 46.5 %collective-permute-start.7 = (bf16[192,2176]{1,0:T(8,128)(2,1)}, bf16[192,2176]{1,0:T(8,128)(2,1)S(1)}, u32[]{:S(2)}, u32[]{:S(2)}) collective-permute-start(bf16[192,2176]{1,0:T(8,128)(2,1)} %bitcast.226), channel_id=1, source_target_pairs={{0,1},{1,0},{2,3},{3,2},{4,5},{5,4},{6,7},{7,6},{8,9},{9,8},{10,11... | collective-permute-start | bytes 2506760 | tf_op jit(solution)/shard_map/ppermute | solution.py:1465
  337.4 64.4 %collective-permute-start.11 = (bf16[192,3968]{1,0:T(8,128)(2,1)}, bf16[192,3968]{1,0:T(8,128)(2,1)}, u32[]{:S(2)}, u32[]{:S(2)}) collective-permute-start(bf16[192,3968]{1,0:T(8,128)(2,1)} %bitcast.87), channel_id=1, source_target_pairs={{0,4},{2,6},{4,0},{6,2},{8,12},{10,14},{12,8},{14,10},{16,20},{18,... | collective-permute-start | bytes 4571144 | tf_op jit(solution)/shard_map/ppermute | solution.py:1465
  340.2 61.5 %collective-permute-start.12 = (bf16[768,768]{1,0:T(8,128)(2,1)}, bf16[768,768]{1,0:T(8,128)(2,1)}, u32[]{:S(2)}, u32[]{:S(2)}) collective-permute-start(bf16[768,768]{1,0:T(8,128)(2,1)} %bitcast.89), channel_id=1, source_target_pairs={{0,1},{1,0},{2,3},{3,2},{4,5},{5,4},{6,7},{7,6},{8,9},{9,8},{10,11... | collective-permute-start | bytes 3538952 | tf_op jit(solution)/shard_map/ppermute | solution.py:1465
  383.6 18.1 %collective-permute-start.10 = (bf16[96,2176]{1,0:T(8,128)(2,1)}, bf16[96,2176]{1,0:T(8,128)(2,1)}, u32[]{:S(2)}, u32[]{:S(2)}) collective-permute-start(bf16[96,2176]{1,0:T(8,128)(2,1)} %bitcast.233), channel_id=1, source_target_pairs={{0,4},{2,6},{4,0},{6,2},{8,12},{10,14},{12,8},{14,10},{16,20},{18,... | collective-permute-start | bytes 1253384 | tf_op jit(solution)/shard_map/ppermute | solution.py:1465
  385.1 16.6 %collective-permute-start.9 = (bf16[96,2048]{1,0:T(8,128)(2,1)}, bf16[96,2048]{1,0:T(8,128)(2,1)}, u32[]{:S(2)}, u32[]{:S(2)}) collective-permute-start(bf16[96,2048]{1,0:T(8,128)(2,1)} %bitcast.236), channel_id=1, source_target_pairs={{0,1},{1,0},{2,3},{3,2},{4,5},{5,4},{6,7},{7,6},{8,9},{9,8},{10,11... | collective-permute-start | bytes 1179656 | tf_op jit(solution)/shard_map/ppermute | solution.py:1465
  393.3 23.6 %collective-permute-start.8 = (bf16[512,768]{1,0:T(8,128)(2,1)}, bf16[512,768]{1,0:T(8,128)(2,1)}, u32[]{:S(2)}, u32[]{:S(2)}) collective-permute-start(bf16[512,768]{1,0:T(8,128)(2,1)} %get-tuple-element.227), channel_id=1, source_target_pairs={{0,1},{1,0},{2,3},{3,2},{4,5},{5,4},{6,7},{7,6},{8,9},{9,8},{10,11... | collective-permute-start | bytes 2359304 | tf_op jit(solution)/shard_map/ppermute | solution.py:1685
  403.1 16.3 %collective-permute-start.13 = (bf16[24,4224]{1,0:T(8,128)(2,1)S(1)}, bf16[24,4224]{1,0:T(8,128)(2,1)S(1)}, u32[]{:S(2)}, u32[]{:S(2)}) collective-permute-start(bf16[24,4224]{1,0:T(8,128)(2,1)S(1)} %get-tuple-element.448), channel_id=1, source_target_pairs={{0,8},{2,10},{4,12},{6,14},{8,0},{10,2},{12,4},{14,6},{16,24},{18,... | collective-permute-start | bytes 608264 | tf_op jit(solution)/shard_map/ppermute | solution.py:1493
  404.8 20.3 %collective-permute-start.14 = (bf16[24,4224]{1,0:T(8,128)(2,1)S(1)}, bf16[24,4224]{1,0:T(8,128)(2,1)S(1)}, u32[]{:S(2)}, u32[]{:S(2)}) collective-permute-start(bf16[24,4224]{1,0:T(8,128)(2,1)S(1)} %get-tuple-element.449), channel_id=1, source_target_pairs={{0,16},{2,18},{4,20},{6,22},{8,24},{10,26},{12,28},{14,30},{16,0},... | collective-permute-start | bytes 608264 | tf_op jit(solution)/shard_map/ppermute | solution.py:1493
  407.4 17.7 %collective-permute-start.15 = (bf16[24,4224]{1,0:T(8,128)(2,1)S(1)}, bf16[24,4224]{1,0:T(8,128)(2,1)S(1)}, u32[]{:S(2)}, u32[]{:S(2)}) collective-permute-start(bf16[24,4224]{1,0:T(8,128)(2,1)S(1)} %get-tuple-element.450), channel_id=1, source_target_pairs={{0,24},{2,26},{4,28},{6,30},{8,16},{10,18},{12,20},{14,22},{16,8},... | collective-permute-start | bytes 608264 | tf_op jit(solution)/shard_map/ppermute | solution.py:1493
  429.6 10.8 %collective-permute-start.18 = (bf16[384,768]{1,0:T(8,128)(2,1)S(1)}, bf16[384,768]{1,0:T(8,128)(2,1)S(1)}, u32[]{:S(2)}, u32[]{:S(2)}) collective-permute-start(bf16[384,768]{1,0:T(8,128)(2,1)S(1)} %bitcast.232), channel_id=1, source_target_pairs={{0,4},{2,6},{4,0},{6,2},{8,12},{10,14},{12,8},{14,10},{16,20},{18,... | collective-permute-start | bytes 1769480 | tf_op jit(solution)/shard_map/ppermute | solution.py:1465
  431.2 14.0 %collective-permute-start.17 = (bf16[96,3968]{1,0:T(8,128)(2,1)S(1)}, bf16[96,3968]{1,0:T(8,128)(2,1)S(1)}, u32[]{:S(2)}, u32[]{:S(2)}) collective-permute-start(bf16[96,3968]{1,0:T(8,128)(2,1)S(1)} %bitcast.227), channel_id=1, source_target_pairs={{0,1},{1,0},{2,3},{3,2},{4,5},{5,4},{6,7},{7,6},{8,9},{9,8},{10,11... | collective-permute-start | bytes 2285576 | tf_op jit(solution)/shard_map/ppermute | solution.py:1465
  445.3 19.0 %collective-permute-start.23 = (bf16[96,768]{1,0:T(8,128)(2,1)S(1)}, bf16[96,768]{1,0:T(8,128)(2,1)S(1)}, u32[]{:S(2)}, u32[]{:S(2)}) collective-permute-start(bf16[96,768]{1,0:T(8,128)(2,1)S(1)} %get-tuple-element.456), channel_id=1, source_target_pairs={{0,8},{2,10},{4,12},{6,14},{8,0},{10,2},{12,4},{14,6},{16,24},{18,... | collective-permute-start | bytes 442376 | tf_op jit(solution)/shard_map/ppermute | solution.py:1493
  455.0 12.7 %collective-permute-start.25 = (bf16[96,768]{1,0:T(8,128)(2,1)S(1)}, bf16[96,768]{1,0:T(8,128)(2,1)S(1)}, u32[]{:S(2)}, u32[]{:S(2)}) collective-permute-start(bf16[96,768]{1,0:T(8,128)(2,1)S(1)} %get-tuple-element.457), channel_id=1, source_target_pairs={{0,24},{2,26},{4,28},{6,30},{8,16},{10,18},{12,20},{14,22},{16,8},... | collective-permute-start | bytes 442376 | tf_op jit(solution)/shard_map/ppermute | solution.py:1493
  459.0 20.8 %collective-permute-start.24 = (bf16[96,768]{1,0:T(8,128)(2,1)S(1)}, bf16[96,768]{1,0:T(8,128)(2,1)S(1)}, u32[]{:S(2)}, u32[]{:S(2)}) collective-permute-start(bf16[96,768]{1,0:T(8,128)(2,1)S(1)} %get-tuple-element.458), channel_id=1, source_target_pairs={{0,16},{2,18},{4,20},{6,22},{8,24},{10,26},{12,28},{14,30},{16,0},... | collective-permute-start | bytes 442376 | tf_op jit(solution)/shard_map/ppermute | solution.py:1493
  459.1 22.4 %collective-permute-start.19 = (bf16[24,3968]{1,0:T(8,128)(2,1)S(1)}, bf16[24,3968]{1,0:T(8,128)(2,1)S(1)}, u32[]{:S(2)}, u32[]{:S(2)}) collective-permute-start(bf16[24,3968]{1,0:T(8,128)(2,1)S(1)} %get-tuple-element.453), channel_id=1, source_target_pairs={{0,8},{2,10},{4,12},{6,14},{8,0},{10,2},{12,4},{14,6},{16,24},{18,... | collective-permute-start | bytes 571400 | tf_op jit(solution)/shard_map/ppermute | solution.py:1493
  459.7 21.7 %collective-permute-start.21 = (bf16[24,3968]{1,0:T(8,128)(2,1)S(1)}, bf16[24,3968]{1,0:T(8,128)(2,1)S(1)}, u32[]{:S(2)}, u32[]{:S(2)}) collective-permute-start(bf16[24,3968]{1,0:T(8,128)(2,1)S(1)} %get-tuple-element.454), channel_id=1, source_target_pairs={{0,24},{2,26},{4,28},{6,30},{8,16},{10,18},{12,20},{14,22},{16,8},... | collective-permute-start | bytes 571400 | tf_op jit(solution)/shard_map/ppermute | solution.py:1493
  464.3 21.1 %collective-permute-start.20 = (bf16[24,3968]{1,0:T(8,128)(2,1)S(1)}, bf16[24,3968]{1,0:T(8,128)(2,1)S(1)}, u32[]{:S(2)}, u32[]{:S(2)}) collective-permute-start(bf16[24,3968]{1,0:T(8,128)(2,1)S(1)} %get-tuple-element.455), channel_id=1, source_target_pairs={{0,16},{2,18},{4,20},{6,22},{8,24},{10,26},{12,28},{14,30},{16,0},... | collective-permute-start | bytes 571400 | tf_op jit(solution)/shard_map/ppermute | solution.py:1493
  (31 other events, 205.0 us)
Sparse Core Ops, SparseCore 0:
  180.6 75.8 reduce-scatter.2
  386.6 77.1 reduce-scatter.4

commit v3 on v2

--- a/solution.py
+++ b/solution.py
@@ -753,9 +753,9 @@
 
 
 def pyramid_back_kernel(
-    lr, cols, shards, core_ref, y_ref, ff_ref, fs_ref, mu_ref, lf_ref, lm_ref, lc0_ref, lc1_ref, p384_ref,
+    lr, cols, y_ref, ff_ref, fs_ref, mu_ref, lf_ref, lm_ref, lc0_ref, lc1_ref, p384_ref,
     fsb_ref, p256_ref, dzf_ref, dzm_ref, dzb_ref, dzc_ref, place_ref,
-    dy_ref, keep_ref, send_ref, s384_ref, s192_ref, s256_ref,
+    dy_ref, pack_ref, s384_ref, s192_ref, s256_ref,
     yt_ref, hat_ref, slope_ref, inv_ref, f2_ref, df2_ref, df1_ref, dl_ref, fs_acc, lf_acc, lm_acc,
     dcol_ref, drest_ref, product_ref, pick_ref, third_ref, stack_ref, dls_ref, sem,
 ):
@@ -765,8 +765,13 @@
     half = ff_ref.shape[1]
     chan = lf_ref.shape[1]
 
-    core = core_ref[0]
     rest = drest_ref.shape[1]
+
+    def col_copy(at):
+        lanes = pl.ds(pl.multiple_of(at * 2 * half, 2 * half), 2 * half)
+        return pltpu.make_async_copy(dcol_ref.at[at], pack_ref.at[:, lanes], sem.at[at])
+
+    rest_copy = pltpu.make_async_copy(drest_ref, pack_ref.at[:, pl.ds(8 * half, rest)], sem.at[4])
 
     @pl.when(step == 0)
     def _():
@@ -874,8 +879,7 @@
     df1_ref[...] = mt(dl_ref[...], lm_ref[...]).astype(BF)
     s384_ref[3:4, :] += rowsum(df1_ref[...].astype(F32))
     dcol_ref[step, :, half:] = mm(yt_ref[...], df1_ref[...]).astype(BF)
-    lanes = pl.ds(pl.multiple_of(step * 2 * half, 2 * half), 2 * half)
-    put_shards(dcol_ref.at[step], keep_ref, send_ref, lanes, shards, 0, core, sem.at[step])
+    col_copy(step).start()
     dy_ref[...] += mt(df1_ref[...], mu_ref[...])
 
     @pl.when(step == pl.num_programs(0) - 1)
@@ -883,16 +887,14 @@
         drest_ref[:, 0:half] = fs_acc[...].astype(BF)
         laterals = jnp.concatenate([lf_acc[...], lm_acc[...]], axis=0).astype(BF)
         drest_ref[:, half + 2 * chan : half + 3 * chan] = mm(place_ref[...], laterals).astype(BF)
-        put_shards(
-            drest_ref, keep_ref, send_ref, pl.ds(8 * half, rest), shards, 0, core, sem.at[4]
-        )
+        rest_copy.start()
         for at in range(4):
-            wait_shards(dcol_ref.at[at], sem.at[at])
-        wait_shards(drest_ref, sem.at[4])
+            col_copy(at).wait()
+        rest_copy.wait()
 
 
 def pyramid_back_call(
-    y, lr, cols, ff, fs, mu, lf, lm, lc0, lc1, p384, fsb, p256, dzf, dzm, dzb, dzc, place, core, shards
+    y, lr, cols, ff, fs, mu, lf, lm, lc0, lc1, p384, fsb, p256, dzf, dzm, dzb, dzc, place
 ):
     tokens, width = y.shape
     half = fs.shape[1]
@@ -900,18 +902,16 @@
     outs = lf.shape[1]
     col_block = pl.BlockSpec((width, half), lambda s: (0, s))
     return call(
-        functools.partial(pyramid_back_kernel, lr, cols, shards),
+        functools.partial(pyramid_back_kernel, lr, cols),
         [
             sds((tokens, width), F32),
-            sds((width // 2, 9 * half + 3 * outs), BF),
-            sds((width // 2, 9 * half + 3 * outs), BF),
+            sds((width, 9 * half + 3 * outs), BF),
             sds((8, half), F32),
             sds((8, quart), F32),
             sds((16, outs), F32),
         ],
         grid=(4,),
         in_specs=[
-            pl.BlockSpec(memory_space=pltpu.SMEM),
             whole(y.shape),
             col_block,
             whole(fs.shape),
@@ -931,7 +931,6 @@
         ],
         out_specs=[
             whole((tokens, width)),
-            pl.BlockSpec(memory_space=pl.ANY),
             pl.BlockSpec(memory_space=pl.ANY),
             whole((8, half)),
             whole((8, quart)),
@@ -961,7 +960,7 @@
         flops=45e9,
         name="pyramid_back",
     )(
-        core, y, ff, fs, mu, lf, lm, lc0, lc1, p384, fsb, p256,
+        y, ff, fs, mu, lf, lm, lc0, lc1, p384, fsb, p256,
         dzf.reshape(2, 2, 2, 2, tokens, outs), dzm, dzb, dzc, place,
     )
 
@@ -1424,14 +1423,6 @@
         self.shape = (2,) * (bits - 1) + (keep.shape[0] >> (bits - 1), keep.shape[1])
         self.keep, self.first = keep.reshape(self.shape), send.reshape(self.shape)
 
-    def lanes(self):
-        first, second = Halving.__new__(Halving), Halving.__new__(Halving)
-        middle = self.shape[-1] // 256 * 128
-        for part, cut in ((first, slice(0, middle)), (second, slice(middle, None))):
-            part.left = list(self.left)
-            part.terms = [term[..., cut] for term in self.terms]
-        return first, second
-
     def split(self, step):
         if step == 0:
             self.route = ("img", [(i, i ^ 1) for i in range(lax.axis_size("img"))])
@@ -1618,12 +1609,6 @@
 
     conv_low = lax.psum_scatter(packed, "img", scatter_dimension=0, tiled=True)
     drims = rim_exchange(drs, "seq")
-    dzs = []
-    for level, ways in enumerate((4, 2, 1, 1)):
-        dr = drs[level]
-        block = min(dr.shape[0], max(1, 2048 // dr.shape[1]))
-        dzs.append(conv_back_call(level, dr, drims[level], conv_weights, ways, block))
-
     unit = width // shards
     packed_row, _ = lax.optimization_barrier((jnp.arange(width)[:, None], level_sums[0]))
     shard_at, within = packed_row // unit, packed_row % unit
@@ -1643,13 +1628,20 @@
     )
     place = (at == source).astype(BF)
     hots = (placed(chan), placed(half), placed(quart))
+    drims, hots, place = lax.optimization_barrier((drims, hots, place))
+    dzs = []
+    for level, ways in enumerate((4, 2, 1, 1)):
+        dr = drs[level]
+        block = min(dr.shape[0], max(1, 2048 // dr.shape[1]))
+        dzs.append(conv_back_call(level, dr, drims[level], conv_weights, ways, block))
+
     core = (lax.axis_index("img") & 1).astype(jnp.int32).reshape(1)
-    dy, low_keep, low_send, s384, s192, s256 = pyramid_back_call(
+    dy, low_pack, s384, s192, s256 = pyramid_back_call(
         y, lr, cols, fine_first, fine_second, middle_up, lateral_fine, lateral_middle, lc0, lc1, p384, fsb, p256,
-        *dzs, place, core, shards,
-    )
-    pyramid_sum = Halving(low_keep, low_send)
-    moving, dy = swap([(pyramid_sum, 0)], dy)
+        *dzs, place,
+    )
+    low_pack, conv_low = lax.optimization_barrier((low_pack, conv_low))
+    low_low = lax.psum_scatter(low_pack, "img", scatter_dimension=0, tiled=True)
 
     level_rows = jnp.concatenate(
         [level_sums[k][0:1] for k in range(4)] + [level_sums[k][1:2] for k in range(4)]
@@ -1658,8 +1650,6 @@
         dy, hidden, slope, fc1_weight, fc2_weight, x1, attended, proj_weight, p768,
         s384, s192, s256, level_rows, hots, core, shards,
     )
-    settle(moving, dout)
-    one, two = pyramid_sum.lanes()
     three, four = Halving(high_keep, high_send), Halving(keep2, send2)
     tables = jnp.concatenate([tw, tr], axis=1)
 
@@ -1669,29 +1659,27 @@
             total_rows, heads, part, 2, grads,
         )
 
-    _, (dout, conv_low) = swap([(one, 1), (two, "y"), (three, 0), (four, 0)], (dout, conv_low))
+    _, dout = swap([(three, 0), (four, 0)], dout)
     dqkv, dtab = attend_part(dout, jnp.zeros((128, 256), F32), 0, None)
     settle([three, four], dtab)
     _, dtab = swap([(three, 1), (four, "y")], dtab)
     dqkv, dtab = attend_part(dout, dtab, 1, dqkv)
-    settle([one, two], dtab)
-    _, dtab = swap([(one, "y"), (two, 1)], dtab)
     last, dx, dx_far = qkv_back_call(
         all_tokens, dqkv, qkv_weight, dx1, p768, dtab, placed(head)
     )
+    last, low_low = lax.optimization_barrier((last, low_low))
     last_low = lax.psum_scatter(last, "img", scatter_dimension=0, tiled=True)
+    settle([three, four], last)
+    swap([(three, "y"), (four, 1)])
+    settle([three, four])
+    dx_far, _ = lax.optimization_barrier((dx_far, [h.terms for h in (three, four)]))
+    high_total, g_w2 = last_swap([three]), last_swap([four])
     for d in range(1, peers):
         part = dx_far[(d - 1) * count : d * count]
         dx = dx + lax.ppermute(part, "seq", [(i, (i - d) % peers) for i in range(peers)])
-    conv_low, _ = lax.optimization_barrier((conv_low, last))
-    conv_total = seq_total(conv_low)
-    settle([one, two, three, four], last)
-    swap([(three, "y"), (four, 1)])
-    settle([three, four])
-    low_total, high_total = last_swap([one, two]), last_swap([three])
-    g_w2 = last_swap([four])
-    last_low, low_total, high_total, g_w2 = lax.optimization_barrier(
-        (last_low, low_total, high_total, g_w2)
+    conv_total, low_total = seq_total(conv_low), seq_total(low_low)
+    last_low, conv_total, low_total, high_total, g_w2, dx = lax.optimization_barrier(
+        (last_low, conv_total, low_total, high_total, g_w2, dx)
     )
     last_total = seq_total(last_low)
 

time: 524 us -> 494 us (0.943)
  starting transfers between devices: 44.2 us -> 24.2 us
  other arithmetic: 47.9 us -> 36.9 us
    ppermute x9 -> x6, starting transfers between devices: 23.3 us -> 8.8 us  [last_swap(): total = total + lax.ppermute(part(mine ^ d), 'img', pairs).astype(F32)]
    ppermute x9 -> x6, waiting for transfers between devices: 25 us -> 35.9 us  [last_swap(): total = total + lax.ppermute(part(mine ^ d), 'img', pairs).astype(F32)]
    ppermute x1, waiting for transfers between devices: 9.36 us -> 0.01 us  [per_device(): lax.ppermute(part, 'seq', [(i, (i - d) % peers) for i in range(peers)])]
    ppermute x11 -> x6, starting transfers between devices: 11.1 us -> 3.42 us  [swap(): h.terms = [keep, lax.ppermute(flat(send), *h.route).reshape(send.shape)]]
    ppermute x2 -> x3, waiting for transfers between devices: 6.77 us -> 13.4 us  [seq_total(): other = lax.ppermute(part, 'seq', [(0, 1), (1, 0)])]
    convert_element_type x8 -> x4, other arithmetic: 16.2 us -> 9.8 us  [half(): return (parts[0].astype(F32) + parts[1].astype(F32)).astype(BF)]
    ppermute x11 -> x6, waiting for transfers between devices: 14.6 us -> 13.9 us  [swap(): h.terms = [keep, lax.ppermute(flat(send), *h.route).reshape(send.shape)]]
  transfers between devices with their start and end apart: 31 -> 24, of which waited for: 14 -> 11; matrix products, arithmetic and copies ran while one was open for 14% -> 12% of each run, Pallas kernels for 31% -> 34%
where the time goes in v3:
time: 494 us; the launch traced here: 484 us
  Pallas kernels  298 us (60%)
  waiting for transfers between devices  70.9 us (14%)
  local copies, waits for them, and re-layouts  38.8 us (8%)
  other arithmetic  36.9 us (7%)
  starting transfers between devices  24.2 us (5%)
  between operations  15.8 us (3%)
    pallas_call x4, Pallas kernels, conv_call(): call(functools.partial(conv_kernel, level, block), [sds((rows * cols, cha...  71.4 us
    pallas_call x1, Pallas kernels, pyramid_back_call(): call(functools.partial(pyramid_back_kernel, lr, cols), [sds((tokens, widt...  45.3 us
    ppermute x6, waiting for transfers between devices, last_swap(): total = total + lax.ppermute(part(mine ^ d), 'img', pairs).astype(F32)  35.9 us
    pallas_call x2, Pallas kernels, attend_back_call(): call(functools.partial(attend_back_kernel, total_rows, scale, sources), [...  33.5 us
    pallas_call x4, Pallas kernels, conv_back_call(): call(functools.partial(conv_back_kernel, ways, block), out, grid=(rows //...  31.9 us
    pallas_call x1, Pallas kernels, mlp_back_call(): call(functools.partial(mlp_back_kernel, shards), [sds((width // 2, hidden...  25.2 us
    pallas_call x1, Pallas kernels, attend_call(): call(functools.partial(attend_kernel, total_rows, scale, parts), [sds((to...  24.6 us
    pallas_call x1, Pallas kernels, pyramid_call(): call(functools.partial(pyramid_kernel, lr, cols), [sds((lr, 4, 4 * cols,...  20.5 us
  transfers between devices with their start and end apart: 24, of which 11 were waited for; matrix products, arithmetic and copies ran while one was open for 12% of the time, Pallas kernels for 34%

profile of v3, /device:TPU:0, one launch (start us, length us, event | category | flops | bytes accessed | tf_op | source)
XLA Modules:
  0.0 484.2 jit_solution(1697388986948636377)
XLA Ops:
  15.4 6.2 %qkv.2.refs_1_.refs_6_.refs_8_.refs_10_.refs_12_ = bf16[512,2304]{1,0:T(8,128)(2,1)} custom-call(bf16[512,768]{1,0:T(8,128)(2,1)} %bitcast.148, bf16[768,2304]{1,0:T(8,128)(2,1)} %w_ref.5, f32[3,1,768]{2,1,0:T(1,128)} %maximum_convert_fusion.2.b_ref, f32[8,768]{1,0:T(8,128)} %convert_element_type.337.p_ref), custom_call_target="tpu_custom_call" | custom-call | flops 18119392 | tf_op jit(solution)/shard_map/qkv/pallas_call | solution.py:155
  32.1 4.6 qkv.3.refs_7_.refs_9_.refs_11_.refs_13_
  36.6 24.6 %attend.1 = (bf16[512,768]{1,0:T(8,128)(2,1)}, bf16[12,512,256]{2,1,0:T(8,128)(2,1)}, f32[6,2,512]{2,1,0:T(2,128)}) custom-call(s32[1]{0:T(128)} %bitcast.1.refs_0_, bf16[512,2304]{1,0:T(8,128)(2,1)} %qkv.2.refs_1_.refs_6_.refs_8_.refs_10_.refs_12_, bf16[128,128]{1,0:T(8,128)(2,1)} %pad_maximum_fusion.6.refs_2_, bf16[128,128]{1,0:T(8,128)(2,1)} %pad_maximum_fusion.7.refs_3_, ...), custom_call_target="tpu_custom_call" | custom-call | flops 250000000 | tf_op jit(solution)/shard_map/attend/pallas_call | solution.py:305
  61.2 14.0 %mlp.1 = (f32[512,768]{1,0:T(8,128)}, bf16[512,3072]{1,0:T(8,128)(2,1)}, bf16[512,3072]{1,0:T(8,128)(2,1)}, bf16[512,768]{1,0:T(8,128)(2,1)}) custom-call(bf16[512,768]{1,0:T(8,128)(2,1)} %bitcast.149, bf16[512,768]{1,0:T(8,128)(2,1)} %get-tuple-element.139.o_ref.refs_4_, bf16[768,768]{1,0:T(8,128)(2,1)} %wp_ref.3, bf16[768,3072]{1,0:T(8,128)(2,1)} %w1_ref.3, ...), custom_call_target="tpu_custom_call" | custom-call | flops 140000000 | tf_op jit(solution)/shard_map/mlp/pallas_call | solution.py:370
  75.2 20.5 %pyramid.1 = (bf16[8,4,256,256]{3,2,1,0:T(8,128)(2,1)}, bf16[8,2,128,256]{3,2,1,0:T(8,128)(2,1)}, bf16[512,256]{1,0:T(8,128)(2,1)}, bf16[128,256]{1,0:T(8,128)(2,1)}) custom-call(bf16[512,768]{1,0:T(8,128)(2,1)} %get-tuple-element.141.y_ref, bf16[768,1536]{1,0:T(8,128)(2,1)} %ff_ref.3, bf16[768,384]{1,0:T(8,128)(2,1)} %fs_ref.3, bf16[768,1536]{1,0:T(8,128)(2,1)} %mu_ref.3, ...), custom_call_target="tpu_custom_call" | custom-call | flops 200000000 | tf_op jit(solution)/shard_map/pyramid/pallas_call | solution.py:506
  99.3 5.1 %copy.122 = bf16[4,2304,256]{2,1,0:T(8,128)(2,1)} copy(bf16[4,2304,256]{2,0,1:T(4,128)(2,1)} %bitcast.155) | data formatting | bytes 9437184 | tf_op jit(solution)/shard_map/transpose | solution.py:1597
  109.4 5.8 %conv3.1 = (bf16[128,256]{1,0:T(8,128)(2,1)}, bf16[128,256]{1,0:T(8,128)(2,1)}, bf16[2304,1024]{1,0:T(8,128)(2,1)}, f32[8,256]{1,0:T(8,128)}) custom-call(bf16[4,32,256]{2,1,0:T(8,128)(2,1)} %bitcast.179, bf16[2,32,256]{2,1,0:T(8,128)(2,1)} %pad_maximum_fusion.5.rim_ref, bf16[4,3,768,256]{3,2,1,0:T(8,128)(2,1)} %bitcast.138, bf16[128,256]{1,0:T(8,128)(2,1)} %bitcast.180, ...), custom_call_target="tpu_custom_call" | custom-call | flops 3774873 | tf_op jit(solution)/shard_map/conv3/pallas_call | solution.py:646
  115.2 7.3 %conv2.1 = (bf16[512,256]{1,0:T(8,128)(2,1)}, bf16[512,256]{1,0:T(8,128)(2,1)}, bf16[2304,1024]{1,0:T(8,128)(2,1)}, f32[8,256]{1,0:T(8,128)}) custom-call(bf16[8,64,256]{2,1,0:T(8,128)(2,1)} %bitcast.175, bf16[2,64,256]{2,1,0:T(8,128)(2,1)} %fusion.39.rim_ref, bf16[4,3,768,256]{3,2,1,0:T(8,128)(2,1)} %bitcast.139, ...), custom_call_target="tpu_custom_call", output_to_operand_aliasing={{2}: (5, {})} | custom-call | flops 15099494 | tf_op jit(solution)/shard_map/conv2/pallas_call | solution.py:646
  122.4 15.4 %conv1.1 = (bf16[2048,256]{1,0:T(8,128)(2,1)}, bf16[2048,256]{1,0:T(8,128)(2,1)}, bf16[2304,1024]{1,0:T(8,128)(2,1)}, f32[8,256]{1,0:T(8,128)}) custom-call(bf16[16,128,256]{2,1,0:T(8,128)(2,1)} %bitcast.166, bf16[2,128,256]{2,1,0:T(8,128)(2,1)} %fusion.37.rim_ref, bf16[4,3,768,256]{3,2,1,0:T(8,128)(2,1)} %bitcast.140, ...), custom_call_target="tpu_custom_call", output_to_operand_aliasing={{2}: (5, {})} | custom-call | flops 60397976 | tf_op jit(solution)/shard_map/conv1/pallas_call | solution.py:646
  137.8 42.9 %conv0.1 = (bf16[8192,256]{1,0:T(8,128)(2,1)}, bf16[8192,256]{1,0:T(8,128)(2,1)}, bf16[2304,1024]{1,0:T(8,128)(2,1)}, f32[8,256]{1,0:T(8,128)}) custom-call(bf16[32,256,256]{2,1,0:T(8,128)(2,1)} %bitcast.154, bf16[2,256,256]{2,1,0:T(8,128)(2,1)} %fusion.27.rim_ref, bf16[4,3,768,256]{3,2,1,0:T(8,128)(2,1)} %bitcast.141, ...), custom_call_target="tpu_custom_call", output_to_operand_aliasing={{2}: (5, {})} | custom-call | flops 241591904 | tf_op jit(solution)/shard_map/conv0/pallas_call | solution.py:646
  199.5 7.0 %conv_back1.1.dzm_ref = bf16[2,2,512,256]{3,2,1,0:T(8,128)(2,1)} custom-call(bf16[16,128,256]{2,1,0:T(8,128)(2,1)} %bitcast.167, bf16[2,128,256]{2,1,0:T(8,128)(2,1)} %fusion.36.rim_ref, bf16[4,3,768,256]{3,2,1,0:T(8,128)(2,1)} %bitcast.144), custom_call_target="tpu_custom_call" | custom-call | flops 36238784 | tf_op jit(solution)/shard_map/conv_back1/pallas_call | solution.py:727
  206.5 19.0 %conv_back0.1 = bf16[4,4,512,256]{3,2,1,0:T(8,128)(2,1)} custom-call(bf16[32,256,256]{2,1,0:T(8,128)(2,1)} %bitcast.152, bf16[2,256,256]{2,1,0:T(8,128)(2,1)} %fusion.26.rim_ref, bf16[4,3,768,256]{3,2,1,0:T(8,128)(2,1)} %bitcast.145), custom_call_target="tpu_custom_call" | custom-call | flops 144955152 | tf_op jit(solution)/shard_map/conv_back0/pallas_call | solution.py:727
  225.5 45.3 %pyramid_back.1 = (f32[512,768]{1,0:T(8,128)}, bf16[768,4224]{1,0:T(8,128)(2,1)}, f32[8,384]{1,0:T(8,128)}, f32[8,192]{1,0:T(8,128)}, f32[16,256]{1,0:T(8,128)}) custom-call(bf16[512,768]{1,0:T(8,128)(2,1)} %get-tuple-element.141.y_ref, bf16[768,1536]{1,0:T(8,128)(2,1)} %ff_ref.3, bf16[768,384]{1,0:T(8,128)(2,1)} %fs_ref.3, bf16[768,1536]{1,0:T(8,128)(2,1)} %mu_ref.3, ...), custom_call_target="tpu_custom_call" | custom-call | flops 450000000 | tf_op jit(solution)/shard_map/pyramid_back/pallas_call | solution.py:904
  274.6 25.2 %mlp_back.1 = (bf16[384,3968]{1,0:T(8,128)(2,1)}, bf16[384,3968]{1,0:T(8,128)(2,1)}, bf16[1536,768]{1,0:T(8,128)(2,1)}, bf16[1536,768]{1,0:T(8,128)(2,1)}, f32[512,768]{1,0:T(8,128)}, /*index=5*/bf16[512,768]{1,0:T(8,128)(2,1)}) custom-call(s32[1]{0:T(128)} %bitcast.40.core_ref, f32[512,768]{1,0:T(8,128)} %get-tuple-element.173.dy_ref, ...), custom_call_target="tpu_custom_call" | custom-call | flops 250000000 | tf_op jit(solution)/shard_map/mlp_back/pallas_call | solution.py:1076
  301.7 17.0 %attend_back.2 = (bf16[3,1024,768]{2,1,0:T(8,128)(2,1)}, f32[128,256]{1,0:T(8,128)}) custom-call(s32[1]{0:T(128)} %bitcast.1.refs_0_, bf16[512,2304]{1,0:T(8,128)(2,1)} %qkv.2.refs_1_.refs_6_.refs_8_.refs_10_.refs_12_, bf16[12,512,256]{2,1,0:T(8,128)(2,1)} %get-tuple-element.161.refs_2_, bf16[512,768]{1,0:T(8,128)(2,1)} %get-tuple-element.191.refs_3_, ...), custom_call_target="tpu_custom_call" | custom-call | flops 150000000 | tf_op jit(solution)/shard_map/attend_back/pallas_call | solution.py:1252
  320.4 4.3 fusion.4
  331.4 16.5 %attend_back.3 = (bf16[3,1024,768]{2,1,0:T(8,128)(2,1)}, f32[128,256]{1,0:T(8,128)}) custom-call(s32[1]{0:T(128)} %bitcast.1.refs_0_, bf16[512,2304]{1,0:T(8,128)(2,1)} %qkv.2.refs_1_.refs_6_.refs_8_.refs_10_.refs_12_, bf16[12,512,256]{2,1,0:T(8,128)(2,1)} %get-tuple-element.161.refs_2_, ...), custom_call_target="tpu_custom_call", output_to_operand_aliasing={{0}: (14, {})} | custom-call | flops 150000000 | tf_op jit(solution)/shard_map/attend_back/pallas_call | solution.py:1252
  347.9 20.4 %qkv_back.1 = (bf16[768,2688]{1,0:T(8,128)(2,1)}, f32[512,768]{1,0:T(8,128)}, bf16[512,768]{1,0:T(8,128)(2,1)}) custom-call(bf16[1024,768]{1,0:T(8,128)(2,1)} %pad_maximum_fusion.x_ref, bf16[3,1024,768]{2,1,0:T(8,128)(2,1)} %get-tuple-element.204.dqkv_ref, bf16[768,2304]{1,0:T(8,128)(2,1)} %w_ref.5, f32[512,768]{1,0:T(8,128)} %get-tuple-element.205.dx1_ref, ...), custom_call_target="tpu_custom_call" | custom-call | flops 80000000 | tf_op jit(solution)/shard_map/qkv_back/pallas_call | solution.py:1359
  370.6 7.0 %collective-permute-done.5 = bf16[144,1024]{1,0:T(8,128)(2,1)} collective-permute-done((bf16[144,1024]{1,0:T(8,128)(2,1)S(1)}, bf16[144,1024]{1,0:T(8,128)(2,1)}, u32[]{:S(2)}, u32[]{:S(2)}) %collective-permute-start.5) | collective-permute-done | bytes 294944 | tf_op jit(solution)/shard_map/ppermute | solution.py:1504
  385.1 6.4 %collective-permute-done.6 = bf16[48,4224]{1,0:T(8,128)(2,1)S(1)} collective-permute-done((bf16[48,4224]{1,0:T(8,128)(2,1)}, bf16[48,4224]{1,0:T(8,128)(2,1)S(1)}, u32[]{:S(2)}, u32[]{:S(2)}) %collective-permute-start.6) | collective-permute-done | bytes 405536 | tf_op jit(solution)/shard_map/ppermute | solution.py:1504
  391.5 6.5 %collective-permute-done.10 = bf16[384,768]{1,0:T(8,128)(2,1)S(1)} collective-permute-done((bf16[384,768]{1,0:T(8,128)(2,1)S(1)}, bf16[384,768]{1,0:T(8,128)(2,1)S(1)}, u32[]{:S(2)}, u32[]{:S(2)}) %collective-permute-start.10) | collective-permute-done | bytes 589856 | tf_op jit(solution)/shard_map/ppermute | solution.py:1456
  398.0 7.4 %collective-permute-done.9 = bf16[96,3968]{1,0:T(8,128)(2,1)S(1)} collective-permute-done((bf16[96,3968]{1,0:T(8,128)(2,1)S(1)}, bf16[96,3968]{1,0:T(8,128)(2,1)S(1)}, u32[]{:S(2)}, u32[]{:S(2)}) %collective-permute-start.9) | collective-permute-done | bytes 761888 | tf_op jit(solution)/shard_map/ppermute | solution.py:1456
  412.4 10.5 %collective-permute-done.15 = bf16[96,768]{1,0:T(8,128)(2,1)S(1)} collective-permute-done((bf16[96,768]{1,0:T(8,128)(2,1)S(1)}, bf16[96,768]{1,0:T(8,128)(2,1)S(1)}, u32[]{:S(2)}, u32[]{:S(2)}) %collective-permute-start.15) | collective-permute-done | bytes 147488 | tf_op jit(solution)/shard_map/ppermute | solution.py:1484
  432.1 21.4 %collective-permute-done.12 = bf16[24,3968]{1,0:T(8,128)(2,1)S(1)} collective-permute-done((bf16[24,3968]{1,0:T(8,128)(2,1)S(1)}, bf16[24,3968]{1,0:T(8,128)(2,1)S(1)}, u32[]{:S(2)}, u32[]{:S(2)}) %collective-permute-start.12) | collective-permute-done | bytes 190496 | tf_op jit(solution)/shard_map/ppermute | solution.py:1484
  (218 shorter events, 108.3 us)
Async XLA Ops:
  7.2 263.6 %reduce-scatter.4.cloned.1.call-start = ((), (), s32[]{:S(2)}) async-start(), calls=%async_computation.3 | async-start | bytes 5013504 | tf_op jit(solution)/shard_map/reduce_scatter | solution.py:1610
  7.2 23.9 %collective-permute-start = (bf16[512,768]{1,0:T(8,128)(2,1)}, bf16[512,768]{1,0:T(8,128)(2,1)S(1)}, u32[]{:S(2)}, u32[]{:S(2)}) collective-permute-start(bf16[512,768]{1,0:T(8,128)(2,1)} %bitcast.147), channel_id=1, source_target_pairs={{0,1},{1,0},{2,3},{3,2},{4,5},{5,4},{6,7},{7,6},{8,9},{9,8},{10,11... | collective-permute-start | bytes 2359304 | tf_op jit(solution)/shard_map/ppermute | solution.py:1530
  99.2 7.5 %collective-permute-start.1 = (bf16[480,256]{1,0:T(8,128)(2,1)S(1)}, bf16[480,256]{1,0:T(8,128)(2,1)S(1)}, u32[]{:S(2)}, u32[]{:S(2)}) collective-permute-start(bf16[480,256]{1,0:T(8,128)(2,1)S(1)} %maximum_select_fusion), channel_id=1, source_target_pairs={{0,1},{1,0},{2,3},{3,2},{4,5},{5,4},{6,7},{7,6},{8,9},{9,8},{10,11... | collective-permute-start | bytes 737288 | tf_op jit(solution)/shard_map/ppermute | solution.py:1404
  180.8 187.6 %reduce-scatter.6.cloned.1.call-start = ((), (), s32[]{:S(2)}) async-start(), calls=%async_computation.4 | async-start | bytes 6893568 | tf_op jit(solution)/shard_map/reduce_scatter | solution.py:1644
  184.3 6.6 %collective-permute-start.2 = (bf16[480,256]{1,0:T(8,128)(2,1)S(1)}, bf16[480,256]{1,0:T(8,128)(2,1)S(1)}, u32[]{:S(2)}, u32[]{:S(2)}) collective-permute-start(bf16[480,256]{1,0:T(8,128)(2,1)S(1)} %maximum_select_fusion.1), channel_id=1, source_target_pairs={{0,1},{1,0},{2,3},{3,2},{4,5},{5,4},{6,7},{7,6},{8,9},{9,8},{10,11... | collective-permute-start | bytes 737288 | tf_op jit(solution)/shard_map/ppermute | solution.py:1404
  270.8 189.9 %reduce-scatter.8.cloned.1.call-start = ((), (), s32[]{:S(2)}) async-start(), calls=%async_computation.5 | async-start | bytes 4386816 | tf_op jit(solution)/shard_map/reduce_scatter | solution.py:1671
  299.8 18.9 %collective-permute-start.3 = (bf16[384,3968]{1,0:T(8,128)(2,1)}, bf16[384,3968]{1,0:T(8,128)(2,1)S(1)}, u32[]{:S(2)}, u32[]{:S(2)}) collective-permute-start(bf16[384,3968]{1,0:T(8,128)(2,1)} %get-tuple-element.186), channel_id=1, source_target_pairs={{0,2},{2,0},{4,6},{6,4},{8,10},{10,8},{12,14},{14,12},{16,18},{18,... | collective-permute-start | bytes 9142280 | tf_op jit(solution)/shard_map/ppermute | solution.py:1456
  299.9 18.8 %collective-permute-start.4 = (bf16[1536,768]{1,0:T(8,128)(2,1)}, bf16[1536,768]{1,0:T(8,128)(2,1)}, u32[]{:S(2)}, u32[]{:S(2)}) collective-permute-start(bf16[1536,768]{1,0:T(8,128)(2,1)} %get-tuple-element.187), channel_id=1, source_target_pairs={{0,2},{2,0},{4,6},{6,4},{8,10},{10,8},{12,14},{14,12},{16,18},{18,... | collective-permute-start | bytes 7077896 | tf_op jit(solution)/shard_map/ppermute | solution.py:1456
  327.2 51.6 %collective-permute-start.7 = (bf16[192,3968]{1,0:T(8,128)(2,1)}, bf16[192,3968]{1,0:T(8,128)(2,1)}, u32[]{:S(2)}, u32[]{:S(2)}) collective-permute-start(bf16[192,3968]{1,0:T(8,128)(2,1)} %bitcast.62), channel_id=1, source_target_pairs={{0,4},{2,6},{4,0},{6,2},{8,12},{10,14},{12,8},{14,10},{16,20},{18,... | collective-permute-start | bytes 4571144 | tf_op jit(solution)/shard_map/ppermute | solution.py:1456
  328.5 50.3 %collective-permute-start.8 = (bf16[768,768]{1,0:T(8,128)(2,1)}, bf16[768,768]{1,0:T(8,128)(2,1)}, u32[]{:S(2)}, u32[]{:S(2)}) collective-permute-start(bf16[768,768]{1,0:T(8,128)(2,1)} %bitcast.64), channel_id=1, source_target_pairs={{0,1},{1,0},{2,3},{3,2},{4,5},{5,4},{6,7},{7,6},{8,9},{9,8},{10,11... | collective-permute-start | bytes 3538952 | tf_op jit(solution)/shard_map/ppermute | solution.py:1456
  369.3 8.4 %collective-permute-start.5 = (bf16[144,1024]{1,0:T(8,128)(2,1)S(1)}, bf16[144,1024]{1,0:T(8,128)(2,1)}, u32[]{:S(2)}, u32[]{:S(2)}) collective-permute-start(bf16[144,1024]{1,0:T(8,128)(2,1)S(1)} %copy-done.9), channel_id=1, source_target_pairs={{0,1},{1,0},{2,3},{3,2},{4,5},{5,4},{6,7},{7,6},{8,9},{9,8},{10,11... | collective-permute-start | bytes 884744 | tf_op jit(solution)/shard_map/ppermute | solution.py:1504
  378.8 12.6 %collective-permute-start.6 = (bf16[48,4224]{1,0:T(8,128)(2,1)}, bf16[48,4224]{1,0:T(8,128)(2,1)S(1)}, u32[]{:S(2)}, u32[]{:S(2)}) collective-permute-start(bf16[48,4224]{1,0:T(8,128)(2,1)} %reduce-scatter.6.cloned.1.call-done), channel_id=1, source_target_pairs={{0,1},{1,0},{2,3},{3,2},{4,5},{5,4},{6,7},{7,6},{8,9},{9,8},{10,11... | collective-permute-start | bytes 1216520 | tf_op jit(solution)/shard_map/ppermute | solution.py:1504
  384.2 21.2 %collective-permute-start.9 = (bf16[96,3968]{1,0:T(8,128)(2,1)S(1)}, bf16[96,3968]{1,0:T(8,128)(2,1)S(1)}, u32[]{:S(2)}, u32[]{:S(2)}) collective-permute-start(bf16[96,3968]{1,0:T(8,128)(2,1)S(1)} %bitcast.169), channel_id=1, source_target_pairs={{0,1},{1,0},{2,3},{3,2},{4,5},{5,4},{6,7},{7,6},{8,9},{9,8},{10,11... | collective-permute-start | bytes 2285576 | tf_op jit(solution)/shard_map/ppermute | solution.py:1456
  384.6 13.4 %collective-permute-start.10 = (bf16[384,768]{1,0:T(8,128)(2,1)S(1)}, bf16[384,768]{1,0:T(8,128)(2,1)S(1)}, u32[]{:S(2)}, u32[]{:S(2)}) collective-permute-start(bf16[384,768]{1,0:T(8,128)(2,1)S(1)} %bitcast.174), channel_id=1, source_target_pairs={{0,4},{2,6},{4,0},{6,2},{8,12},{10,14},{12,8},{14,10},{16,20},{18,... | collective-permute-start | bytes 1769480 | tf_op jit(solution)/shard_map/ppermute | solution.py:1456
  405.4 54.0 %collective-permute-start.19 = (bf16[512,768]{1,0:T(8,128)(2,1)S(1)}, bf16[512,768]{1,0:T(8,128)(2,1)S(1)}, u32[]{:S(2)}, u32[]{:S(2)}) collective-permute-start(bf16[512,768]{1,0:T(8,128)(2,1)S(1)} %copy-done.21), channel_id=1, source_target_pairs={{0,1},{1,0},{2,3},{3,2},{4,5},{5,4},{6,7},{7,6},{8,9},{9,8},{10,11... | collective-permute-start | bytes 2359304 | tf_op jit(solution)/shard_map/ppermute | solution.py:1679
  407.3 15.6 %collective-permute-start.15 = (bf16[96,768]{1,0:T(8,128)(2,1)S(1)}, bf16[96,768]{1,0:T(8,128)(2,1)S(1)}, u32[]{:S(2)}, u32[]{:S(2)}) collective-permute-start(bf16[96,768]{1,0:T(8,128)(2,1)S(1)} %get-tuple-element.425), channel_id=1, source_target_pairs={{0,8},{2,10},{4,12},{6,14},{8,0},{10,2},{12,4},{14,6},{16,24},{18,... | collective-permute-start | bytes 442376 | tf_op jit(solution)/shard_map/ppermute | solution.py:1484
  408.7 18.8 %collective-permute-start.16 = (bf16[96,768]{1,0:T(8,128)(2,1)S(1)}, bf16[96,768]{1,0:T(8,128)(2,1)S(1)}, u32[]{:S(2)}, u32[]{:S(2)}) collective-permute-start(bf16[96,768]{1,0:T(8,128)(2,1)S(1)} %get-tuple-element.427), channel_id=1, source_target_pairs={{0,16},{2,18},{4,20},{6,22},{8,24},{10,26},{12,28},{14,30},{16,0},... | collective-permute-start | bytes 442376 | tf_op jit(solution)/shard_map/ppermute | solution.py:1484
  411.5 19.2 %collective-permute-start.17 = (bf16[96,768]{1,0:T(8,128)(2,1)S(1)}, bf16[96,768]{1,0:T(8,128)(2,1)S(1)}, u32[]{:S(2)}, u32[]{:S(2)}) collective-permute-start(bf16[96,768]{1,0:T(8,128)(2,1)S(1)} %get-tuple-element.426), channel_id=1, source_target_pairs={{0,24},{2,26},{4,28},{6,30},{8,16},{10,18},{12,20},{14,22},{16,8},... | collective-permute-start | bytes 442376 | tf_op jit(solution)/shard_map/ppermute | solution.py:1484
  411.9 20.2 %collective-permute-start.11 = (bf16[24,3968]{1,0:T(8,128)(2,1)S(1)}, bf16[24,3968]{1,0:T(8,128)(2,1)S(1)}, u32[]{:S(2)}, u32[]{:S(2)}) collective-permute-start(bf16[24,3968]{1,0:T(8,128)(2,1)S(1)} %get-tuple-element.422), channel_id=1, source_target_pairs={{0,8},{2,10},{4,12},{6,14},{8,0},{10,2},{12,4},{14,6},{16,24},{18,... | collective-permute-start | bytes 571400 | tf_op jit(solution)/shard_map/ppermute | solution.py:1484
  422.9 30.6 %collective-permute-start.12 = (bf16[24,3968]{1,0:T(8,128)(2,1)S(1)}, bf16[24,3968]{1,0:T(8,128)(2,1)S(1)}, u32[]{:S(2)}, u32[]{:S(2)}) collective-permute-start(bf16[24,3968]{1,0:T(8,128)(2,1)S(1)} %get-tuple-element.424), channel_id=1, source_target_pairs={{0,16},{2,18},{4,20},{6,22},{8,24},{10,26},{12,28},{14,30},{16,0},... | collective-permute-start | bytes 571400 | tf_op jit(solution)/shard_map/ppermute | solution.py:1484
  427.5 26.0 %collective-permute-start.13 = (bf16[24,3968]{1,0:T(8,128)(2,1)S(1)}, bf16[24,3968]{1,0:T(8,128)(2,1)S(1)}, u32[]{:S(2)}, u32[]{:S(2)}) collective-permute-start(bf16[24,3968]{1,0:T(8,128)(2,1)S(1)} %get-tuple-element.423), channel_id=1, source_target_pairs={{0,24},{2,26},{4,28},{6,30},{8,16},{10,18},{12,20},{14,22},{16,8},... | collective-permute-start | bytes 571400 | tf_op jit(solution)/shard_map/ppermute | solution.py:1484
  430.9 24.0 %collective-permute-start.18 = (bf16[96,768]{1,0:T(8,128)(2,1)S(1)}, bf16[96,768]{1,0:T(8,128)(2,1)S(1)}, u32[]{:S(2)}, u32[]{:S(2)}) collective-permute-start(bf16[96,768]{1,0:T(8,128)(2,1)S(1)} %fusion.25), channel_id=1, source_target_pairs={{0,1},{1,0},{2,3},{3,2},{4,5},{5,4},{6,7},{7,6},{8,9},{9,8},{10,11... | collective-permute-start | bytes 442376 | tf_op jit(solution)/shard_map/ppermute | solution.py:1489
  453.6 5.7 %collective-permute-start.14 = (bf16[24,3968]{1,0:T(8,128)(2,1)S(1)}, bf16[24,3968]{1,0:T(8,128)(2,1)S(1)}, u32[]{:S(2)}, u32[]{:S(2)}) collective-permute-start(bf16[24,3968]{1,0:T(8,128)(2,1)S(1)} %fusion.22), channel_id=1, source_target_pairs={{0,1},{1,0},{2,3},{3,2},{4,5},{5,4},{6,7},{7,6},{8,9},{9,8},{10,11... | collective-permute-start | bytes 571400 | tf_op jit(solution)/shard_map/ppermute | solution.py:1489
  463.7 9.5 %collective-permute-start.20 = (bf16[48,2688]{1,0:T(8,128)(2,1)}, bf16[48,2688]{1,0:T(8,128)(2,1)S(1)}, u32[]{:S(2)}, u32[]{:S(2)}) collective-permute-start(bf16[48,2688]{1,0:T(8,128)(2,1)} %reduce-scatter.8.cloned.1.call-done), channel_id=1, source_target_pairs={{0,1},{1,0},{2,3},{3,2},{4,5},{5,4},{6,7},{7,6},{8,9},{9,8},{10,11... | collective-permute-start | bytes 774152 | tf_op jit(solution)/shard_map/ppermute | solution.py:1504
  (23 other events, 166.6 us)
Sparse Core Ops, SparseCore 0:
  180.9 75.8 reduce-scatter.3
  271.0 91.6 reduce-scatter.5
  368.5 86.3 reduce-scatter.7

commit v4 on v3

--- a/solution.py
+++ b/solution.py
@@ -580,6 +580,10 @@
     lax.fori_loop(0, block // group, move_group, 0)
 
 
+def conv_rows(rows, cols, block):
+    return min(block, max(1, (CONV_PIXELS if rows * cols > 4096 else CONV_PIXELS // 2) // cols))
+
+
 def conv_kernel(level, block, z_ref, rim_ref, w_ref, cot_ref, p_ref, *refs):
     map_ref, dr_ref, dw_ref, sums_ref, pad_ref, dwt_ref, gradt_ref = refs[-7:]
     step = pl.program_id(0)
@@ -589,13 +593,20 @@
     )
     gain = p_ref[4 + level : 5 + level, :]
     shift = p_ref[12 + level : 13 + level, :]
-    few = min(block, max(1, (CONV_PIXELS if rows * cols > 4096 else CONV_PIXELS // 2) // cols))
+    few = conv_rows(rows, cols, block)
     pixels = few * cols
 
     @pl.when(step == 0)
     def _():
         sums_ref[...] = jnp.zeros_like(sums_ref)
         dwt_ref[...] = jnp.zeros_like(dwt_ref)
+        gradt_ref[...] = jnp.zeros_like(gradt_ref)
+
+    def add_grad(row):
+        for a in range(3):
+            for b in range(3):
+                window = pad_ref[pl.ds(row + a, few), :, b * chan : (b + 1) * chan]
+                dwt_ref[3 * a + b] += mm(gradt_ref[...], window.reshape(pixels, chan))
 
     def forward(k, carry):
         sum_gain, sum_shift = carry
@@ -605,6 +616,7 @@
             part = mm(pad_ref[pl.ds(row + a, few)].reshape(pixels, 3 * chan), w_ref[0, a])
             result = part if result is None else result + part
         base = pl.multiple_of(k * pixels, pixels)
+        add_grad(jnp.maximum(row - few, 0))
         for q in range(0, pixels, 64):
             sl = pl.ds(base + q, 64)
             hat, inverse = stats(result[q : q + 64])
@@ -613,7 +625,7 @@
             sum_gain = sum_gain + rowsum(cot * hat)
             sum_shift = sum_shift + rowsum(cot)
             dr_ref[sl, :] = norm_back(cot * gain, hat, inverse).astype(BF)
-        gradt_ref[:, pl.ds(base, pixels)] = dr_ref[pl.ds(base, pixels), :].T
+        gradt_ref[...] = dr_ref[pl.ds(base, pixels), :].T
         return sum_gain, sum_shift
 
     zero = jnp.zeros((1, chan), F32)
@@ -621,17 +633,10 @@
     sums_ref[0:1, :] += sum_gain
     sums_ref[1:2, :] += sum_shift
 
-    def add_grad(k, carry):
-        a, b = lax.div(k, 3), lax.rem(k, 3)
-        lanes = pl.ds(pl.multiple_of(b * chan, chan), chan)
-        window = pad_ref[pl.ds(step * block + a, block), :, lanes].reshape(block * cols, chan)
-        dwt_ref[k] += mm(gradt_ref[...], window)
-        return carry
-
-    lax.fori_loop(0, 9, add_grad, 0)
-
     @pl.when(step == pl.num_programs(0) - 1)
     def _():
+        add_grad(rows - few)
+
         def turn(k, carry):
             dw_ref[pl.ds(pl.multiple_of(k * chan, chan), chan), :] = dwt_ref[k].T.astype(BF)
             return carry
@@ -669,7 +674,7 @@
         scratch=[
             pltpu.VMEM((rows + 2, cols, 3 * chan), BF),
             pltpu.VMEM((9, chan, chan), F32),
-            pltpu.VMEM((chan, block * cols), BF),
+            pltpu.VMEM((chan, conv_rows(rows, cols, block) * cols), BF),
         ],
         flops=5 * 9 * rows * cols * chan * chan,
         name=f"conv{level}",
@@ -1531,7 +1536,6 @@
         for d in range(1, peers)
     ]
     far_tokens = jnp.concatenate(far, axis=0) if len(far) > 1 else (far[0] if far else None)
-    all_tokens = jnp.concatenate([own_tokens] + far, axis=0)
 
     p768 = jnp.stack(
         [
@@ -1628,7 +1632,14 @@
     )
     place = (at == source).astype(BF)
     hots = (placed(chan), placed(half), placed(quart))
-    drims, hots, place = lax.optimization_barrier((drims, hots, place))
+    all_tokens = jnp.concatenate([own_tokens] + far, axis=0)
+    tables = jnp.concatenate([tw, tr], axis=1)
+    level_rows = jnp.concatenate(
+        [level_sums[k][0:1] for k in range(4)] + [level_sums[k][1:2] for k in range(4)]
+    )
+    drims, hots, place, all_tokens, tables, level_rows, head_hot = lax.optimization_barrier(
+        (drims, hots, place, all_tokens, tables, level_rows, placed(head))
+    )
     dzs = []
     for level, ways in enumerate((4, 2, 1, 1)):
         dr = drs[level]
@@ -1643,15 +1654,11 @@
     low_pack, conv_low = lax.optimization_barrier((low_pack, conv_low))
     low_low = lax.psum_scatter(low_pack, "img", scatter_dimension=0, tiled=True)
 
-    level_rows = jnp.concatenate(
-        [level_sums[k][0:1] for k in range(4)] + [level_sums[k][1:2] for k in range(4)]
-    )
     high_keep, high_send, keep2, send2, dx1, dout = mlp_back_call(
         dy, hidden, slope, fc1_weight, fc2_weight, x1, attended, proj_weight, p768,
         s384, s192, s256, level_rows, hots, core, shards,
     )
     three, four = Halving(high_keep, high_send), Halving(keep2, send2)
-    tables = jnp.concatenate([tw, tr], axis=1)
 
     def attend_part(dout_now, dtab, part, grads):
         return attend_back_call(
@@ -1665,14 +1672,16 @@
     _, dtab = swap([(three, 1), (four, "y")], dtab)
     dqkv, dtab = attend_part(dout, dtab, 1, dqkv)
     last, dx, dx_far = qkv_back_call(
-        all_tokens, dqkv, qkv_weight, dx1, p768, dtab, placed(head)
+        all_tokens, dqkv, qkv_weight, dx1, p768, dtab, head_hot
     )
     last, low_low = lax.optimization_barrier((last, low_low))
     last_low = lax.psum_scatter(last, "img", scatter_dimension=0, tiled=True)
     settle([three, four], last)
     swap([(three, "y"), (four, 1)])
     settle([three, four])
-    dx_far, _ = lax.optimization_barrier((dx_far, [h.terms for h in (three, four)]))
+    (dx_far, conv_low, low_low), _ = lax.optimization_barrier(
+        ((dx_far, conv_low, low_low), [h.terms for h in (three, four)])
+    )
     high_total, g_w2 = last_swap([three]), last_swap([four])
     for d in range(1, peers):
         part = dx_far[(d - 1) * count : d * count]

time: 494 us -> 484 us (0.980)
  Pallas kernels: 298 us -> 290 us
    ppermute x3, waiting for transfers between devices: 13.4 us -> 0.01 us  [seq_total(): other = lax.ppermute(part, 'seq', [(0, 1), (1, 0)])]
    reduce_scatter x1, waiting for transfers between devices: 0.01 us -> 8.71 us  [per_device(): last_low = lax.psum_scatter(last, 'img', scatter_dimension=0, tiled=True)]
    pallas_call x4, Pallas kernels: 71.4 us -> 64 us  [conv_call(): call(functools.partial(conv_kernel, level, block), [sds((rows * cols, cha...]
where the time goes in v4:
time: 484 us; the launch traced here: 475 us
  Pallas kernels  290 us (60%)
  waiting for transfers between devices  66.3 us (14%)
  other arithmetic  38.2 us (8%)
  local copies, waits for them, and re-layouts  37.4 us (8%)
  starting transfers between devices  26.8 us (6%)
  between operations  16 us (3%)
    pallas_call x4, Pallas kernels, conv_call(): call(functools.partial(conv_kernel, level, block), [sds((rows * cols, cha...  64 us
    pallas_call x1, Pallas kernels, pyramid_back_call(): call(functools.partial(pyramid_back_kernel, lr, cols), [sds((tokens, widt...  45.4 us
    ppermute x6, waiting for transfers between devices, last_swap(): total = total + lax.ppermute(part(mine ^ d), 'img', pairs).astype(F32)  33.6 us
    pallas_call x2, Pallas kernels, attend_back_call(): call(functools.partial(attend_back_kernel, total_rows, scale, sources), [...  33.3 us
    pallas_call x4, Pallas kernels, conv_back_call(): call(functools.partial(conv_back_kernel, ways, block), out, grid=(rows //...  31.9 us
    pallas_call x1, Pallas kernels, mlp_back_call(): call(functools.partial(mlp_back_kernel, shards), [sds((width // 2, hidden...  24.6 us
    pallas_call x1, Pallas kernels, attend_call(): call(functools.partial(attend_kernel, total_rows, scale, parts), [sds((to...  24.6 us
    pallas_call x1, Pallas kernels, qkv_back_call(): call(qkv_back_kernel, [sds((width, 3 * width + 384), BF), sds((rows, widt...  20.8 us
  transfers between devices with their start and end apart: 24, of which 11 were waited for; matrix products, arithmetic and copies ran while one was open for 12% of the time, Pallas kernels for 34%

profile of v4, /device:TPU:0, one launch (start us, length us, event | category | flops | bytes accessed | tf_op | source)
XLA Modules:
  0.0 474.9 jit_solution(3422595519019339521)
XLA Ops:
  15.4 6.2 %qkv.2.refs_1_.refs_6_.refs_8_.refs_10_.refs_12_ = bf16[512,2304]{1,0:T(8,128)(2,1)} custom-call(bf16[512,768]{1,0:T(8,128)(2,1)} %bitcast.148, bf16[768,2304]{1,0:T(8,128)(2,1)} %w_ref.5, f32[3,1,768]{2,1,0:T(1,128)} %maximum_convert_fusion.2.b_ref, f32[8,768]{1,0:T(8,128)} %convert_element_type.337.p_ref), custom_call_target="tpu_custom_call" | custom-call | flops 18119392 | tf_op jit(solution)/shard_map/qkv/pallas_call | solution.py:155
  32.1 4.6 qkv.3.refs_7_.refs_9_.refs_11_.refs_13_
  36.6 24.6 %attend.1 = (bf16[512,768]{1,0:T(8,128)(2,1)}, bf16[12,512,256]{2,1,0:T(8,128)(2,1)}, f32[6,2,512]{2,1,0:T(2,128)}) custom-call(s32[1]{0:T(128)} %bitcast.1.refs_0_, bf16[512,2304]{1,0:T(8,128)(2,1)} %qkv.2.refs_1_.refs_6_.refs_8_.refs_10_.refs_12_, bf16[128,128]{1,0:T(8,128)(2,1)} %pad_maximum_fusion.6.refs_2_, bf16[128,128]{1,0:T(8,128)(2,1)} %pad_maximum_fusion.7.refs_3_, ...), custom_call_target="tpu_custom_call" | custom-call | flops 250000000 | tf_op jit(solution)/shard_map/attend/pallas_call | solution.py:305
  61.2 14.1 %mlp.1 = (f32[512,768]{1,0:T(8,128)}, bf16[512,3072]{1,0:T(8,128)(2,1)}, bf16[512,3072]{1,0:T(8,128)(2,1)}, bf16[512,768]{1,0:T(8,128)(2,1)}) custom-call(bf16[512,768]{1,0:T(8,128)(2,1)} %bitcast.149, bf16[512,768]{1,0:T(8,128)(2,1)} %get-tuple-element.145.o_ref.refs_4_, bf16[768,768]{1,0:T(8,128)(2,1)} %wp_ref.3, bf16[768,3072]{1,0:T(8,128)(2,1)} %w1_ref.3, ...), custom_call_target="tpu_custom_call" | custom-call | flops 140000000 | tf_op jit(solution)/shard_map/mlp/pallas_call | solution.py:370
  75.4 20.8 %pyramid.1 = (bf16[8,4,256,256]{3,2,1,0:T(8,128)(2,1)}, bf16[8,2,128,256]{3,2,1,0:T(8,128)(2,1)}, bf16[512,256]{1,0:T(8,128)(2,1)}, bf16[128,256]{1,0:T(8,128)(2,1)}) custom-call(bf16[512,768]{1,0:T(8,128)(2,1)} %get-tuple-element.147.y_ref, bf16[768,1536]{1,0:T(8,128)(2,1)} %ff_ref.3, bf16[768,384]{1,0:T(8,128)(2,1)} %fs_ref.3, bf16[768,1536]{1,0:T(8,128)(2,1)} %mu_ref.3, ...), custom_call_target="tpu_custom_call" | custom-call | flops 200000000 | tf_op jit(solution)/shard_map/pyramid/pallas_call | solution.py:506
  99.7 5.1 %copy.122 = bf16[4,2304,256]{2,1,0:T(8,128)(2,1)} copy(bf16[4,2304,256]{2,0,1:T(4,128)(2,1)} %bitcast.155) | data formatting | bytes 9437184 | tf_op jit(solution)/shard_map/transpose | solution.py:1601
  109.7 4.9 %conv3.1 = (bf16[128,256]{1,0:T(8,128)(2,1)}, bf16[128,256]{1,0:T(8,128)(2,1)}, bf16[2304,1024]{1,0:T(8,128)(2,1)}, f32[8,256]{1,0:T(8,128)}) custom-call(bf16[4,32,256]{2,1,0:T(8,128)(2,1)} %bitcast.177, bf16[2,32,256]{2,1,0:T(8,128)(2,1)} %pad_maximum_fusion.5.rim_ref, bf16[4,3,768,256]{3,2,1,0:T(8,128)(2,1)} %bitcast.138, bf16[128,256]{1,0:T(8,128)(2,1)} %bitcast.178, ...), custom_call_target="tpu_custom_call" | custom-call | flops 3774873 | tf_op jit(solution)/shard_map/conv3/pallas_call | solution.py:651
  114.7 6.9 %conv2.1 = (bf16[512,256]{1,0:T(8,128)(2,1)}, bf16[512,256]{1,0:T(8,128)(2,1)}, bf16[2304,1024]{1,0:T(8,128)(2,1)}, f32[8,256]{1,0:T(8,128)}) custom-call(bf16[8,64,256]{2,1,0:T(8,128)(2,1)} %bitcast.173, bf16[2,64,256]{2,1,0:T(8,128)(2,1)} %fusion.39.rim_ref, bf16[4,3,768,256]{3,2,1,0:T(8,128)(2,1)} %bitcast.139, ...), custom_call_target="tpu_custom_call", output_to_operand_aliasing={{2}: (5, {})} | custom-call | flops 15099494 | tf_op jit(solution)/shard_map/conv2/pallas_call | solution.py:651
  121.6 14.1 %conv1.1 = (bf16[2048,256]{1,0:T(8,128)(2,1)}, bf16[2048,256]{1,0:T(8,128)(2,1)}, bf16[2304,1024]{1,0:T(8,128)(2,1)}, f32[8,256]{1,0:T(8,128)}) custom-call(bf16[16,128,256]{2,1,0:T(8,128)(2,1)} %bitcast.166, bf16[2,128,256]{2,1,0:T(8,128)(2,1)} %fusion.37.rim_ref, bf16[4,3,768,256]{3,2,1,0:T(8,128)(2,1)} %bitcast.140, ...), custom_call_target="tpu_custom_call", output_to_operand_aliasing={{2}: (5, {})} | custom-call | flops 60397976 | tf_op jit(solution)/shard_map/conv1/pallas_call | solution.py:651
  135.7 38.0 %conv0.1 = (bf16[8192,256]{1,0:T(8,128)(2,1)}, bf16[8192,256]{1,0:T(8,128)(2,1)}, bf16[2304,1024]{1,0:T(8,128)(2,1)}, f32[8,256]{1,0:T(8,128)}) custom-call(bf16[32,256,256]{2,1,0:T(8,128)(2,1)} %bitcast.154, bf16[2,256,256]{2,1,0:T(8,128)(2,1)} %fusion.27.rim_ref, bf16[4,3,768,256]{3,2,1,0:T(8,128)(2,1)} %bitcast.141, ...), custom_call_target="tpu_custom_call", output_to_operand_aliasing={{2}: (5, {})} | custom-call | flops 241591904 | tf_op jit(solution)/shard_map/conv0/pallas_call | solution.py:651
  197.5 6.9 %conv_back1.1.dzm_ref = bf16[2,2,512,256]{3,2,1,0:T(8,128)(2,1)} custom-call(bf16[16,128,256]{2,1,0:T(8,128)(2,1)} %bitcast.167, bf16[2,128,256]{2,1,0:T(8,128)(2,1)} %fusion.36.rim_ref, bf16[4,3,768,256]{3,2,1,0:T(8,128)(2,1)} %bitcast.144), custom_call_target="tpu_custom_call" | custom-call | flops 36238784 | tf_op jit(solution)/shard_map/conv_back1/pallas_call | solution.py:732
  204.3 19.0 %conv_back0.1 = bf16[4,4,512,256]{3,2,1,0:T(8,128)(2,1)} custom-call(bf16[32,256,256]{2,1,0:T(8,128)(2,1)} %bitcast.152, bf16[2,256,256]{2,1,0:T(8,128)(2,1)} %fusion.26.rim_ref, bf16[4,3,768,256]{3,2,1,0:T(8,128)(2,1)} %bitcast.145), custom_call_target="tpu_custom_call" | custom-call | flops 144955152 | tf_op jit(solution)/shard_map/conv_back0/pallas_call | solution.py:732
  223.4 45.4 %pyramid_back.1 = (f32[512,768]{1,0:T(8,128)}, bf16[768,4224]{1,0:T(8,128)(2,1)}, f32[8,384]{1,0:T(8,128)}, f32[8,192]{1,0:T(8,128)}, f32[16,256]{1,0:T(8,128)}) custom-call(bf16[512,768]{1,0:T(8,128)(2,1)} %get-tuple-element.147.y_ref, bf16[768,1536]{1,0:T(8,128)(2,1)} %ff_ref.3, bf16[768,384]{1,0:T(8,128)(2,1)} %fs_ref.3, bf16[768,1536]{1,0:T(8,128)(2,1)} %mu_ref.3, ...), custom_call_target="tpu_custom_call" | custom-call | flops 450000000 | tf_op jit(solution)/shard_map/pyramid_back/pallas_call | solution.py:909
  268.8 24.6 %mlp_back.1 = (bf16[384,3968]{1,0:T(8,128)(2,1)}, bf16[384,3968]{1,0:T(8,128)(2,1)}, bf16[1536,768]{1,0:T(8,128)(2,1)}, bf16[1536,768]{1,0:T(8,128)(2,1)}, f32[512,768]{1,0:T(8,128)}, /*index=5*/bf16[512,768]{1,0:T(8,128)(2,1)}) custom-call(s32[1]{0:T(128)} %bitcast.42.core_ref, f32[512,768]{1,0:T(8,128)} %get-tuple-element.183.dy_ref, ...), custom_call_target="tpu_custom_call" | custom-call | flops 250000000 | tf_op jit(solution)/shard_map/mlp_back/pallas_call | solution.py:1081
  294.7 16.9 %attend_back.2 = (bf16[3,1024,768]{2,1,0:T(8,128)(2,1)}, f32[128,256]{1,0:T(8,128)}) custom-call(s32[1]{0:T(128)} %bitcast.1.refs_0_, bf16[512,2304]{1,0:T(8,128)(2,1)} %qkv.2.refs_1_.refs_6_.refs_8_.refs_10_.refs_12_, bf16[12,512,256]{2,1,0:T(8,128)(2,1)} %get-tuple-element.177.refs_2_, bf16[512,768]{1,0:T(8,128)(2,1)} %get-tuple-element.199.refs_3_, ...), custom_call_target="tpu_custom_call" | custom-call | flops 150000000 | tf_op jit(solution)/shard_map/attend_back/pallas_call | solution.py:1257
  313.2 4.2 fusion.4
  322.6 16.5 %attend_back.3 = (bf16[3,1024,768]{2,1,0:T(8,128)(2,1)}, f32[128,256]{1,0:T(8,128)}) custom-call(s32[1]{0:T(128)} %bitcast.1.refs_0_, bf16[512,2304]{1,0:T(8,128)(2,1)} %qkv.2.refs_1_.refs_6_.refs_8_.refs_10_.refs_12_, bf16[12,512,256]{2,1,0:T(8,128)(2,1)} %get-tuple-element.177.refs_2_, ...), custom_call_target="tpu_custom_call", output_to_operand_aliasing={{0}: (14, {})} | custom-call | flops 150000000 | tf_op jit(solution)/shard_map/attend_back/pallas_call | solution.py:1257
  339.1 20.8 %qkv_back.1 = (bf16[768,2688]{1,0:T(8,128)(2,1)}, f32[512,768]{1,0:T(8,128)}, bf16[512,768]{1,0:T(8,128)(2,1)}) custom-call(bf16[1024,768]{1,0:T(8,128)(2,1)} %pad_maximum_fusion.x_ref, bf16[3,1024,768]{2,1,0:T(8,128)(2,1)} %get-tuple-element.213.dqkv_ref, bf16[768,2304]{1,0:T(8,128)(2,1)} %w_ref.5, f32[512,768]{1,0:T(8,128)} %get-tuple-element.214.dx1_ref, ...), custom_call_target="tpu_custom_call" | custom-call | flops 80000000 | tf_op jit(solution)/shard_map/qkv_back/pallas_call | solution.py:1364
  368.8 13.4 %collective-permute-done.8 = bf16[384,768]{1,0:T(8,128)(2,1)S(1)} collective-permute-done((bf16[384,768]{1,0:T(8,128)(2,1)}, bf16[384,768]{1,0:T(8,128)(2,1)S(1)}, u32[]{:S(2)}, u32[]{:S(2)}) %collective-permute-start.8) | collective-permute-done | bytes 589856 | tf_op jit(solution)/shard_map/ppermute | solution.py:1461
  395.5 8.0 %collective-permute-done.16 = bf16[96,768]{1,0:T(8,128)(2,1)S(1)} collective-permute-done((bf16[96,768]{1,0:T(8,128)(2,1)S(1)}, bf16[96,768]{1,0:T(8,128)(2,1)S(1)}, u32[]{:S(2)}, u32[]{:S(2)}) %collective-permute-start.16) | collective-permute-done | bytes 147488 | tf_op jit(solution)/shard_map/ppermute | solution.py:1489
  403.4 3.5 collective-permute-start.13
  408.3 3.8 collective-permute-done.11
  412.1 20.3 %collective-permute-done.12 = bf16[24,3968]{1,0:T(8,128)(2,1)S(1)} collective-permute-done((bf16[24,3968]{1,0:T(8,128)(2,1)S(1)}, bf16[24,3968]{1,0:T(8,128)(2,1)S(1)}, u32[]{:S(2)}, u32[]{:S(2)}) %collective-permute-start.12) | collective-permute-done | bytes 190496 | tf_op jit(solution)/shard_map/ppermute | solution.py:1489
  442.1 8.7 %reduce-scatter.8.cloned.1.call-done = bf16[48,2688]{1,0:T(8,128)(2,1)} async-done(((bf16[768,2688]{1,0:T(8,128)(2,1)}), bf16[48,2688]{1,0:T(8,128)(2,1)}) %reduce-scatter.8.cloned.1.call-update) | async-done | bytes 258064 | tf_op jit(solution)/shard_map/reduce_scatter | solution.py:1678
  (214 shorter events, 107.8 us)
Async XLA Ops:
  7.2 261.6 %reduce-scatter.4.cloned.1.call-start = ((), (), s32[]{:S(2)}) async-start(), calls=%async_computation.3 | async-start | bytes 5013504 | tf_op jit(solution)/shard_map/reduce_scatter | solution.py:1614
  7.2 24.0 %collective-permute-start = (bf16[512,768]{1,0:T(8,128)(2,1)}, bf16[512,768]{1,0:T(8,128)(2,1)S(1)}, u32[]{:S(2)}, u32[]{:S(2)}) collective-permute-start(bf16[512,768]{1,0:T(8,128)(2,1)} %bitcast.147), channel_id=1, source_target_pairs={{0,1},{1,0},{2,3},{3,2},{4,5},{5,4},{6,7},{7,6},{8,9},{9,8},{10,11... | collective-permute-start | bytes 2359304 | tf_op jit(solution)/shard_map/ppermute | solution.py:1535
  99.6 7.5 %collective-permute-start.1 = (bf16[480,256]{1,0:T(8,128)(2,1)S(1)}, bf16[480,256]{1,0:T(8,128)(2,1)S(1)}, u32[]{:S(2)}, u32[]{:S(2)}) collective-permute-start(bf16[480,256]{1,0:T(8,128)(2,1)S(1)} %maximum_select_fusion), channel_id=1, source_target_pairs={{0,1},{1,0},{2,3},{3,2},{4,5},{5,4},{6,7},{7,6},{8,9},{9,8},{10,11... | collective-permute-start | bytes 737288 | tf_op jit(solution)/shard_map/ppermute | solution.py:1409
  173.8 188.0 %reduce-scatter.6.cloned.1.call-start = ((), (), s32[]{:S(2)}) async-start(), calls=%async_computation.4 | async-start | bytes 6893568 | tf_op jit(solution)/shard_map/reduce_scatter | solution.py:1655
  179.2 9.6 %collective-permute-start.2 = (bf16[480,256]{1,0:T(8,128)(2,1)S(1)}, bf16[480,256]{1,0:T(8,128)(2,1)S(1)}, u32[]{:S(2)}, u32[]{:S(2)}) collective-permute-start(bf16[480,256]{1,0:T(8,128)(2,1)S(1)} %maximum_select_fusion.1), channel_id=1, source_target_pairs={{0,1},{1,0},{2,3},{3,2},{4,5},{5,4},{6,7},{7,6},{8,9},{9,8},{10,11... | collective-permute-start | bytes 737288 | tf_op jit(solution)/shard_map/ppermute | solution.py:1409
  268.8 182.0 %reduce-scatter.8.cloned.1.call-start = ((), (), s32[]{:S(2)}) async-start(), calls=%async_computation.5 | async-start | bytes 4386816 | tf_op jit(solution)/shard_map/reduce_scatter | solution.py:1678
  293.5 18.1 %collective-permute-start.3 = (bf16[384,3968]{1,0:T(8,128)(2,1)}, bf16[384,3968]{1,0:T(8,128)(2,1)S(1)}, u32[]{:S(2)}, u32[]{:S(2)}) collective-permute-start(bf16[384,3968]{1,0:T(8,128)(2,1)} %get-tuple-element.194), channel_id=1, source_target_pairs={{0,2},{2,0},{4,6},{6,4},{8,10},{10,8},{12,14},{14,12},{16,18},{18,... | collective-permute-start | bytes 9142280 | tf_op jit(solution)/shard_map/ppermute | solution.py:1461
  293.5 18.0 %collective-permute-start.4 = (bf16[1536,768]{1,0:T(8,128)(2,1)}, bf16[1536,768]{1,0:T(8,128)(2,1)}, u32[]{:S(2)}, u32[]{:S(2)}) collective-permute-start(bf16[1536,768]{1,0:T(8,128)(2,1)} %get-tuple-element.195), channel_id=1, source_target_pairs={{0,2},{2,0},{4,6},{6,4},{8,10},{10,8},{12,14},{14,12},{16,18},{18,... | collective-permute-start | bytes 7077896 | tf_op jit(solution)/shard_map/ppermute | solution.py:1461
  319.5 42.3 %collective-permute-start.5 = (bf16[192,3968]{1,0:T(8,128)(2,1)}, bf16[192,3968]{1,0:T(8,128)(2,1)}, u32[]{:S(2)}, u32[]{:S(2)}) collective-permute-start(bf16[192,3968]{1,0:T(8,128)(2,1)} %bitcast.62), channel_id=1, source_target_pairs={{0,4},{2,6},{4,0},{6,2},{8,12},{10,14},{12,8},{14,10},{16,20},{18,... | collective-permute-start | bytes 4571144 | tf_op jit(solution)/shard_map/ppermute | solution.py:1461
  321.1 40.7 %collective-permute-start.6 = (bf16[768,768]{1,0:T(8,128)(2,1)}, bf16[768,768]{1,0:T(8,128)(2,1)}, u32[]{:S(2)}, u32[]{:S(2)}) collective-permute-start(bf16[768,768]{1,0:T(8,128)(2,1)} %bitcast.64), channel_id=1, source_target_pairs={{0,1},{1,0},{2,3},{3,2},{4,5},{5,4},{6,7},{7,6},{8,9},{9,8},{10,11... | collective-permute-start | bytes 3538952 | tf_op jit(solution)/shard_map/ppermute | solution.py:1461
  366.8 17.8 %collective-permute-start.7 = (bf16[96,3968]{1,0:T(8,128)(2,1)}, bf16[96,3968]{1,0:T(8,128)(2,1)S(1)}, u32[]{:S(2)}, u32[]{:S(2)}) collective-permute-start(bf16[96,3968]{1,0:T(8,128)(2,1)} %bitcast.72), channel_id=1, source_target_pairs={{0,1},{1,0},{2,3},{3,2},{4,5},{5,4},{6,7},{7,6},{8,9},{9,8},{10,11... | collective-permute-start | bytes 2285576 | tf_op jit(solution)/shard_map/ppermute | solution.py:1461
  368.3 13.9 %collective-permute-start.8 = (bf16[384,768]{1,0:T(8,128)(2,1)}, bf16[384,768]{1,0:T(8,128)(2,1)S(1)}, u32[]{:S(2)}, u32[]{:S(2)}) collective-permute-start(bf16[384,768]{1,0:T(8,128)(2,1)} %bitcast.74), channel_id=1, source_target_pairs={{0,4},{2,6},{4,0},{6,2},{8,12},{10,14},{12,8},{14,10},{16,20},{18,... | collective-permute-start | bytes 1769480 | tf_op jit(solution)/shard_map/ppermute | solution.py:1461
  384.6 56.2 %collective-permute-start.19 = (bf16[512,768]{1,0:T(8,128)(2,1)}, bf16[512,768]{1,0:T(8,128)(2,1)S(1)}, u32[]{:S(2)}, u32[]{:S(2)}) collective-permute-start(bf16[512,768]{1,0:T(8,128)(2,1)} %get-tuple-element.244), channel_id=1, source_target_pairs={{0,1},{1,0},{2,3},{3,2},{4,5},{5,4},{6,7},{7,6},{8,9},{9,8},{10,11... | collective-permute-start | bytes 2359304 | tf_op jit(solution)/shard_map/ppermute | solution.py:1688
  386.2 6.7 %collective-permute-start.15 = (bf16[96,768]{1,0:T(8,128)(2,1)S(1)}, bf16[96,768]{1,0:T(8,128)(2,1)S(1)}, u32[]{:S(2)}, u32[]{:S(2)}) collective-permute-start(bf16[96,768]{1,0:T(8,128)(2,1)S(1)} %get-tuple-element.437), channel_id=1, source_target_pairs={{0,8},{2,10},{4,12},{6,14},{8,0},{10,2},{12,4},{14,6},{16,24},{18,... | collective-permute-start | bytes 442376 | tf_op jit(solution)/shard_map/ppermute | solution.py:1489
  387.7 15.8 %collective-permute-start.16 = (bf16[96,768]{1,0:T(8,128)(2,1)S(1)}, bf16[96,768]{1,0:T(8,128)(2,1)S(1)}, u32[]{:S(2)}, u32[]{:S(2)}) collective-permute-start(bf16[96,768]{1,0:T(8,128)(2,1)S(1)} %get-tuple-element.439), channel_id=1, source_target_pairs={{0,16},{2,18},{4,20},{6,22},{8,24},{10,26},{12,28},{14,30},{16,0},... | collective-permute-start | bytes 442376 | tf_op jit(solution)/shard_map/ppermute | solution.py:1489
  388.9 18.0 %collective-permute-start.17 = (bf16[96,768]{1,0:T(8,128)(2,1)S(1)}, bf16[96,768]{1,0:T(8,128)(2,1)S(1)}, u32[]{:S(2)}, u32[]{:S(2)}) collective-permute-start(bf16[96,768]{1,0:T(8,128)(2,1)S(1)} %get-tuple-element.438), channel_id=1, source_target_pairs={{0,24},{2,26},{4,28},{6,30},{8,16},{10,18},{12,20},{14,22},{16,8},... | collective-permute-start | bytes 442376 | tf_op jit(solution)/shard_map/ppermute | solution.py:1489
  390.8 21.3 %collective-permute-start.11 = (bf16[24,3968]{1,0:T(8,128)(2,1)S(1)}, bf16[24,3968]{1,0:T(8,128)(2,1)S(1)}, u32[]{:S(2)}, u32[]{:S(2)}) collective-permute-start(bf16[24,3968]{1,0:T(8,128)(2,1)S(1)} %get-tuple-element.434), channel_id=1, source_target_pairs={{0,8},{2,10},{4,12},{6,14},{8,0},{10,2},{12,4},{14,6},{16,24},{18,... | collective-permute-start | bytes 571400 | tf_op jit(solution)/shard_map/ppermute | solution.py:1489
  392.9 39.5 %collective-permute-start.12 = (bf16[24,3968]{1,0:T(8,128)(2,1)S(1)}, bf16[24,3968]{1,0:T(8,128)(2,1)S(1)}, u32[]{:S(2)}, u32[]{:S(2)}) collective-permute-start(bf16[24,3968]{1,0:T(8,128)(2,1)S(1)} %get-tuple-element.436), channel_id=1, source_target_pairs={{0,16},{2,18},{4,20},{6,22},{8,24},{10,26},{12,28},{14,30},{16,0},... | collective-permute-start | bytes 571400 | tf_op jit(solution)/shard_map/ppermute | solution.py:1489
  403.4 29.4 %collective-permute-start.13 = (bf16[24,3968]{1,0:T(8,128)(2,1)S(1)}, bf16[24,3968]{1,0:T(8,128)(2,1)S(1)}, u32[]{:S(2)}, u32[]{:S(2)}) collective-permute-start(bf16[24,3968]{1,0:T(8,128)(2,1)S(1)} %get-tuple-element.435), channel_id=1, source_target_pairs={{0,24},{2,26},{4,28},{6,30},{8,16},{10,18},{12,20},{14,22},{16,8},... | collective-permute-start | bytes 571400 | tf_op jit(solution)/shard_map/ppermute | solution.py:1489
  406.9 32.8 %collective-permute-start.10 = (bf16[48,4224]{1,0:T(8,128)(2,1)}, bf16[48,4224]{1,0:T(8,128)(2,1)S(1)}, u32[]{:S(2)}, u32[]{:S(2)}) collective-permute-start(bf16[48,4224]{1,0:T(8,128)(2,1)} %reduce-scatter.6.cloned.1.call-done), channel_id=1, source_target_pairs={{0,1},{1,0},{2,3},{3,2},{4,5},{5,4},{6,7},{7,6},{8,9},{9,8},{10,11... | collective-permute-start | bytes 1216520 | tf_op jit(solution)/shard_map/ppermute | solution.py:1509
  412.1 22.5 %collective-permute-start.9 = (bf16[144,1024]{1,0:T(8,128)(2,1)S(1)}, bf16[144,1024]{1,0:T(8,128)(2,1)S(1)}, u32[]{:S(2)}, u32[]{:S(2)}) collective-permute-start(bf16[144,1024]{1,0:T(8,128)(2,1)S(1)} %copy-done.8), channel_id=1, source_target_pairs={{0,1},{1,0},{2,3},{3,2},{4,5},{5,4},{6,7},{7,6},{8,9},{9,8},{10,11... | collective-permute-start | bytes 884744 | tf_op jit(solution)/shard_map/ppermute | solution.py:1509
  432.4 5.1 %collective-permute-start.18 = (bf16[96,768]{1,0:T(8,128)(2,1)S(1)}, bf16[96,768]{1,0:T(8,128)(2,1)S(1)}, u32[]{:S(2)}, u32[]{:S(2)}) collective-permute-start(bf16[96,768]{1,0:T(8,128)(2,1)S(1)} %fusion.25), channel_id=1, source_target_pairs={{0,1},{1,0},{2,3},{3,2},{4,5},{5,4},{6,7},{7,6},{8,9},{9,8},{10,11... | collective-permute-start | bytes 442376 | tf_op jit(solution)/shard_map/ppermute | solution.py:1494
  433.0 6.6 %collective-permute-start.14 = (bf16[24,3968]{1,0:T(8,128)(2,1)S(1)}, bf16[24,3968]{1,0:T(8,128)(2,1)S(1)}, u32[]{:S(2)}, u32[]{:S(2)}) collective-permute-start(bf16[24,3968]{1,0:T(8,128)(2,1)S(1)} %fusion.22), channel_id=1, source_target_pairs={{0,1},{1,0},{2,3},{3,2},{4,5},{5,4},{6,7},{7,6},{8,9},{9,8},{10,11... | collective-permute-start | bytes 571400 | tf_op jit(solution)/shard_map/ppermute | solution.py:1494
  453.8 9.8 %collective-permute-start.20 = (bf16[48,2688]{1,0:T(8,128)(2,1)}, bf16[48,2688]{1,0:T(8,128)(2,1)S(1)}, u32[]{:S(2)}, u32[]{:S(2)}) collective-permute-start(bf16[48,2688]{1,0:T(8,128)(2,1)} %reduce-scatter.8.cloned.1.call-done), channel_id=1, source_target_pairs={{0,1},{1,0},{2,3},{3,2},{4,5},{5,4},{6,7},{7,6},{8,9},{9,8},{10,11... | collective-permute-start | bytes 774152 | tf_op jit(solution)/shard_map/ppermute | solution.py:1509
  (21 other events, 151.8 us)
Sparse Core Ops, SparseCore 0:
  173.9 75.8 reduce-scatter.3
  268.9 92.7 reduce-scatter.5
  365.6 85.1 reduce-scatter.7

commit v5 on v4

--- a/solution.py
+++ b/solution.py
@@ -136,7 +136,7 @@
     return jnp.where(in_at == source, 1.0, 0.0).astype(BF)
 
 
-def qkv_kernel(x_ref, w_ref, b_ref, p_ref, out_ref, n1_ref):
+def qkv_kernel(first, x_ref, w_ref, p_ref, out_ref, n1_ref):
     @pl.when(pl.program_id(1) == 0)
     def _():
         def norm(sl, carry):
@@ -145,28 +145,29 @@
 
         by_chunks(x_ref.shape[0], 32, norm)
 
-    out_ref[...] = (mm(n1_ref[...], w_ref[...]) + b_ref[0]).astype(BF)
-
-
-def qkv_call(tokens, weight, bias3, p768, first):
+    which = pl.program_id(1) + first
+    bias = jnp.where(which == 0, p_ref[4:5, :], jnp.where(which == 2, p_ref[5:6, :], 0.0))
+    out_ref[...] = (mm(n1_ref[...], w_ref[...]) + bias).astype(BF)
+
+
+def qkv_call(tokens, weight, p768, first):
     rows, width = tokens.shape
     block = 512
     count = 3 - first
     return call(
-        qkv_kernel,
+        functools.partial(qkv_kernel, first),
         sds((rows, count * width), BF),
         grid=(rows // block, count),
         in_specs=[
             pl.BlockSpec((block, width), lambda i, j: (i, 0)),
             pl.BlockSpec((width, width), lambda i, j: (0, j + first)),
-            pl.BlockSpec((1, 1, width), lambda i, j: (j + first, 0, 0)),
             whole(p768.shape),
         ],
         out_specs=pl.BlockSpec((block, width), lambda i, j: (i, j)),
         scratch=[pltpu.VMEM((block, width), BF)],
         flops=2 * rows * width * width * count,
         name="qkv",
-    )(tokens, weight, bias3, p768)
+    )(tokens, weight, p768)
 
 
 def aug_layout(total_rows):
@@ -1537,14 +1538,10 @@
     ]
     far_tokens = jnp.concatenate(far, axis=0) if len(far) > 1 else (far[0] if far else None)
 
-    p768 = jnp.stack(
-        [
-            block_gains[:, 0], block_gains[:, 1], block_shifts[:, 0], block_shifts[:, 1],
-            qv_bias[:, 0], qv_bias[:, 1], proj_bias, fc2_bias,
-        ]
+    p768 = jnp.concatenate(
+        [block_gains.T, block_shifts.T, qv_bias.T, proj_bias[None], fc2_bias[None]]
     ).astype(F32)
-    bias3 = jnp.stack([qv_bias[:, 0], jnp.zeros_like(proj_bias), qv_bias[:, 1]]).astype(F32)[:, None, :]
-    qkv_own = qkv_call(own_tokens, qkv_weight, bias3, p768, 0)
+    qkv_own = qkv_call(own_tokens, qkv_weight, p768, 0)
     (
         fc1_bias, fine_first_bias, fine_norm_gain, fine_norm_shift, middle_up_bias, fine_second_bias, level_gains,
         level_shifts, table_cols, table_rows, valid_rows, qkv_own,
@@ -1582,7 +1579,7 @@
     bad = (key_rows >= valid_rows[0]) | (key_cols >= valid_cols[0])
     oh2 = jnp.where(bad & (lane == off + total_rows), NEG, hot.astype(F32)).astype(BF)
 
-    kv_far = qkv_call(far_tokens, qkv_weight, bias3, p768, 1) if far else None
+    kv_far = qkv_call(far_tokens, qkv_weight, p768, 1) if far else None
     attended, qaug, lse = attend_call(
         first, qkv_own, kv_far, (tw, tr), oh1, oh2, total_rows, heads
     )
@@ -1687,8 +1684,8 @@
         part = dx_far[(d - 1) * count : d * count]
         dx = dx + lax.ppermute(part, "seq", [(i, (i - d) % peers) for i in range(peers)])
     conv_total, low_total = seq_total(conv_low), seq_total(low_low)
-    last_low, conv_total, low_total, high_total, g_w2, dx = lax.optimization_barrier(
-        (last_low, conv_total, low_total, high_total, g_w2, dx)
+    last_low, _ = lax.optimization_barrier(
+        (last_low, (conv_total, low_total, high_total, g_w2, dx))
     )
     last_total = seq_total(last_low)
 

time: 484 us -> 478 us (0.988)
  waiting for transfers between devices: 66.3 us -> 58.6 us
  transfers between devices with their start and end apart: 24 -> 24, of which waited for: 11 -> 11; matrix products, arithmetic and copies ran while one was open for 12% -> 12% of each run, Pallas kernels for 34% -> 35%
where the time goes in v5:
time: 478 us; the launch traced here: 469 us
  Pallas kernels  290 us (61%)
  waiting for transfers between devices  58.6 us (12%)
  other arithmetic  38.8 us (8%)
  local copies, waits for them, and re-layouts  37.1 us (8%)
  starting transfers between devices  28.6 us (6%)
  between operations  16 us (3%)
    pallas_call x4, Pallas kernels, conv_call(): call(functools.partial(conv_kernel, level, block), [sds((rows * cols, cha...  64 us
    pallas_call x1, Pallas kernels, pyramid_back_call(): call(functools.partial(pyramid_back_kernel, lr, cols), [sds((tokens, widt...  45.4 us
    pallas_call x2, Pallas kernels, attend_back_call(): call(functools.partial(attend_back_kernel, total_rows, scale, sources), [...  33.1 us
    pallas_call x4, Pallas kernels, conv_back_call(): call(functools.partial(conv_back_kernel, ways, block), out, grid=(rows //...  31.9 us
    ppermute x6, waiting for transfers between devices, last_swap(): total = total + lax.ppermute(part(mine ^ d), 'img', pairs).astype(F32)  29.7 us
    pallas_call x1, Pallas kernels, mlp_back_call(): call(functools.partial(mlp_back_kernel, shards), [sds((width // 2, hidden...  24.7 us
    pallas_call x1, Pallas kernels, attend_call(): call(functools.partial(attend_kernel, total_rows, scale, parts), [sds((to...  24.6 us
    pallas_call x1, Pallas kernels, qkv_back_call(): call(qkv_back_kernel, [sds((width, 3 * width + 384), BF), sds((rows, widt...  20.8 us
  transfers between devices with their start and end apart: 24, of which 11 were waited for; matrix products, arithmetic and copies ran while one was open for 12% of the time, Pallas kernels for 35%

profile of v5, /device:TPU:0, one launch (start us, length us, event | category | flops | bytes accessed | tf_op | source)
XLA Modules:
  0.0 469.1 jit_solution(1630465773983514874)
XLA Ops:
  13.8 6.2 %qkv.2.refs_1_.refs_6_.refs_8_.refs_10_.refs_12_ = bf16[512,2304]{1,0:T(8,128)(2,1)} custom-call(bf16[512,768]{1,0:T(8,128)(2,1)} %bitcast.134, bf16[768,2304]{1,0:T(8,128)(2,1)} %w_ref.5, f32[8,768]{1,0:T(8,128)} %convert_element_type.326.p_ref), custom_call_target="tpu_custom_call" | custom-call | flops 18119392 | tf_op jit(solution)/shard_map/qkv/pallas_call | solution.py:157
  29.9 4.5 qkv.3.refs_7_.refs_9_.refs_11_.refs_13_
  34.4 24.6 %attend.1 = (bf16[512,768]{1,0:T(8,128)(2,1)}, bf16[12,512,256]{2,1,0:T(8,128)(2,1)}, f32[6,2,512]{2,1,0:T(2,128)}) custom-call(s32[1]{0:T(128)} %bitcast.1.refs_0_, bf16[512,2304]{1,0:T(8,128)(2,1)} %qkv.2.refs_1_.refs_6_.refs_8_.refs_10_.refs_12_, bf16[128,128]{1,0:T(8,128)(2,1)} %get-tuple-element.485.refs_2_, ...), custom_call_target="tpu_custom_call" | custom-call | flops 250000000 | tf_op jit(solution)/shard_map/attend/pallas_call | solution.py:306
  59.0 14.0 %mlp.1 = (f32[512,768]{1,0:T(8,128)}, bf16[512,3072]{1,0:T(8,128)(2,1)}, bf16[512,3072]{1,0:T(8,128)(2,1)}, bf16[512,768]{1,0:T(8,128)(2,1)}) custom-call(bf16[512,768]{1,0:T(8,128)(2,1)} %bitcast.135, bf16[512,768]{1,0:T(8,128)(2,1)} %get-tuple-element.140.o_ref.refs_4_, bf16[768,768]{1,0:T(8,128)(2,1)} %wp_ref.3, bf16[768,3072]{1,0:T(8,128)(2,1)} %w1_ref.3, ...), custom_call_target="tpu_custom_call" | custom-call | flops 140000000 | tf_op jit(solution)/shard_map/mlp/pallas_call | solution.py:371
  73.0 20.8 %pyramid.1 = (bf16[8,4,256,256]{3,2,1,0:T(8,128)(2,1)}, bf16[8,2,128,256]{3,2,1,0:T(8,128)(2,1)}, bf16[512,256]{1,0:T(8,128)(2,1)}, bf16[128,256]{1,0:T(8,128)(2,1)}) custom-call(bf16[512,768]{1,0:T(8,128)(2,1)} %get-tuple-element.142.y_ref, bf16[768,1536]{1,0:T(8,128)(2,1)} %ff_ref.3, bf16[768,384]{1,0:T(8,128)(2,1)} %fs_ref.3, bf16[768,1536]{1,0:T(8,128)(2,1)} %mu_ref.3, ...), custom_call_target="tpu_custom_call" | custom-call | flops 200000000 | tf_op jit(solution)/shard_map/pyramid/pallas_call | solution.py:507
  98.1 5.1 %copy.122 = bf16[4,2304,256]{2,1,0:T(8,128)(2,1)} copy(bf16[4,2304,256]{2,0,1:T(4,128)(2,1)} %bitcast.141) | data formatting | bytes 9437184 | tf_op jit(solution)/shard_map/transpose | solution.py:1598
  107.4 4.9 %conv3.1 = (bf16[128,256]{1,0:T(8,128)(2,1)}, bf16[128,256]{1,0:T(8,128)(2,1)}, bf16[2304,1024]{1,0:T(8,128)(2,1)}, f32[8,256]{1,0:T(8,128)}) custom-call(bf16[4,32,256]{2,1,0:T(8,128)(2,1)} %bitcast.163, bf16[2,32,256]{2,1,0:T(8,128)(2,1)} %pad_maximum_fusion.5.rim_ref, bf16[4,3,768,256]{3,2,1,0:T(8,128)(2,1)} %bitcast.124, bf16[128,256]{1,0:T(8,128)(2,1)} %bitcast.164, ...), custom_call_target="tpu_custom_call" | custom-call | flops 3774873 | tf_op jit(solution)/shard_map/conv3/pallas_call | solution.py:652
  112.3 7.0 %conv2.1 = (bf16[512,256]{1,0:T(8,128)(2,1)}, bf16[512,256]{1,0:T(8,128)(2,1)}, bf16[2304,1024]{1,0:T(8,128)(2,1)}, f32[8,256]{1,0:T(8,128)}) custom-call(bf16[8,64,256]{2,1,0:T(8,128)(2,1)} %bitcast.159, bf16[2,64,256]{2,1,0:T(8,128)(2,1)} %fusion.39.rim_ref, bf16[4,3,768,256]{3,2,1,0:T(8,128)(2,1)} %bitcast.125, ...), custom_call_target="tpu_custom_call", output_to_operand_aliasing={{2}: (5, {})} | custom-call | flops 15099494 | tf_op jit(solution)/shard_map/conv2/pallas_call | solution.py:652
  119.3 14.1 %conv1.1 = (bf16[2048,256]{1,0:T(8,128)(2,1)}, bf16[2048,256]{1,0:T(8,128)(2,1)}, bf16[2304,1024]{1,0:T(8,128)(2,1)}, f32[8,256]{1,0:T(8,128)}) custom-call(bf16[16,128,256]{2,1,0:T(8,128)(2,1)} %bitcast.152, bf16[2,128,256]{2,1,0:T(8,128)(2,1)} %fusion.37.rim_ref, bf16[4,3,768,256]{3,2,1,0:T(8,128)(2,1)} %bitcast.126, ...), custom_call_target="tpu_custom_call", output_to_operand_aliasing={{2}: (5, {})} | custom-call | flops 60397976 | tf_op jit(solution)/shard_map/conv1/pallas_call | solution.py:652
  133.4 38.0 %conv0.1 = (bf16[8192,256]{1,0:T(8,128)(2,1)}, bf16[8192,256]{1,0:T(8,128)(2,1)}, bf16[2304,1024]{1,0:T(8,128)(2,1)}, f32[8,256]{1,0:T(8,128)}) custom-call(bf16[32,256,256]{2,1,0:T(8,128)(2,1)} %bitcast.140, bf16[2,256,256]{2,1,0:T(8,128)(2,1)} %fusion.27.rim_ref, bf16[4,3,768,256]{3,2,1,0:T(8,128)(2,1)} %bitcast.127, ...), custom_call_target="tpu_custom_call", output_to_operand_aliasing={{2}: (5, {})} | custom-call | flops 241591904 | tf_op jit(solution)/shard_map/conv0/pallas_call | solution.py:652
  192.0 3.2 conv_back2.1.dzb_ref
  195.2 6.9 %conv_back1.1.dzm_ref = bf16[2,2,512,256]{3,2,1,0:T(8,128)(2,1)} custom-call(bf16[16,128,256]{2,1,0:T(8,128)(2,1)} %bitcast.153, bf16[2,128,256]{2,1,0:T(8,128)(2,1)} %fusion.36.rim_ref, bf16[4,3,768,256]{3,2,1,0:T(8,128)(2,1)} %bitcast.130), custom_call_target="tpu_custom_call" | custom-call | flops 36238784 | tf_op jit(solution)/shard_map/conv_back1/pallas_call | solution.py:733
  202.1 19.0 %conv_back0.1 = bf16[4,4,512,256]{3,2,1,0:T(8,128)(2,1)} custom-call(bf16[32,256,256]{2,1,0:T(8,128)(2,1)} %bitcast.138, bf16[2,256,256]{2,1,0:T(8,128)(2,1)} %fusion.26.rim_ref, bf16[4,3,768,256]{3,2,1,0:T(8,128)(2,1)} %bitcast.131), custom_call_target="tpu_custom_call" | custom-call | flops 144955152 | tf_op jit(solution)/shard_map/conv_back0/pallas_call | solution.py:733
  221.0 45.4 %pyramid_back.1 = (f32[512,768]{1,0:T(8,128)}, bf16[768,4224]{1,0:T(8,128)(2,1)}, f32[8,384]{1,0:T(8,128)}, f32[8,192]{1,0:T(8,128)}, f32[16,256]{1,0:T(8,128)}) custom-call(bf16[512,768]{1,0:T(8,128)(2,1)} %get-tuple-element.142.y_ref, bf16[768,1536]{1,0:T(8,128)(2,1)} %ff_ref.3, bf16[768,384]{1,0:T(8,128)(2,1)} %fs_ref.3, bf16[768,1536]{1,0:T(8,128)(2,1)} %mu_ref.3, ...), custom_call_target="tpu_custom_call" | custom-call | flops 450000000 | tf_op jit(solution)/shard_map/pyramid_back/pallas_call | solution.py:910
  266.5 24.7 %mlp_back.1 = (bf16[384,3968]{1,0:T(8,128)(2,1)}, bf16[384,3968]{1,0:T(8,128)(2,1)}, bf16[1536,768]{1,0:T(8,128)(2,1)}, bf16[1536,768]{1,0:T(8,128)(2,1)}, f32[512,768]{1,0:T(8,128)}, /*index=5*/bf16[512,768]{1,0:T(8,128)(2,1)}) custom-call(s32[1]{0:T(128)} %bitcast.37.core_ref, f32[512,768]{1,0:T(8,128)} %get-tuple-element.178.dy_ref, ...), custom_call_target="tpu_custom_call" | custom-call | flops 250000000 | tf_op jit(solution)/shard_map/mlp_back/pallas_call | solution.py:1082
  292.5 16.7 %attend_back.2 = (bf16[3,1024,768]{2,1,0:T(8,128)(2,1)}, f32[128,256]{1,0:T(8,128)}) custom-call(s32[1]{0:T(128)} %bitcast.1.refs_0_, bf16[512,2304]{1,0:T(8,128)(2,1)} %qkv.2.refs_1_.refs_6_.refs_8_.refs_10_.refs_12_, bf16[12,512,256]{2,1,0:T(8,128)(2,1)} %get-tuple-element.172.refs_2_, bf16[512,768]{1,0:T(8,128)(2,1)} %get-tuple-element.194.refs_3_, ...), custom_call_target="tpu_custom_call" | custom-call | flops 150000000 | tf_op jit(solution)/shard_map/attend_back/pallas_call | solution.py:1258
  310.8 4.2 fusion.4
  320.2 16.4 %attend_back.3 = (bf16[3,1024,768]{2,1,0:T(8,128)(2,1)}, f32[128,256]{1,0:T(8,128)}) custom-call(s32[1]{0:T(128)} %bitcast.1.refs_0_, bf16[512,2304]{1,0:T(8,128)(2,1)} %qkv.2.refs_1_.refs_6_.refs_8_.refs_10_.refs_12_, bf16[12,512,256]{2,1,0:T(8,128)(2,1)} %get-tuple-element.172.refs_2_, ...), custom_call_target="tpu_custom_call", output_to_operand_aliasing={{0}: (14, {})} | custom-call | flops 150000000 | tf_op jit(solution)/shard_map/attend_back/pallas_call | solution.py:1258
  336.6 20.8 %qkv_back.1 = (bf16[768,2688]{1,0:T(8,128)(2,1)}, f32[512,768]{1,0:T(8,128)}, bf16[512,768]{1,0:T(8,128)(2,1)}) custom-call(bf16[1024,768]{1,0:T(8,128)(2,1)} %pad_maximum_fusion.x_ref, bf16[3,1024,768]{2,1,0:T(8,128)(2,1)} %get-tuple-element.208.dqkv_ref, bf16[768,2304]{1,0:T(8,128)(2,1)} %w_ref.5, f32[512,768]{1,0:T(8,128)} %get-tuple-element.209.dx1_ref, ...), custom_call_target="tpu_custom_call" | custom-call | flops 80000000 | tf_op jit(solution)/shard_map/qkv_back/pallas_call | solution.py:1365
  366.4 13.3 %collective-permute-done.8 = bf16[384,768]{1,0:T(8,128)(2,1)S(1)} collective-permute-done((bf16[384,768]{1,0:T(8,128)(2,1)}, bf16[384,768]{1,0:T(8,128)(2,1)S(1)}, u32[]{:S(2)}, u32[]{:S(2)}) %collective-permute-start.8) | collective-permute-done | bytes 589856 | tf_op jit(solution)/shard_map/ppermute | solution.py:1462
  390.1 3.1 collective-permute-start.14
  398.8 4.4 collective-permute-done.12
  404.5 22.6 %collective-permute-done.13 = bf16[24,3968]{1,0:T(8,128)(2,1)S(1)} collective-permute-done((bf16[24,3968]{1,0:T(8,128)(2,1)S(1)}, bf16[24,3968]{1,0:T(8,128)(2,1)S(1)}, u32[]{:S(2)}, u32[]{:S(2)}) %collective-permute-start.13) | collective-permute-done | bytes 190496 | tf_op jit(solution)/shard_map/ppermute | solution.py:1490
  445.3 4.1 reduce-scatter.8.cloned.1.call-done
  (207 shorter events, 109.4 us)
Async XLA Ops:
  7.2 259.2 %reduce-scatter.4.cloned.1.call-start = ((), (), s32[]{:S(2)}) async-start(), calls=%async_computation.3 | async-start | bytes 5013504 | tf_op jit(solution)/shard_map/reduce_scatter | solution.py:1611
  7.2 21.7 %collective-permute-start = (bf16[512,768]{1,0:T(8,128)(2,1)}, bf16[512,768]{1,0:T(8,128)(2,1)S(1)}, u32[]{:S(2)}, u32[]{:S(2)}) collective-permute-start(bf16[512,768]{1,0:T(8,128)(2,1)} %bitcast.133), channel_id=1, source_target_pairs={{0,1},{1,0},{2,3},{3,2},{4,5},{5,4},{6,7},{7,6},{8,9},{9,8},{10,11... | collective-permute-start | bytes 2359304 | tf_op jit(solution)/shard_map/ppermute | solution.py:1536
  97.3 7.5 %collective-permute-start.1 = (bf16[480,256]{1,0:T(8,128)(2,1)S(1)}, bf16[480,256]{1,0:T(8,128)(2,1)S(1)}, u32[]{:S(2)}, u32[]{:S(2)}) collective-permute-start(bf16[480,256]{1,0:T(8,128)(2,1)S(1)} %maximum_select_fusion), channel_id=1, source_target_pairs={{0,1},{1,0},{2,3},{3,2},{4,5},{5,4},{6,7},{7,6},{8,9},{9,8},{10,11... | collective-permute-start | bytes 737288 | tf_op jit(solution)/shard_map/ppermute | solution.py:1410
  171.5 187.9 %reduce-scatter.6.cloned.1.call-start = ((), (), s32[]{:S(2)}) async-start(), calls=%async_computation.4 | async-start | bytes 6893568 | tf_op jit(solution)/shard_map/reduce_scatter | solution.py:1652
  176.9 9.6 %collective-permute-start.2 = (bf16[480,256]{1,0:T(8,128)(2,1)S(1)}, bf16[480,256]{1,0:T(8,128)(2,1)S(1)}, u32[]{:S(2)}, u32[]{:S(2)}) collective-permute-start(bf16[480,256]{1,0:T(8,128)(2,1)S(1)} %maximum_select_fusion.1), channel_id=1, source_target_pairs={{0,1},{1,0},{2,3},{3,2},{4,5},{5,4},{6,7},{7,6},{8,9},{9,8},{10,11... | collective-permute-start | bytes 737288 | tf_op jit(solution)/shard_map/ppermute | solution.py:1410
  266.5 182.9 %reduce-scatter.8.cloned.1.call-start = ((), (), s32[]{:S(2)}) async-start(), calls=%async_computation.5 | async-start | bytes 4386816 | tf_op jit(solution)/shard_map/reduce_scatter | solution.py:1675
  291.2 17.9 %collective-permute-start.3 = (bf16[384,3968]{1,0:T(8,128)(2,1)}, bf16[384,3968]{1,0:T(8,128)(2,1)S(1)}, u32[]{:S(2)}, u32[]{:S(2)}) collective-permute-start(bf16[384,3968]{1,0:T(8,128)(2,1)} %get-tuple-element.189), channel_id=1, source_target_pairs={{0,2},{2,0},{4,6},{6,4},{8,10},{10,8},{12,14},{14,12},{16,18},{18,... | collective-permute-start | bytes 9142280 | tf_op jit(solution)/shard_map/ppermute | solution.py:1462
  291.3 17.9 %collective-permute-start.4 = (bf16[1536,768]{1,0:T(8,128)(2,1)}, bf16[1536,768]{1,0:T(8,128)(2,1)}, u32[]{:S(2)}, u32[]{:S(2)}) collective-permute-start(bf16[1536,768]{1,0:T(8,128)(2,1)} %get-tuple-element.190), channel_id=1, source_target_pairs={{0,2},{2,0},{4,6},{6,4},{8,10},{10,8},{12,14},{14,12},{16,18},{18,... | collective-permute-start | bytes 7077896 | tf_op jit(solution)/shard_map/ppermute | solution.py:1462
  317.1 42.2 %collective-permute-start.5 = (bf16[192,3968]{1,0:T(8,128)(2,1)}, bf16[192,3968]{1,0:T(8,128)(2,1)}, u32[]{:S(2)}, u32[]{:S(2)}) collective-permute-start(bf16[192,3968]{1,0:T(8,128)(2,1)} %bitcast.57), channel_id=1, source_target_pairs={{0,4},{2,6},{4,0},{6,2},{8,12},{10,14},{12,8},{14,10},{16,20},{18,... | collective-permute-start | bytes 4571144 | tf_op jit(solution)/shard_map/ppermute | solution.py:1462
  318.6 40.7 %collective-permute-start.6 = (bf16[768,768]{1,0:T(8,128)(2,1)}, bf16[768,768]{1,0:T(8,128)(2,1)}, u32[]{:S(2)}, u32[]{:S(2)}) collective-permute-start(bf16[768,768]{1,0:T(8,128)(2,1)} %bitcast.59), channel_id=1, source_target_pairs={{0,1},{1,0},{2,3},{3,2},{4,5},{5,4},{6,7},{7,6},{8,9},{9,8},{10,11... | collective-permute-start | bytes 3538952 | tf_op jit(solution)/shard_map/ppermute | solution.py:1462
  364.3 17.9 %collective-permute-start.7 = (bf16[96,3968]{1,0:T(8,128)(2,1)}, bf16[96,3968]{1,0:T(8,128)(2,1)S(1)}, u32[]{:S(2)}, u32[]{:S(2)}) collective-permute-start(bf16[96,3968]{1,0:T(8,128)(2,1)} %bitcast.67), channel_id=1, source_target_pairs={{0,1},{1,0},{2,3},{3,2},{4,5},{5,4},{6,7},{7,6},{8,9},{9,8},{10,11... | collective-permute-start | bytes 2285576 | tf_op jit(solution)/shard_map/ppermute | solution.py:1462
  365.8 13.9 %collective-permute-start.8 = (bf16[384,768]{1,0:T(8,128)(2,1)}, bf16[384,768]{1,0:T(8,128)(2,1)S(1)}, u32[]{:S(2)}, u32[]{:S(2)}) collective-permute-start(bf16[384,768]{1,0:T(8,128)(2,1)} %bitcast.69), channel_id=1, source_target_pairs={{0,4},{2,6},{4,0},{6,2},{8,12},{10,14},{12,8},{14,10},{16,20},{18,... | collective-permute-start | bytes 1769480 | tf_op jit(solution)/shard_map/ppermute | solution.py:1462
  382.4 7.7 %collective-permute-start.16 = (bf16[96,768]{1,0:T(8,128)(2,1)S(1)}, bf16[96,768]{1,0:T(8,128)(2,1)S(1)}, u32[]{:S(2)}, u32[]{:S(2)}) collective-permute-start(bf16[96,768]{1,0:T(8,128)(2,1)S(1)} %get-tuple-element.427), channel_id=1, source_target_pairs={{0,8},{2,10},{4,12},{6,14},{8,0},{10,2},{12,4},{14,6},{16,24},{18,... | collective-permute-start | bytes 442376 | tf_op jit(solution)/shard_map/ppermute | solution.py:1490
  383.7 12.2 %collective-permute-start.17 = (bf16[96,768]{1,0:T(8,128)(2,1)S(1)}, bf16[96,768]{1,0:T(8,128)(2,1)S(1)}, u32[]{:S(2)}, u32[]{:S(2)}) collective-permute-start(bf16[96,768]{1,0:T(8,128)(2,1)S(1)} %get-tuple-element.429), channel_id=1, source_target_pairs={{0,16},{2,18},{4,20},{6,22},{8,24},{10,26},{12,28},{14,30},{16,0},... | collective-permute-start | bytes 442376 | tf_op jit(solution)/shard_map/ppermute | solution.py:1490
  385.5 12.0 %collective-permute-start.18 = (bf16[96,768]{1,0:T(8,128)(2,1)S(1)}, bf16[96,768]{1,0:T(8,128)(2,1)S(1)}, u32[]{:S(2)}, u32[]{:S(2)}) collective-permute-start(bf16[96,768]{1,0:T(8,128)(2,1)S(1)} %get-tuple-element.428), channel_id=1, source_target_pairs={{0,24},{2,26},{4,28},{6,30},{8,16},{10,18},{12,20},{14,22},{16,8},... | collective-permute-start | bytes 442376 | tf_op jit(solution)/shard_map/ppermute | solution.py:1490
  387.0 16.2 %collective-permute-start.12 = (bf16[24,3968]{1,0:T(8,128)(2,1)S(1)}, bf16[24,3968]{1,0:T(8,128)(2,1)S(1)}, u32[]{:S(2)}, u32[]{:S(2)}) collective-permute-start(bf16[24,3968]{1,0:T(8,128)(2,1)S(1)} %get-tuple-element.424), channel_id=1, source_target_pairs={{0,8},{2,10},{4,12},{6,14},{8,0},{10,2},{12,4},{14,6},{16,24},{18,... | collective-permute-start | bytes 571400 | tf_op jit(solution)/shard_map/ppermute | solution.py:1490
  387.4 39.7 %collective-permute-start.13 = (bf16[24,3968]{1,0:T(8,128)(2,1)S(1)}, bf16[24,3968]{1,0:T(8,128)(2,1)S(1)}, u32[]{:S(2)}, u32[]{:S(2)}) collective-permute-start(bf16[24,3968]{1,0:T(8,128)(2,1)S(1)} %get-tuple-element.426), channel_id=1, source_target_pairs={{0,16},{2,18},{4,20},{6,22},{8,24},{10,26},{12,28},{14,30},{16,0},... | collective-permute-start | bytes 571400 | tf_op jit(solution)/shard_map/ppermute | solution.py:1490
  390.1 38.5 %collective-permute-start.14 = (bf16[24,3968]{1,0:T(8,128)(2,1)S(1)}, bf16[24,3968]{1,0:T(8,128)(2,1)S(1)}, u32[]{:S(2)}, u32[]{:S(2)}) collective-permute-start(bf16[24,3968]{1,0:T(8,128)(2,1)S(1)} %get-tuple-element.425), channel_id=1, source_target_pairs={{0,24},{2,26},{4,28},{6,30},{8,16},{10,18},{12,20},{14,22},{16,8},... | collective-permute-start | bytes 571400 | tf_op jit(solution)/shard_map/ppermute | solution.py:1490
  395.9 44.8 %collective-permute-start.11 = (bf16[48,4224]{1,0:T(8,128)(2,1)}, bf16[48,4224]{1,0:T(8,128)(2,1)}, u32[]{:S(2)}, u32[]{:S(2)}) collective-permute-start(bf16[48,4224]{1,0:T(8,128)(2,1)} %reduce-scatter.6.cloned.1.call-done), channel_id=1, source_target_pairs={{0,1},{1,0},{2,3},{3,2},{4,5},{5,4},{6,7},{7,6},{8,9},{9,8},{10,11... | collective-permute-start | bytes 1216520 | tf_op jit(solution)/shard_map/ppermute | solution.py:1510
  397.5 31.9 %collective-permute-start.10 = (bf16[144,1024]{1,0:T(8,128)(2,1)S(1)}, bf16[144,1024]{1,0:T(8,128)(2,1)S(1)}, u32[]{:S(2)}, u32[]{:S(2)}) collective-permute-start(bf16[144,1024]{1,0:T(8,128)(2,1)S(1)} %copy-done.8), channel_id=1, source_target_pairs={{0,1},{1,0},{2,3},{3,2},{4,5},{5,4},{6,7},{7,6},{8,9},{9,8},{10,11... | collective-permute-start | bytes 884744 | tf_op jit(solution)/shard_map/ppermute | solution.py:1510
  403.2 40.8 %collective-permute-start.9 = (bf16[512,768]{1,0:T(8,128)(2,1)}, bf16[512,768]{1,0:T(8,128)(2,1)S(1)}, u32[]{:S(2)}, u32[]{:S(2)}) collective-permute-start(bf16[512,768]{1,0:T(8,128)(2,1)} %get-tuple-element.237), channel_id=1, source_target_pairs={{0,1},{1,0},{2,3},{3,2},{4,5},{5,4},{6,7},{7,6},{8,9},{9,8},{10,11... | collective-permute-start | bytes 2359304 | tf_op jit(solution)/shard_map/ppermute | solution.py:1685
  427.1 5.1 %collective-permute-start.19 = (bf16[96,768]{1,0:T(8,128)(2,1)S(1)}, bf16[96,768]{1,0:T(8,128)(2,1)S(1)}, u32[]{:S(2)}, u32[]{:S(2)}) collective-permute-start(bf16[96,768]{1,0:T(8,128)(2,1)S(1)} %fusion.25), channel_id=1, source_target_pairs={{0,1},{1,0},{2,3},{3,2},{4,5},{5,4},{6,7},{7,6},{8,9},{9,8},{10,11... | collective-permute-start | bytes 442376 | tf_op jit(solution)/shard_map/ppermute | solution.py:1495
  428.8 5.7 %collective-permute-start.15 = (bf16[24,3968]{1,0:T(8,128)(2,1)S(1)}, bf16[24,3968]{1,0:T(8,128)(2,1)S(1)}, u32[]{:S(2)}, u32[]{:S(2)}) collective-permute-start(bf16[24,3968]{1,0:T(8,128)(2,1)S(1)} %fusion.22), channel_id=1, source_target_pairs={{0,1},{1,0},{2,3},{3,2},{4,5},{5,4},{6,7},{7,6},{8,9},{9,8},{10,11... | collective-permute-start | bytes 571400 | tf_op jit(solution)/shard_map/ppermute | solution.py:1495
  449.4 7.6 %collective-permute-start.20 = (bf16[48,2688]{1,0:T(8,128)(2,1)}, bf16[48,2688]{1,0:T(8,128)(2,1)S(1)}, u32[]{:S(2)}, u32[]{:S(2)}) collective-permute-start(bf16[48,2688]{1,0:T(8,128)(2,1)} %reduce-scatter.8.cloned.1.call-done), channel_id=1, source_target_pairs={{0,1},{1,0},{2,3},{3,2},{4,5},{5,4},{6,7},{7,6},{8,9},{9,8},{10,11... | collective-permute-start | bytes 774152 | tf_op jit(solution)/shard_map/ppermute | solution.py:1510
  (20 other events, 142.5 us)
Sparse Core Ops, SparseCore 0:
  171.6 75.8 reduce-scatter.3
  266.6 92.7 reduce-scatter.5
  366.5 82.8 reduce-scatter.7

commit v6 on v5

--- a/solution.py
+++ b/solution.py
@@ -1671,7 +1671,6 @@
     last, dx, dx_far = qkv_back_call(
         all_tokens, dqkv, qkv_weight, dx1, p768, dtab, head_hot
     )
-    last, low_low = lax.optimization_barrier((last, low_low))
     last_low = lax.psum_scatter(last, "img", scatter_dimension=0, tiled=True)
     settle([three, four], last)
     swap([(three, "y"), (four, 1)])

time: 478 us -> 498 us (1.042)
  waiting for transfers between devices: 58.6 us -> 83.1 us
    ppermute x3, waiting for transfers between devices: 2.53 us -> 13.9 us  [seq_total(): other = lax.ppermute(part, 'seq', [(0, 1), (1, 0)])]
    ppermute x1, waiting for transfers between devices: 0.01 us -> 11.1 us  [per_device(): lax.ppermute(part, 'seq', [(i, (i - d) % peers) for i in range(peers)])]
    ppermute x6, waiting for transfers between devices: 29.7 us -> 36.4 us  [last_swap(): total = total + lax.ppermute(part(mine ^ d), 'img', pairs).astype(F32)]
  transfers between devices with their start and end apart: 24 -> 24, of which waited for: 11 -> 11; matrix products, arithmetic and copies ran while one was open for 12% -> 12% of each run, Pallas kernels for 35% -> 33%
where the time goes in v6:
time: 498 us; the launch traced here: 489 us
  Pallas kernels  290 us (58%)
  waiting for transfers between devices  83.1 us (17%)
  other arithmetic  36.9 us (7%)
  local copies, waits for them, and re-layouts  36.6 us (7%)
  starting transfers between devices  26.3 us (5%)
  between operations  16 us (3%)
    pallas_call x4, Pallas kernels, conv_call(): call(functools.partial(conv_kernel, level, block), [sds((rows * cols, cha...  63.9 us
    pallas_call x1, Pallas kernels, pyramid_back_call(): call(functools.partial(pyramid_back_kernel, lr, cols), [sds((tokens, widt...  45.3 us
    ppermute x6, waiting for transfers between devices, last_swap(): total = total + lax.ppermute(part(mine ^ d), 'img', pairs).astype(F32)  36.4 us
    pallas_call x2, Pallas kernels, attend_back_call(): call(functools.partial(attend_back_kernel, total_rows, scale, sources), [...  33.1 us
    pallas_call x4, Pallas kernels, conv_back_call(): call(functools.partial(conv_back_kernel, ways, block), out, grid=(rows //...  31.9 us
    pallas_call x1, Pallas kernels, mlp_back_call(): call(functools.partial(mlp_back_kernel, shards), [sds((width // 2, hidden...  24.7 us
    pallas_call x1, Pallas kernels, attend_call(): call(functools.partial(attend_kernel, total_rows, scale, parts), [sds((to...  24.6 us
    pallas_call x1, Pallas kernels, qkv_back_call(): call(qkv_back_kernel, [sds((width, 3 * width + 384), BF), sds((rows, widt...  20.9 us
  transfers between devices with their start and end apart: 24, of which 11 were waited for; matrix products, arithmetic and copies ran while one was open for 12% of the time, Pallas kernels for 33%

profile of v6, /device:TPU:0, one launch (start us, length us, event | category | flops | bytes accessed | tf_op | source)
XLA Modules:
  0.0 489.0 jit_solution(11046813274573207591)
XLA Ops:
  14.8 6.2 %qkv.2.refs_1_.refs_6_.refs_8_.refs_10_.refs_12_ = bf16[512,2304]{1,0:T(8,128)(2,1)} custom-call(bf16[512,768]{1,0:T(8,128)(2,1)} %bitcast.134, bf16[768,2304]{1,0:T(8,128)(2,1)} %w_ref.5, f32[8,768]{1,0:T(8,128)} %convert_element_type.326.p_ref), custom_call_target="tpu_custom_call" | custom-call | flops 18119392 | tf_op jit(solution)/shard_map/qkv/pallas_call | solution.py:157
  29.9 4.5 qkv.3.refs_7_.refs_9_.refs_11_.refs_13_
  34.4 24.6 %attend.1 = (bf16[512,768]{1,0:T(8,128)(2,1)}, bf16[12,512,256]{2,1,0:T(8,128)(2,1)}, f32[6,2,512]{2,1,0:T(2,128)}) custom-call(s32[1]{0:T(128)} %bitcast.1.refs_0_, bf16[512,2304]{1,0:T(8,128)(2,1)} %qkv.2.refs_1_.refs_6_.refs_8_.refs_10_.refs_12_, bf16[128,128]{1,0:T(8,128)(2,1)} %get-tuple-element.481.refs_2_, ...), custom_call_target="tpu_custom_call" | custom-call | flops 250000000 | tf_op jit(solution)/shard_map/attend/pallas_call | solution.py:306
  59.0 14.0 %mlp.1 = (f32[512,768]{1,0:T(8,128)}, bf16[512,3072]{1,0:T(8,128)(2,1)}, bf16[512,3072]{1,0:T(8,128)(2,1)}, bf16[512,768]{1,0:T(8,128)(2,1)}) custom-call(bf16[512,768]{1,0:T(8,128)(2,1)} %bitcast.135, bf16[512,768]{1,0:T(8,128)(2,1)} %get-tuple-element.138.o_ref.refs_4_, bf16[768,768]{1,0:T(8,128)(2,1)} %wp_ref.3, bf16[768,3072]{1,0:T(8,128)(2,1)} %w1_ref.3, ...), custom_call_target="tpu_custom_call" | custom-call | flops 140000000 | tf_op jit(solution)/shard_map/mlp/pallas_call | solution.py:371
  73.0 20.8 %pyramid.1 = (bf16[8,4,256,256]{3,2,1,0:T(8,128)(2,1)}, bf16[8,2,128,256]{3,2,1,0:T(8,128)(2,1)}, bf16[512,256]{1,0:T(8,128)(2,1)}, bf16[128,256]{1,0:T(8,128)(2,1)}) custom-call(bf16[512,768]{1,0:T(8,128)(2,1)} %get-tuple-element.140.y_ref, bf16[768,1536]{1,0:T(8,128)(2,1)} %ff_ref.3, bf16[768,384]{1,0:T(8,128)(2,1)} %fs_ref.3, bf16[768,1536]{1,0:T(8,128)(2,1)} %mu_ref.3, ...), custom_call_target="tpu_custom_call" | custom-call | flops 200000000 | tf_op jit(solution)/shard_map/pyramid/pallas_call | solution.py:507
  98.1 5.2 %copy.122 = bf16[4,2304,256]{2,1,0:T(8,128)(2,1)} copy(bf16[4,2304,256]{2,0,1:T(4,128)(2,1)} %bitcast.141) | data formatting | bytes 9437184 | tf_op jit(solution)/shard_map/transpose | solution.py:1598
  107.4 4.9 %conv3.1 = (bf16[128,256]{1,0:T(8,128)(2,1)}, bf16[128,256]{1,0:T(8,128)(2,1)}, bf16[2304,1024]{1,0:T(8,128)(2,1)}, f32[8,256]{1,0:T(8,128)}) custom-call(bf16[4,32,256]{2,1,0:T(8,128)(2,1)} %bitcast.163, bf16[2,32,256]{2,1,0:T(8,128)(2,1)} %pad_maximum_fusion.5.rim_ref, bf16[4,3,768,256]{3,2,1,0:T(8,128)(2,1)} %bitcast.124, bf16[128,256]{1,0:T(8,128)(2,1)} %bitcast.164, ...), custom_call_target="tpu_custom_call" | custom-call | flops 3774873 | tf_op jit(solution)/shard_map/conv3/pallas_call | solution.py:652
  112.4 6.9 %conv2.1 = (bf16[512,256]{1,0:T(8,128)(2,1)}, bf16[512,256]{1,0:T(8,128)(2,1)}, bf16[2304,1024]{1,0:T(8,128)(2,1)}, f32[8,256]{1,0:T(8,128)}) custom-call(bf16[8,64,256]{2,1,0:T(8,128)(2,1)} %bitcast.159, bf16[2,64,256]{2,1,0:T(8,128)(2,1)} %fusion.39.rim_ref, bf16[4,3,768,256]{3,2,1,0:T(8,128)(2,1)} %bitcast.125, ...), custom_call_target="tpu_custom_call", output_to_operand_aliasing={{2}: (5, {})} | custom-call | flops 15099494 | tf_op jit(solution)/shard_map/conv2/pallas_call | solution.py:652
  119.3 14.1 %conv1.1 = (bf16[2048,256]{1,0:T(8,128)(2,1)}, bf16[2048,256]{1,0:T(8,128)(2,1)}, bf16[2304,1024]{1,0:T(8,128)(2,1)}, f32[8,256]{1,0:T(8,128)}) custom-call(bf16[16,128,256]{2,1,0:T(8,128)(2,1)} %bitcast.152, bf16[2,128,256]{2,1,0:T(8,128)(2,1)} %fusion.37.rim_ref, bf16[4,3,768,256]{3,2,1,0:T(8,128)(2,1)} %bitcast.126, ...), custom_call_target="tpu_custom_call", output_to_operand_aliasing={{2}: (5, {})} | custom-call | flops 60397976 | tf_op jit(solution)/shard_map/conv1/pallas_call | solution.py:652
  133.4 37.9 %conv0.1 = (bf16[8192,256]{1,0:T(8,128)(2,1)}, bf16[8192,256]{1,0:T(8,128)(2,1)}, bf16[2304,1024]{1,0:T(8,128)(2,1)}, f32[8,256]{1,0:T(8,128)}) custom-call(bf16[32,256,256]{2,1,0:T(8,128)(2,1)} %bitcast.140, bf16[2,256,256]{2,1,0:T(8,128)(2,1)} %fusion.27.rim_ref, bf16[4,3,768,256]{3,2,1,0:T(8,128)(2,1)} %bitcast.127, ...), custom_call_target="tpu_custom_call", output_to_operand_aliasing={{2}: (5, {})} | custom-call | flops 241591904 | tf_op jit(solution)/shard_map/conv0/pallas_call | solution.py:652
  195.1 6.9 %conv_back1.1.dzm_ref = bf16[2,2,512,256]{3,2,1,0:T(8,128)(2,1)} custom-call(bf16[16,128,256]{2,1,0:T(8,128)(2,1)} %bitcast.153, bf16[2,128,256]{2,1,0:T(8,128)(2,1)} %fusion.36.rim_ref, bf16[4,3,768,256]{3,2,1,0:T(8,128)(2,1)} %bitcast.130), custom_call_target="tpu_custom_call" | custom-call | flops 36238784 | tf_op jit(solution)/shard_map/conv_back1/pallas_call | solution.py:733
  202.0 19.0 %conv_back0.1 = bf16[4,4,512,256]{3,2,1,0:T(8,128)(2,1)} custom-call(bf16[32,256,256]{2,1,0:T(8,128)(2,1)} %bitcast.138, bf16[2,256,256]{2,1,0:T(8,128)(2,1)} %fusion.26.rim_ref, bf16[4,3,768,256]{3,2,1,0:T(8,128)(2,1)} %bitcast.131), custom_call_target="tpu_custom_call" | custom-call | flops 144955152 | tf_op jit(solution)/shard_map/conv_back0/pallas_call | solution.py:733
  221.0 45.3 %pyramid_back.1 = (f32[512,768]{1,0:T(8,128)}, bf16[768,4224]{1,0:T(8,128)(2,1)}, f32[8,384]{1,0:T(8,128)}, f32[8,192]{1,0:T(8,128)}, f32[16,256]{1,0:T(8,128)}) custom-call(bf16[512,768]{1,0:T(8,128)(2,1)} %get-tuple-element.140.y_ref, bf16[768,1536]{1,0:T(8,128)(2,1)} %ff_ref.3, bf16[768,384]{1,0:T(8,128)(2,1)} %fs_ref.3, bf16[768,1536]{1,0:T(8,128)(2,1)} %mu_ref.3, ...), custom_call_target="tpu_custom_call" | custom-call | flops 450000000 | tf_op jit(solution)/shard_map/pyramid_back/pallas_call | solution.py:910
  266.5 24.7 %mlp_back.1 = (bf16[384,3968]{1,0:T(8,128)(2,1)}, bf16[384,3968]{1,0:T(8,128)(2,1)}, bf16[1536,768]{1,0:T(8,128)(2,1)}, bf16[1536,768]{1,0:T(8,128)(2,1)}, f32[512,768]{1,0:T(8,128)}, /*index=5*/bf16[512,768]{1,0:T(8,128)(2,1)}) custom-call(s32[1]{0:T(128)} %bitcast.37.core_ref, f32[512,768]{1,0:T(8,128)} %get-tuple-element.176.dy_ref, ...), custom_call_target="tpu_custom_call" | custom-call | flops 250000000 | tf_op jit(solution)/shard_map/mlp_back/pallas_call | solution.py:1082
  292.4 16.7 %attend_back.2 = (bf16[3,1024,768]{2,1,0:T(8,128)(2,1)}, f32[128,256]{1,0:T(8,128)}) custom-call(s32[1]{0:T(128)} %bitcast.1.refs_0_, bf16[512,2304]{1,0:T(8,128)(2,1)} %qkv.2.refs_1_.refs_6_.refs_8_.refs_10_.refs_12_, bf16[12,512,256]{2,1,0:T(8,128)(2,1)} %get-tuple-element.170.refs_2_, bf16[512,768]{1,0:T(8,128)(2,1)} %get-tuple-element.192.refs_3_, ...), custom_call_target="tpu_custom_call" | custom-call | flops 150000000 | tf_op jit(solution)/shard_map/attend_back/pallas_call | solution.py:1258
  310.7 4.2 fusion.4
  320.1 16.5 %attend_back.3 = (bf16[3,1024,768]{2,1,0:T(8,128)(2,1)}, f32[128,256]{1,0:T(8,128)}) custom-call(s32[1]{0:T(128)} %bitcast.1.refs_0_, bf16[512,2304]{1,0:T(8,128)(2,1)} %qkv.2.refs_1_.refs_6_.refs_8_.refs_10_.refs_12_, bf16[12,512,256]{2,1,0:T(8,128)(2,1)} %get-tuple-element.170.refs_2_, ...), custom_call_target="tpu_custom_call", output_to_operand_aliasing={{0}: (14, {})} | custom-call | flops 150000000 | tf_op jit(solution)/shard_map/attend_back/pallas_call | solution.py:1258
  336.6 20.9 %qkv_back.1 = (bf16[768,2688]{1,0:T(8,128)(2,1)}, f32[512,768]{1,0:T(8,128)}, bf16[512,768]{1,0:T(8,128)(2,1)}) custom-call(bf16[1024,768]{1,0:T(8,128)(2,1)} %pad_maximum_fusion.x_ref, bf16[3,1024,768]{2,1,0:T(8,128)(2,1)} %get-tuple-element.206.dqkv_ref, bf16[768,2304]{1,0:T(8,128)(2,1)} %w_ref.5, f32[512,768]{1,0:T(8,128)} %get-tuple-element.207.dx1_ref, ...), custom_call_target="tpu_custom_call" | custom-call | flops 80000000 | tf_op jit(solution)/shard_map/qkv_back/pallas_call | solution.py:1365
  365.1 13.0 %collective-permute-done.8 = bf16[384,768]{1,0:T(8,128)(2,1)S(1)} collective-permute-done((bf16[384,768]{1,0:T(8,128)(2,1)}, bf16[384,768]{1,0:T(8,128)(2,1)S(1)}, u32[]{:S(2)}, u32[]{:S(2)}) %collective-permute-start.8) | collective-permute-done | bytes 589856 | tf_op jit(solution)/shard_map/ppermute | solution.py:1462
  393.3 17.7 %collective-permute-done.17 = bf16[96,768]{1,0:T(8,128)(2,1)S(1)} collective-permute-done((bf16[96,768]{1,0:T(8,128)(2,1)S(1)}, bf16[96,768]{1,0:T(8,128)(2,1)S(1)}, u32[]{:S(2)}, u32[]{:S(2)}) %collective-permute-start.17) | collective-permute-done | bytes 147488 | tf_op jit(solution)/shard_map/ppermute | solution.py:1490
  411.9 18.3 %collective-permute-done.13 = bf16[24,3968]{1,0:T(8,128)(2,1)S(1)} collective-permute-done((bf16[24,3968]{1,0:T(8,128)(2,1)S(1)}, bf16[24,3968]{1,0:T(8,128)(2,1)S(1)}, u32[]{:S(2)}, u32[]{:S(2)}) %collective-permute-start.13) | collective-permute-done | bytes 190496 | tf_op jit(solution)/shard_map/ppermute | solution.py:1490
  431.8 4.2 collective-permute-done.15
  448.7 7.5 %collective-permute-done.11 = bf16[48,4224]{1,0:T(8,128)(2,1)S(1)} collective-permute-done((bf16[48,4224]{1,0:T(8,128)(2,1)}, bf16[48,4224]{1,0:T(8,128)(2,1)S(1)}, u32[]{:S(2)}, u32[]{:S(2)}) %collective-permute-start.11) | collective-permute-done | bytes 405536 | tf_op jit(solution)/shard_map/ppermute | solution.py:1510
  457.8 11.1 %collective-permute-done.9 = bf16[512,768]{1,0:T(8,128)(2,1)S(1)} collective-permute-done((bf16[512,768]{1,0:T(8,128)(2,1)}, bf16[512,768]{1,0:T(8,128)(2,1)S(1)}, u32[]{:S(2)}, u32[]{:S(2)}) %collective-permute-start.9) | collective-permute-done | bytes 786464 | tf_op jit(solution)/shard_map/ppermute | solution.py:1684
  (209 shorter events, 107.8 us)
Async XLA Ops:
  7.2 259.2 %reduce-scatter.4.cloned.1.call-start = ((), (), s32[]{:S(2)}) async-start(), calls=%async_computation.3 | async-start | bytes 5013504 | tf_op jit(solution)/shard_map/reduce_scatter | solution.py:1611
  7.2 21.8 %collective-permute-start = (bf16[512,768]{1,0:T(8,128)(2,1)}, bf16[512,768]{1,0:T(8,128)(2,1)S(1)}, u32[]{:S(2)}, u32[]{:S(2)}) collective-permute-start(bf16[512,768]{1,0:T(8,128)(2,1)} %bitcast.133), channel_id=1, source_target_pairs={{0,1},{1,0},{2,3},{3,2},{4,5},{5,4},{6,7},{7,6},{8,9},{9,8},{10,11... | collective-permute-start | bytes 2359304 | tf_op jit(solution)/shard_map/ppermute | solution.py:1536
  97.3 7.5 %collective-permute-start.1 = (bf16[480,256]{1,0:T(8,128)(2,1)S(1)}, bf16[480,256]{1,0:T(8,128)(2,1)S(1)}, u32[]{:S(2)}, u32[]{:S(2)}) collective-permute-start(bf16[480,256]{1,0:T(8,128)(2,1)S(1)} %maximum_select_fusion), channel_id=1, source_target_pairs={{0,1},{1,0},{2,3},{3,2},{4,5},{5,4},{6,7},{7,6},{8,9},{9,8},{10,11... | collective-permute-start | bytes 737288 | tf_op jit(solution)/shard_map/ppermute | solution.py:1410
  171.5 266.2 %reduce-scatter.6.cloned.1.call-start = ((), (), s32[]{:S(2)}) async-start(), calls=%async_computation.4 | async-start | bytes 6893568 | tf_op jit(solution)/shard_map/reduce_scatter | solution.py:1652
  176.9 9.5 %collective-permute-start.2 = (bf16[480,256]{1,0:T(8,128)(2,1)S(1)}, bf16[480,256]{1,0:T(8,128)(2,1)S(1)}, u32[]{:S(2)}, u32[]{:S(2)}) collective-permute-start(bf16[480,256]{1,0:T(8,128)(2,1)S(1)} %maximum_select_fusion.1), channel_id=1, source_target_pairs={{0,1},{1,0},{2,3},{3,2},{4,5},{5,4},{6,7},{7,6},{8,9},{9,8},{10,11... | collective-permute-start | bytes 737288 | tf_op jit(solution)/shard_map/ppermute | solution.py:1410
  266.4 203.8 %reduce-scatter.8.cloned.1.call-start = ((), (), s32[]{:S(2)}) async-start(), calls=%async_computation.5 | async-start | bytes 4386816 | tf_op jit(solution)/shard_map/reduce_scatter | solution.py:1674
  291.2 17.9 %collective-permute-start.3 = (bf16[384,3968]{1,0:T(8,128)(2,1)}, bf16[384,3968]{1,0:T(8,128)(2,1)S(1)}, u32[]{:S(2)}, u32[]{:S(2)}) collective-permute-start(bf16[384,3968]{1,0:T(8,128)(2,1)} %get-tuple-element.187), channel_id=1, source_target_pairs={{0,2},{2,0},{4,6},{6,4},{8,10},{10,8},{12,14},{14,12},{16,18},{18,... | collective-permute-start | bytes 9142280 | tf_op jit(solution)/shard_map/ppermute | solution.py:1462
  291.3 17.8 %collective-permute-start.4 = (bf16[1536,768]{1,0:T(8,128)(2,1)}, bf16[1536,768]{1,0:T(8,128)(2,1)}, u32[]{:S(2)}, u32[]{:S(2)}) collective-permute-start(bf16[1536,768]{1,0:T(8,128)(2,1)} %get-tuple-element.188), channel_id=1, source_target_pairs={{0,2},{2,0},{4,6},{6,4},{8,10},{10,8},{12,14},{14,12},{16,18},{18,... | collective-permute-start | bytes 7077896 | tf_op jit(solution)/shard_map/ppermute | solution.py:1462
  317.1 40.4 %collective-permute-start.5 = (bf16[192,3968]{1,0:T(8,128)(2,1)}, bf16[192,3968]{1,0:T(8,128)(2,1)}, u32[]{:S(2)}, u32[]{:S(2)}) collective-permute-start(bf16[192,3968]{1,0:T(8,128)(2,1)} %bitcast.57), channel_id=1, source_target_pairs={{0,4},{2,6},{4,0},{6,2},{8,12},{10,14},{12,8},{14,10},{16,20},{18,... | collective-permute-start | bytes 4571144 | tf_op jit(solution)/shard_map/ppermute | solution.py:1462
  318.6 38.9 %collective-permute-start.6 = (bf16[768,768]{1,0:T(8,128)(2,1)}, bf16[768,768]{1,0:T(8,128)(2,1)}, u32[]{:S(2)}, u32[]{:S(2)}) collective-permute-start(bf16[768,768]{1,0:T(8,128)(2,1)} %bitcast.59), channel_id=1, source_target_pairs={{0,1},{1,0},{2,3},{3,2},{4,5},{5,4},{6,7},{7,6},{8,9},{9,8},{10,11... | collective-permute-start | bytes 3538952 | tf_op jit(solution)/shard_map/ppermute | solution.py:1462
  362.5 18.7 %collective-permute-start.7 = (bf16[96,3968]{1,0:T(8,128)(2,1)}, bf16[96,3968]{1,0:T(8,128)(2,1)S(1)}, u32[]{:S(2)}, u32[]{:S(2)}) collective-permute-start(bf16[96,3968]{1,0:T(8,128)(2,1)} %bitcast.67), channel_id=1, source_target_pairs={{0,1},{1,0},{2,3},{3,2},{4,5},{5,4},{6,7},{7,6},{8,9},{9,8},{10,11... | collective-permute-start | bytes 2285576 | tf_op jit(solution)/shard_map/ppermute | solution.py:1462
  363.7 14.4 %collective-permute-start.8 = (bf16[384,768]{1,0:T(8,128)(2,1)}, bf16[384,768]{1,0:T(8,128)(2,1)S(1)}, u32[]{:S(2)}, u32[]{:S(2)}) collective-permute-start(bf16[384,768]{1,0:T(8,128)(2,1)} %bitcast.69), channel_id=1, source_target_pairs={{0,4},{2,6},{4,0},{6,2},{8,12},{10,14},{12,8},{14,10},{16,20},{18,... | collective-permute-start | bytes 1769480 | tf_op jit(solution)/shard_map/ppermute | solution.py:1462
  381.3 8.7 %collective-permute-start.16 = (bf16[96,768]{1,0:T(8,128)(2,1)S(1)}, bf16[96,768]{1,0:T(8,128)(2,1)S(1)}, u32[]{:S(2)}, u32[]{:S(2)}) collective-permute-start(bf16[96,768]{1,0:T(8,128)(2,1)S(1)} %get-tuple-element.423), channel_id=1, source_target_pairs={{0,8},{2,10},{4,12},{6,14},{8,0},{10,2},{12,4},{14,6},{16,24},{18,... | collective-permute-start | bytes 442376 | tf_op jit(solution)/shard_map/ppermute | solution.py:1490
  382.8 10.5 %collective-permute-start.18 = (bf16[96,768]{1,0:T(8,128)(2,1)S(1)}, bf16[96,768]{1,0:T(8,128)(2,1)S(1)}, u32[]{:S(2)}, u32[]{:S(2)}) collective-permute-start(bf16[96,768]{1,0:T(8,128)(2,1)S(1)} %get-tuple-element.424), channel_id=1, source_target_pairs={{0,24},{2,26},{4,28},{6,30},{8,16},{10,18},{12,20},{14,22},{16,8},... | collective-permute-start | bytes 442376 | tf_op jit(solution)/shard_map/ppermute | solution.py:1490
  385.4 25.7 %collective-permute-start.17 = (bf16[96,768]{1,0:T(8,128)(2,1)S(1)}, bf16[96,768]{1,0:T(8,128)(2,1)S(1)}, u32[]{:S(2)}, u32[]{:S(2)}) collective-permute-start(bf16[96,768]{1,0:T(8,128)(2,1)S(1)} %get-tuple-element.425), channel_id=1, source_target_pairs={{0,16},{2,18},{4,20},{6,22},{8,24},{10,26},{12,28},{14,30},{16,0},... | collective-permute-start | bytes 442376 | tf_op jit(solution)/shard_map/ppermute | solution.py:1490
  385.6 26.3 %collective-permute-start.12 = (bf16[24,3968]{1,0:T(8,128)(2,1)S(1)}, bf16[24,3968]{1,0:T(8,128)(2,1)S(1)}, u32[]{:S(2)}, u32[]{:S(2)}) collective-permute-start(bf16[24,3968]{1,0:T(8,128)(2,1)S(1)} %get-tuple-element.420), channel_id=1, source_target_pairs={{0,8},{2,10},{4,12},{6,14},{8,0},{10,2},{12,4},{14,6},{16,24},{18,... | collective-permute-start | bytes 571400 | tf_op jit(solution)/shard_map/ppermute | solution.py:1490
  387.4 24.5 %collective-permute-start.14 = (bf16[24,3968]{1,0:T(8,128)(2,1)S(1)}, bf16[24,3968]{1,0:T(8,128)(2,1)S(1)}, u32[]{:S(2)}, u32[]{:S(2)}) collective-permute-start(bf16[24,3968]{1,0:T(8,128)(2,1)S(1)} %get-tuple-element.421), channel_id=1, source_target_pairs={{0,24},{2,26},{4,28},{6,30},{8,16},{10,18},{12,20},{14,22},{16,8},... | collective-permute-start | bytes 571400 | tf_op jit(solution)/shard_map/ppermute | solution.py:1490
  390.0 40.2 %collective-permute-start.13 = (bf16[24,3968]{1,0:T(8,128)(2,1)S(1)}, bf16[24,3968]{1,0:T(8,128)(2,1)S(1)}, u32[]{:S(2)}, u32[]{:S(2)}) collective-permute-start(bf16[24,3968]{1,0:T(8,128)(2,1)S(1)} %get-tuple-element.422), channel_id=1, source_target_pairs={{0,16},{2,18},{4,20},{6,22},{8,24},{10,26},{12,28},{14,30},{16,0},... | collective-permute-start | bytes 571400 | tf_op jit(solution)/shard_map/ppermute | solution.py:1490
  411.1 19.8 %collective-permute-start.19 = (bf16[96,768]{1,0:T(8,128)(2,1)S(1)}, bf16[96,768]{1,0:T(8,128)(2,1)S(1)}, u32[]{:S(2)}, u32[]{:S(2)}) collective-permute-start(bf16[96,768]{1,0:T(8,128)(2,1)S(1)} %fusion.25), channel_id=1, source_target_pairs={{0,1},{1,0},{2,3},{3,2},{4,5},{5,4},{6,7},{7,6},{8,9},{9,8},{10,11... | collective-permute-start | bytes 442376 | tf_op jit(solution)/shard_map/ppermute | solution.py:1495
  430.3 5.7 %collective-permute-start.15 = (bf16[24,3968]{1,0:T(8,128)(2,1)S(1)}, bf16[24,3968]{1,0:T(8,128)(2,1)S(1)}, u32[]{:S(2)}, u32[]{:S(2)}) collective-permute-start(bf16[24,3968]{1,0:T(8,128)(2,1)S(1)} %fusion.22), channel_id=1, source_target_pairs={{0,1},{1,0},{2,3},{3,2},{4,5},{5,4},{6,7},{7,6},{8,9},{9,8},{10,11... | collective-permute-start | bytes 571400 | tf_op jit(solution)/shard_map/ppermute | solution.py:1495
  437.6 9.9 %collective-permute-start.10 = (bf16[144,1024]{1,0:T(8,128)(2,1)S(1)}, bf16[144,1024]{1,0:T(8,128)(2,1)S(1)}, u32[]{:S(2)}, u32[]{:S(2)}) collective-permute-start(bf16[144,1024]{1,0:T(8,128)(2,1)S(1)} %copy-done.9), channel_id=1, source_target_pairs={{0,1},{1,0},{2,3},{3,2},{4,5},{5,4},{6,7},{7,6},{8,9},{9,8},{10,11... | collective-permute-start | bytes 884744 | tf_op jit(solution)/shard_map/ppermute | solution.py:1510
  438.2 18.1 %collective-permute-start.11 = (bf16[48,4224]{1,0:T(8,128)(2,1)}, bf16[48,4224]{1,0:T(8,128)(2,1)S(1)}, u32[]{:S(2)}, u32[]{:S(2)}) collective-permute-start(bf16[48,4224]{1,0:T(8,128)(2,1)} %reduce-scatter.6.cloned.1.call-done), channel_id=1, source_target_pairs={{0,1},{1,0},{2,3},{3,2},{4,5},{5,4},{6,7},{7,6},{8,9},{9,8},{10,11... | collective-permute-start | bytes 1216520 | tf_op jit(solution)/shard_map/ppermute | solution.py:1510
  444.3 24.6 %collective-permute-start.9 = (bf16[512,768]{1,0:T(8,128)(2,1)}, bf16[512,768]{1,0:T(8,128)(2,1)S(1)}, u32[]{:S(2)}, u32[]{:S(2)}) collective-permute-start(bf16[512,768]{1,0:T(8,128)(2,1)} %get-tuple-element.233), channel_id=1, source_target_pairs={{0,1},{1,0},{2,3},{3,2},{4,5},{5,4},{6,7},{7,6},{8,9},{9,8},{10,11... | collective-permute-start | bytes 2359304 | tf_op jit(solution)/shard_map/ppermute | solution.py:1684
  470.2 6.5 %collective-permute-start.20 = (bf16[48,2688]{1,0:T(8,128)(2,1)}, bf16[48,2688]{1,0:T(8,128)(2,1)S(1)}, u32[]{:S(2)}, u32[]{:S(2)}) collective-permute-start(bf16[48,2688]{1,0:T(8,128)(2,1)} %reduce-scatter.8.cloned.1.call-done), channel_id=1, source_target_pairs={{0,1},{1,0},{2,3},{3,2},{4,5},{5,4},{6,7},{7,6},{8,9},{9,8},{10,11... | collective-permute-start | bytes 774152 | tf_op jit(solution)/shard_map/ppermute | solution.py:1510
  (21 other events, 137.8 us)
Sparse Core Ops, SparseCore 0:
  171.6 75.8 reduce-scatter.3
  266.5 92.7 reduce-scatter.5
  365.2 84.0 reduce-scatter.7
